TPU v7x, 32 devices: a whole 2x2x4 slice. The times are simulated.
32 devices in a mesh: seq: 8 (over z, core), chan: 4 (over y, x).
Axes of the slice: x: 2, y: 2, z: 4, core: 2. Of those that a mesh axis runs over, the one named last changes fastest.
Arguments:
- arrived: bfloat16 [3, 4096, 8192], P(None, ('seq', 'chan')), may hold values from -6 to 6
- landing: int32 [8, 8], P('seq'), may hold values from 0 to 7, each once within a row
- resets: int32 [4096], P('seq'), may hold values 0 or 1
- short_taps: float32 [3, 7, 8192], P(None, None, 'chan'), may hold values from -3 to 3
- decay_rate: float32 [16, 8192], P(None, 'chan'), may hold values from 0 to 1, as said below
- residues: float32 [16, 8192], P(None, 'chan'), may hold values from -2 to 2
- skip_gain: float32 [8192], P('chan'), may hold values from 0.5 to 1.5
Outputs:
- mixed: bfloat16 [4096, 8192], P('seq', 'chan')
Inputs may be any that keep to these rules, and one draw needn't show every extreme that they name: Each row is a permutation: landing[r, s] is the place, among the blocks of shard r, of the block that comes from loader group s. `resets`: 1 marks the first token of a document. `decay_rate`: positive decay rates.
All inputs are finite; a program needn't handle non-finite values. No bound on the sum of `resets` on one device may be relied on, other than what follows from the above.
Results may differ from a plain program's by a relative error of at most 0.01.
Values may be sent and summed in bfloat16 or wider, within the bound.
No kernel may reach another device: no remote copies, remote signals or barrier semaphores. Data moves between devices by JAX's collectives and lax.ppermute only.
A program may use at most 128 MiB of HBM per device.

v0:
```python
import jax
import jax.numpy as jnp
from jax import lax
from jax.sharding import PartitionSpec as P


def passed_along(shard, axis, by):
    count = lax.axis_size(axis)
    pairs = [(i, i + by) for i in range(count) if 0 <= i + by < count]
    return lax.ppermute(shard, axis, pairs)


def short_filter(extended, tap_table, out_rows):
    tap_count = tap_table.shape[1]
    combined = jnp.zeros((extended.shape[0], out_rows, extended.shape[2]), jnp.float32)
    for tap_index in range(tap_count):
        offset_rows = tap_count - 1 - tap_index
        combined = (
            combined
            + tap_table[:, tap_index][:, None, :]
            * extended[:, offset_rows : offset_rows + out_rows, :]
        )
    return combined


def modal_local(gated_mix, resets, decay_rates, mode_gain):
    length, channels = gated_mix.shape
    modes = decay_rates.shape[0]
    block_len = 64
    blocks = length // block_len
    offsets = jnp.arange(block_len, dtype=jnp.float32)
    growth = jnp.exp(offsets[:, None, None] * decay_rates[None])
    shrink = jnp.exp(-offsets[:, None, None] * decay_rates[None])
    decay_step = jnp.exp(-decay_rates)
    doc_ids = jnp.cumsum(resets)
    row_ids = lax.broadcasted_iota(jnp.int32, (block_len, block_len), 0)
    col_ids = lax.broadcasted_iota(jnp.int32, (block_len, block_len), 1)

    def advance(carried_state, inputs):
        values, block_docs, reset_marks = inputs
        same_doc = ((block_docs[:, None] == block_docs[None, :]) & (col_ids <= row_ids)).astype(
            jnp.float32
        )
        lifted = (growth * values.astype(jnp.float32)[:, None, :]).reshape(
            block_len, modes * channels
        )
        summed = jnp.dot(same_doc, lifted, precision=lax.Precision.HIGHEST).reshape(
            block_len, modes, channels
        )
        untouched = (jnp.cumsum(reset_marks) == 0).astype(jnp.float32)
        inner_sum = summed + untouched[:, None, None] * (decay_step * carried_state)[None]
        states = shrink * inner_sum
        return (states[-1], jnp.sum(mode_gain[None] * states, axis=1))

    end_state, outputs = lax.scan(
        advance,
        jnp.zeros((modes, channels), jnp.float32),
        (
            gated_mix.reshape(blocks, block_len, channels),
            doc_ids.reshape(blocks, block_len),
            resets.reshape(blocks, block_len),
        ),
    )
    return (end_state, outputs.reshape(length, channels))


def modal_carry(entering, resets, decay_rates, mode_gain):
    length = resets.shape[0]
    channels = entering.shape[1]
    block_len = 64
    blocks = length // block_len
    untouched = (jnp.cumsum(resets) == 0).astype(jnp.float32).reshape(blocks, block_len)
    places = (jnp.arange(length, dtype=jnp.float32) + 1.0).reshape(blocks, block_len)
    weighted = mode_gain * entering

    def one_block(inputs):
        powers, keep_mask = inputs
        factor = jnp.exp(-powers[:, None, None] * decay_rates[None])
        return keep_mask[:, None] * jnp.sum(weighted[None] * factor, axis=1)

    result = lax.map(one_block, (places, untouched))
    return result.reshape(length, channels)


def on_device(arrived, landing, resets, short_taps, decay_rate, residues, skip_gain):
    shards = lax.axis_size("seq")
    regrouped = lax.all_to_all(
        lax.all_to_all(arrived, "chan", split_axis=2, concat_axis=1, tiled=True),
        "seq",
        split_axis=1,
        concat_axis=1,
        tiled=True,
    )
    kinds, length, channels = regrouped.shape
    slab_rows = length // shards
    slot_ids = lax.broadcasted_iota(jnp.int32, (shards, shards), 0)
    group_ids = lax.broadcasted_iota(jnp.int32, (shards, shards), 1)
    matches = (landing[0][None, :] == slot_ids).astype(jnp.int32)
    source = jnp.sum(matches * group_ids, axis=1)
    ordered = jnp.take(
        regrouped.reshape(kinds, shards, slab_rows, channels), source, axis=1
    ).reshape(kinds, length, channels)
    short_reach = short_taps.shape[1]
    border = passed_along(ordered[:, length - (short_reach - 1) :, :], "seq", 1)
    filtered = short_filter(jnp.concatenate([border, ordered], axis=1), short_taps, length)
    front_conv = filtered[0]
    gated_mix = (filtered[1] * filtered[2]).astype(jnp.bfloat16)
    mode_gain = residues * jnp.sqrt(-jnp.expm1(-2.0 * decay_rate))
    end_state, local_part = modal_local(gated_mix, resets, decay_rate, mode_gain)
    through = jnp.exp(-decay_rate * length) * (jnp.sum(resets) == 0).astype(jnp.float32)
    all_through, all_end = (
        lax.all_gather(through[None], "seq", axis=0, tiled=True),
        lax.all_gather(end_state[None], "seq", axis=0, tiled=True),
    )
    position = lax.axis_index("seq")

    def absorb(shard_idx, carried_state):
        updated = all_through[shard_idx] * carried_state + all_end[shard_idx]
        return jnp.where(shard_idx < position, updated, carried_state)

    entering = lax.fori_loop(0, all_end.shape[0], absorb, jnp.zeros_like(end_state))
    carried = modal_carry(entering, resets, decay_rate, mode_gain)
    combined = local_part + carried + skip_gain[None, :] * gated_mix.astype(jnp.float32)
    return (front_conv * combined).astype(jnp.bfloat16)


def solution(mesh):
    in_specs = (
        P(None, ("seq", "chan"), None),
        P("seq", None),
        P("seq"),
        P(None, None, "chan"),
        P(None, "chan"),
        P(None, "chan"),
        P("chan"),
    )
    out_specs = P("seq", "chan")
    return jax.shard_map(
        on_device, mesh=mesh, in_specs=in_specs, out_specs=out_specs, check_vma=False
    )
```

profile of v0, /device:TPU:16, one launch (start us, length us, event | category | flops | bytes accessed | tf_op | source)
XLA Modules:
  0.0 632.0 jit_solution(1205601314427497172)
XLA Ops:
  6.5 13.1 %copy.26 = bf16[3,128,8192]{1,0,2:T(4,128)(2,1)} copy(bf16[3,128,8192]{2,1,0:T(8,128)(2,1)} %param.13) | data formatting | bytes 12582912 | tf_op args[0]
  19.7 97.2 %all_to_all.23 = bf16[3,128,8192]{1,0,2:T(4,128)(2,1)S(1)} all-to-all(bf16[3,128,8192]{1,0,2:T(4,128)(2,1)} %copy.26), channel_id=1, replica_groups=mesh['seq'=8,'chan'=4] {'chan'}, dimensions={2} | all-to-all | bytes 12582912 | tf_op jit(solution)/shard_map/all_to_all | solution.py:88
  120.4 8.7 %copy.28 = bf16[3,4,128,2048]{3,2,1,0:T(8,128)(2,1)} copy(bf16[3,4,128,2048]{2,3,1,0:T(8,128)(2,1)} %bitcast.120) | data formatting | bytes 12582912 | tf_op jit(solution)/shard_map/all_to_all | solution.py:88
  129.1 11.4 %copy.29 = bf16[3,512,2048]{2,0,1:T(4,128)(2,1)} copy(bf16[3,512,2048]{2,1,0:T(8,128)(2,1)} %bitcast.121) | data formatting | bytes 12582912 | tf_op jit(solution)/shard_map/all_to_all | solution.py:88
  140.5 5.4 all-to-all-start.1
  149.7 185.2 %all-to-all-done.1 = bf16[3,512,2048]{2,0,1:T(4,128)(2,1)} async-done(((bf16[3,512,2048]{2,0,1:T(4,128)(2,1)}), bf16[3,512,2048]{2,0,1:T(4,128)(2,1)}, u32[]{:S(2)}, u32[]{:S(2)}) %all-to-all-start.1) | async-done | bytes 6291488 | tf_op jit(solution)/shard_map/all_to_all | solution.py:87
  334.9 10.6 %copy.30 = bf16[3,512,2048]{2,1,0:T(8,128)(2,1)} copy(bf16[3,512,2048]{2,0,1:T(4,128)(2,1)} %all-to-all-done.1) | data formatting | bytes 12582912 | tf_op jit(solution)/shard_map/all_to_all | solution.py:87
  345.5 6.4 %gather_fusion = bf16[8,3,64,2048]{3,2,1,0:T(8,128)(2,1)} fusion(bf16[3,8,64,2048]{3,2,1,0:T(8,128)(2,1)} %bitcast.118, s32[1024]{0:T(1024)S(1)} %pad_clamp_fusion), kind=kCustom, calls=%fused_computation | custom fusion | bytes 12582944 | tf_op jit(solution)/shard_map/jit(_take)/gather | solution.py:100
  362.3 11.4 %multiply_add_fusion = f32[3,512,2048]{2,1,0:T(8,128)S(1)} fusion(bf16[3,512,2048]{2,1,0:T(8,128)(2,1)S(1)} %bitcast_select_fusion, bf16[3,6,2048]{2,1,0:T(8,128)(2,1)S(1)} %collective-permute-done, f32[3,2048]{1,0:T(4,128)S(1)} %get-tuple-element.402, f32[3,2048]{1,0:T(4,128)S(1)} %get-tuple-element.403, f32[3,2048]{1,0:T(4,128)S(1)} %get-tuple-element.404, ...), kind=kLoop, calls=%fused_computation.40 | loop fusion | flops 119537664 | bytes 19120128 | tf_op jit(solution)/shard_map/add | solution.py:19
  373.8 4.5 copy-done
  381.4 170.4 %while.42 = (s32[]{:T(128)}, f32[16,2048]{1,0:T(8,128)S(1)}, f32[8,64,2048]{2,1,0:T(8,128)}, s32[8,64]{1,0:T(8,128)S(1)}, bf16[8,64,2048]{2,1,0:T(8,128)(2,1)S(1...) while((s32[]{:T(128)}, f32[16,2048]{1,0:T(8,128)S(1)}, ...), condition=%wide.region_6.7_spmd.clone.clone, body=%wide.region_3.6_spmd.clone.clone.sunk | while | flops 1627439232 | bytes 29495172 | solution.py:55
  381.5 4.3 exponential_multiply_fusion.4
  386.2 15.5 %multiply_reduce_fusion.5 = (f32[64,2048]{1,0:T(8,128)S(1)}, f32[64,16,2048]{2,0,1:T(8,128)S(1)}) fusion(f32[16,2048]{1,0:T(8,128)S(1)} %get-tuple-element.576, f32[16,2048]{1,0:T(8,128)S(1)} %mul.421, f32[64]{0:T(128)S(1)} %convert_reduce_fusion.2, s32[64]{0:T(128)S(1)} %fusion.44, f32[16,2048]{1,0:T(8,128)S(1)} %get-tuple-element.577, ...), kind=kOutput, calls=%fused_computation.20.clone.1 | convolution fusion | flops 1623076864 | bytes 17695488 | tf_op jit(solution)/shard_map/while/body/eval_jaxpr/dot_general | solution.py:47
  407.5 15.5 %multiply_reduce_fusion.5 = (f32[64,2048]{1,0:T(8,128)S(1)}, f32[64,16,2048]{2,0,1:T(8,128)S(1)}) fusion(f32[16,2048]{1,0:T(8,128)S(1)} %get-tuple-element.576, f32[16,2048]{1,0:T(8,128)S(1)} %mul.421, f32[64]{0:T(128)S(1)} %convert_reduce_fusion.2, s32[64]{0:T(128)S(1)} %fusion.44, f32[16,2048]{1,0:T(8,128)S(1)} %get-tuple-element.577, ...), kind=kOutput, calls=%fused_computation.20.clone.1 | convolution fusion | flops 1623076864 | bytes 17695488 | tf_op jit(solution)/shard_map/while/body/eval_jaxpr/dot_general | solution.py:47
  428.8 15.5 %multiply_reduce_fusion.5 = (f32[64,2048]{1,0:T(8,128)S(1)}, f32[64,16,2048]{2,0,1:T(8,128)S(1)}) fusion(f32[16,2048]{1,0:T(8,128)S(1)} %get-tuple-element.576, f32[16,2048]{1,0:T(8,128)S(1)} %mul.421, f32[64]{0:T(128)S(1)} %convert_reduce_fusion.2, s32[64]{0:T(128)S(1)} %fusion.44, f32[16,2048]{1,0:T(8,128)S(1)} %get-tuple-element.577, ...), kind=kOutput, calls=%fused_computation.20.clone.1 | convolution fusion | flops 1623076864 | bytes 17695488 | tf_op jit(solution)/shard_map/while/body/eval_jaxpr/dot_general | solution.py:47
  450.1 15.5 %multiply_reduce_fusion.5 = (f32[64,2048]{1,0:T(8,128)S(1)}, f32[64,16,2048]{2,0,1:T(8,128)S(1)}) fusion(f32[16,2048]{1,0:T(8,128)S(1)} %get-tuple-element.576, f32[16,2048]{1,0:T(8,128)S(1)} %mul.421, f32[64]{0:T(128)S(1)} %convert_reduce_fusion.2, s32[64]{0:T(128)S(1)} %fusion.44, f32[16,2048]{1,0:T(8,128)S(1)} %get-tuple-element.577, ...), kind=kOutput, calls=%fused_computation.20.clone.1 | convolution fusion | flops 1623076864 | bytes 17695488 | tf_op jit(solution)/shard_map/while/body/eval_jaxpr/dot_general | solution.py:47
  471.4 15.5 %multiply_reduce_fusion.5 = (f32[64,2048]{1,0:T(8,128)S(1)}, f32[64,16,2048]{2,0,1:T(8,128)S(1)}) fusion(f32[16,2048]{1,0:T(8,128)S(1)} %get-tuple-element.576, f32[16,2048]{1,0:T(8,128)S(1)} %mul.421, f32[64]{0:T(128)S(1)} %convert_reduce_fusion.2, s32[64]{0:T(128)S(1)} %fusion.44, f32[16,2048]{1,0:T(8,128)S(1)} %get-tuple-element.577, ...), kind=kOutput, calls=%fused_computation.20.clone.1 | convolution fusion | flops 1623076864 | bytes 17695488 | tf_op jit(solution)/shard_map/while/body/eval_jaxpr/dot_general | solution.py:47
  492.7 15.5 %multiply_reduce_fusion.5 = (f32[64,2048]{1,0:T(8,128)S(1)}, f32[64,16,2048]{2,0,1:T(8,128)S(1)}) fusion(f32[16,2048]{1,0:T(8,128)S(1)} %get-tuple-element.576, f32[16,2048]{1,0:T(8,128)S(1)} %mul.421, f32[64]{0:T(128)S(1)} %convert_reduce_fusion.2, s32[64]{0:T(128)S(1)} %fusion.44, f32[16,2048]{1,0:T(8,128)S(1)} %get-tuple-element.577, ...), kind=kOutput, calls=%fused_computation.20.clone.1 | convolution fusion | flops 1623076864 | bytes 17695488 | tf_op jit(solution)/shard_map/while/body/eval_jaxpr/dot_general | solution.py:47
  514.0 15.5 %multiply_reduce_fusion.5 = (f32[64,2048]{1,0:T(8,128)S(1)}, f32[64,16,2048]{2,0,1:T(8,128)S(1)}) fusion(f32[16,2048]{1,0:T(8,128)S(1)} %get-tuple-element.576, f32[16,2048]{1,0:T(8,128)S(1)} %mul.421, f32[64]{0:T(128)S(1)} %convert_reduce_fusion.2, s32[64]{0:T(128)S(1)} %fusion.44, f32[16,2048]{1,0:T(8,128)S(1)} %get-tuple-element.577, ...), kind=kOutput, calls=%fused_computation.20.clone.1 | convolution fusion | flops 1623076864 | bytes 17695488 | tf_op jit(solution)/shard_map/while/body/eval_jaxpr/dot_general | solution.py:47
  535.3 15.5 %multiply_reduce_fusion.5 = (f32[64,2048]{1,0:T(8,128)S(1)}, f32[64,16,2048]{2,0,1:T(8,128)S(1)}) fusion(f32[16,2048]{1,0:T(8,128)S(1)} %get-tuple-element.576, f32[16,2048]{1,0:T(8,128)S(1)} %mul.421, f32[64]{0:T(128)S(1)} %convert_reduce_fusion.2, s32[64]{0:T(128)S(1)} %fusion.44, f32[16,2048]{1,0:T(8,128)S(1)} %get-tuple-element.577, ...), kind=kOutput, calls=%fused_computation.20.clone.1 | convolution fusion | flops 1623076864 | bytes 17695488 | tf_op jit(solution)/shard_map/while/body/eval_jaxpr/dot_general | solution.py:47
  552.6 22.0 %all-gather.7.cloned.1.call-done = f32[128,2048]{1,0:T(8,128)} async-done(((f32[16,2048]{1,0:T(8,128)}), f32[128,2048]{1,0:T(8,128)}) %all-gather.7.cloned.1.call-update) | async-done | bytes 1048592 | tf_op jit(solution)/shard_map/all_gather | solution.py:113
  574.6 8.7 %while.41 = (s32[]{:T(128)}, f32[16,2048]{1,0:T(8,128)S(1)}, s32[]{:T(128)}, f32[8,16,2048]{2,1,0:T(8,128)}, f32[8,16,2048]{2,1,0:T(8,128)}, /*index=5*/s32[]{:T(128)}, s32[]{:T(128)}) while((s32[]{:T(128)}, f32[16,2048]{1,0:T(8,128)S(1)}, s32[]{:T(128)}, f32[8,16,2048]{2,1,0:T(8,128)}, f32[8,16,2048]{2,1,0:T(8,128)}, ...), condition=%wide.region_9.10_spmd.clone, body=%wide.region_8.9_spmd.clone.sunk | while | flops 131076 | bytes 524389 | solution.py:121
  585.8 27.5 %while.40 = (s32[]{:T(128)}, f32[8,64,2048]{2,1,0:T(8,128)}, f32[8,64]{1,0:T(8,128)S(1)}, f32[16,2048]{1,0:T(8,128)S(1)}, f32[8,64]{1,0:T(8,128)S(1)}, /*index=5*/f32[16,2048]{1,0:T(8,128)S(1)}, s32[]{:T(128)}) while((s32[]{:T(128)}, f32[8,64,2048]{2,1,0:T(8,128)}, f32[8,64]{1,0:T(8,128)S(1)}, f32[16,2048]{1,0:T(8,128)S(1)}, ...), condition=%wide.region_12.13_spmd, body=%wide.region_10.12_spmd.sunk | while | flops 6291522 | bytes 1837137 | solution.py:81
  617.6 7.6 %fusion.31 = bf16[512,2048]{1,0:T(8,128)(2,1)} fusion(f32[3,512,2048]{2,1,0:T(8,128)} %copy-done, f32[8,64,2048]{2,1,0:T(8,128)S(1)} %add.102, f32[2048]{0:T(1024)S(1)} %copy-done.6), kind=kLoop, calls=%fused_computation.55 | loop fusion | flops 7340032 | bytes 18882560 | tf_op jit(solution)/shard_map/convert_element_type | solution.py:124
  (176 shorter events, 105.0 us)
Async XLA Ops:
  140.5 5.4 copy-start.5
  140.5 6.7 %copy-start.2 = (f32[16,2048]{1,0:T(8,128)S(1)}, f32[16,2048]{1,0:T(8,128)}, u32[]{:S(2)}) copy-start(f32[16,2048]{1,0:T(8,128)} %param.17) | copy-start | bytes 393220
  140.5 6.7 %copy-start.4 = (f32[16,2048]{1,0:T(8,128)S(1)}, f32[16,2048]{1,0:T(8,128)}, u32[]{:S(2)}) copy-start(f32[16,2048]{1,0:T(8,128)} %param.18) | copy-start | bytes 393220
  140.5 8.2 %copy-start.3 = (f32[3,7,2048]{2,1,0:T(8,128)S(1)}, f32[3,7,2048]{2,1,0:T(8,128)}, u32[]{:S(2)}) copy-start(f32[3,7,2048]{2,1,0:T(8,128)} %param.16) | copy-start | bytes 516100
  140.5 8.4 %copy-start.7 = (s32[1,8]{1,0:T(1,128)S(1)}, s32[1,8]{1,0:T(1,128)}, u32[]{:S(2)}) copy-start(s32[1,8]{1,0:T(1,128)} %param.14) | copy-start | bytes 100
  140.5 194.4 %all-to-all-start.1 = ((bf16[3,512,2048]{2,0,1:T(4,128)(2,1)}), bf16[3,512,2048]{2,0,1:T(4,128)(2,1)}, u32[]{:S(2)}, u32[]{:S(2)}) async-start(bf16[3,512,2048]{2,0,1:T(4,128)(2,1)} %copy.29), calls=%async_computation.1 | async-start | bytes 16777216 | tf_op jit(solution)/shard_map/all_to_all | solution.py:87
  145.9 406.7 %all-gather.5.cloned.1.call-start = ((), (), s32[]{:S(2)}) async-start(), calls=%async_computation.2 | async-start | bytes 1179648 | tf_op jit(solution)/shard_map/all_gather | solution.py:112
  148.0 426.7 %all-gather.7.cloned.1.call-start = ((), (), s32[]{:S(2)}) async-start(), calls=%async_computation.3 | async-start | bytes 1179648 | tf_op jit(solution)/shard_map/all_gather | solution.py:113
  356.4 5.9 collective-permute-start
  373.7 4.6 copy-start
  551.9 0.6 copy-start.1
  613.3 4.2 copy-start.6
Sparse Core Ops, SparseCore 0:
  148.3 38.4 all-gather.4
  552.6 21.9 all-gather.6
where the time goes:
time: 635 us; the launch traced here: 632 us
  waiting for transfers between devices  211 us (33%)
  matrix products  124 us (20%)
  other arithmetic  99.8 us (16%)
  blocking collectives  97.2 us (15%)
  local copies, waits for them, and re-layouts  77.2 us (12%)
  between operations  14.3 us (2%)
  starting transfers between devices  7.72 us (1%)
    all_to_all x1, waiting for transfers between devices, on_device(): lax.all_to_all(lax.all_to_all(arrived, 'chan', split_axis=2, concat_axis=...  185 us
    dot_general x8, matrix products, advance(): jnp.dot(same_doc, lifted, precision=lax.Precision.HIGHEST)  124 us
    all_to_all x1, blocking collectives, on_device(): lax.all_to_all(arrived, 'chan', split_axis=2, concat_axis=1, tiled=True)  97.2 us
    mul x8, other arithmetic, advance(): growth * values.astype(jnp.float32)[:, None, :]  34.8 us
    all_to_all x3, local copies, waits for them, and re-layouts, on_device(): lax.all_to_all(arrived, 'chan', split_axis=2, concat_axis=1, tiled=True)  23.6 us
    all_gather x1, waiting for transfers between devices, on_device(): lax.all_gather(end_state[None], 'seq', axis=0, tiled=True)  22 us
    reduce_sum x8, other arithmetic, one_block(): return keep_mask[:, None] * jnp.sum(weighted[None] * factor, axis=1)  20.1 us
    unnamed x21, local copies, waits for them, and re-layouts  18.4 us
  transfers between devices with their start and end apart: 4, of which 3 were waited for; matrix products, arithmetic and copies ran while one was open for 33% of the time, Pallas kernels for 0%

commit v1 on v0

v1 whole, which is shorter than its diff:
```python
import functools

import jax
import jax.numpy as jnp
from jax import lax
from jax.experimental import pallas as pl
from jax.experimental.pallas import tpu as pltpu
from jax.sharding import PartitionSpec as P

LANES = 128
SUBLANES = 8
GROUP = 8
CHUNKS = 4
VMEM_BYTES = 50 * 1024 * 1024

SMEM = pl.BlockSpec(memory_space=pltpu.SMEM)
VMEM = pl.BlockSpec(memory_space=pltpu.VMEM)
ANY = pl.BlockSpec(memory_space=pl.ANY)
PARAMS = pltpu.CompilerParams(vmem_limit_bytes=VMEM_BYTES)


def columns_of(table, chunk, width):
    lead = table.shape[:-1]
    return pl.BlockSpec((*lead, width), lambda g: (0,) * len(lead) + (chunk,))


def column_start(place_ref, d, chunk, width):
    return pl.multiple_of(((place_ref[0] ^ d) * CHUNKS + chunk) * width, LANES)


def cut_blocks(chunk, width, chans, place, arrived, later):

    def body(place_ref, arrived_ref, *refs):
        outs, sems = refs[len(later) : -1], refs[-1]
        copies = []
        for d, out in enumerate(outs, start=1):
            start = column_start(place_ref, d, chunk, width)
            copies.append(
                pltpu.make_async_copy(
                    arrived_ref.at[:, :, pl.ds(start, width)], out, sems.at[d - 1]
                )
            )
        for copy in copies:
            copy.start()
        for copy in copies:
            copy.wait()

    shape = jax.ShapeDtypeStruct((*arrived.shape[:2], width), arrived.dtype)
    return pl.pallas_call(
        body,
        in_specs=[SMEM, ANY] + [ANY] * len(later),
        out_specs=[VMEM] * (chans - 1),
        out_shape=[shape] * (chans - 1),
        scratch_shapes=[pltpu.SemaphoreType.DMA((chans - 1,))],
        compiler_params=PARAMS,
        name="cut_blocks",
    )(place, arrived, *later)


def shift_window(rows, start, count):
    return lax.slice_in_dim(rows, start, start + count, axis=0)


def cut_edges(place, arrived, per_device, reach, channels, chans):
    slab = arrived.shape[1] // per_device

    def body(place_ref, arrived_ref, *refs):
        outs, (tails, heads, sems) = refs[:chans], refs[chans:]
        copies = []
        for d in range(chans):
            start = pl.multiple_of((place_ref[0] ^ d) * channels, LANES)
            here = pl.ds(start, channels)
            for i in range(per_device):
                at = len(copies)
                copies.append(
                    pltpu.make_async_copy(
                        arrived_ref.at[:, pl.ds((i + 1) * slab - 16, 16), here],
                        tails.at[d, i],
                        sems.at[at],
                    )
                )
                copies.append(
                    pltpu.make_async_copy(
                        arrived_ref.at[2, pl.ds(i * slab, 16), here],
                        heads.at[d, i],
                        sems.at[at + 1],
                    )
                )
        for copy in copies:
            copy.start()
        for copy in copies:
            copy.wait()

        for d in range(chans):

            def one_block(block, carry, d=d):
                lanes = pl.ds(pl.multiple_of(block * LANES, LANES), LANES)
                for i in range(per_device):
                    parts = [
                        tails[d, i, k, :, lanes].astype(jnp.float32)[16 - reach :] for k in range(3)
                    ]
                    parts.append(heads[d, i, :, lanes].astype(jnp.float32)[:reach])
                    outs[d][i, :, lanes] = jnp.concatenate(parts, axis=0).astype(arrived.dtype)
                return carry

            lax.fori_loop(0, channels // LANES, one_block, 0)

    shape = jax.ShapeDtypeStruct((per_device, 4 * reach, channels), arrived.dtype)
    return pl.pallas_call(
        body,
        in_specs=[SMEM, ANY],
        out_specs=[VMEM] * chans,
        out_shape=[shape] * chans,
        scratch_shapes=[
            pltpu.VMEM((chans, per_device, 3, 16, channels), arrived.dtype),
            pltpu.VMEM((chans, per_device, 16, channels), arrived.dtype),
            pltpu.SemaphoreType.DMA((2 * chans * per_device,)),
        ],
        compiler_params=PARAMS,
        name="cut_edges",
    )(place, arrived)


def by_shard(place, parts, later):
    count = len(parts)
    per_device, rows, channels = parts[0].shape

    def body(place_ref, *refs):
        part_refs, (out_ref, sems) = refs[:count], refs[-2:]
        copies = [
            pltpu.make_async_copy(
                part_refs[d],
                out_ref.at[pl.ds((place_ref[0] ^ d) * per_device, per_device)],
                sems.at[d],
            )
            for d in range(count)
        ]
        for copy in copies:
            copy.start()
        for copy in copies:
            copy.wait()

    return pl.pallas_call(
        body,
        in_specs=[SMEM] + [ANY] * (count + len(later)),
        out_specs=VMEM,
        out_shape=jax.ShapeDtypeStruct((count * per_device, rows, channels), parts[0].dtype),
        scratch_shapes=[pltpu.SemaphoreType.DMA((count,))],
        compiler_params=PARAMS,
        name="by_shard",
    )(place, *parts, *later)


def front_body(chunk, count, place_ref, arrived_ref, *refs):
    block_refs = refs[: count - 1]
    taps_ref, out_ref, held, padded, sems = refs[-5:]
    shards, _, width = out_ref.shape
    per_device = shards // count
    slab = held.shape[2] // per_device
    taps = taps_ref.shape[1]
    reach = taps - 1
    blocks = width // LANES
    row_ids = lax.broadcasted_iota(jnp.int32, (slab, LANES), 0)
    sources = [arrived_ref.at[:, :, pl.ds(column_start(place_ref, 0, chunk, width), width)]]
    sources += block_refs
    copies = [pltpu.make_async_copy(sources[d], held.at[d], sems.at[d]) for d in range(count)]
    for copy in copies:
        copy.start()
    for k in range(3):
        padded[k, :8, :] = jnp.zeros((8, LANES), jnp.float32)
    for d in range(count):
        copies[d].wait()

        def one_block(step, carry, d=d):
            i, block = step // blocks, step % blocks
            lanes = pl.ds(pl.multiple_of(block * LANES, LANES), LANES)
            own = pl.ds(pl.multiple_of(i * slab, slab), slab)
            shard = (place_ref[0] ^ d) * per_device + i

            def conv(k):
                rows = held[d, k, own, lanes].astype(jnp.float32)
                padded[k, 8:, :] = rows
                total = taps_ref[k, 0:1, lanes] * rows
                for j in range(1, taps):
                    total = total + taps_ref[k, j : j + 1, lanes] * padded[k, 8 - j : 8 - j + slab, :]
                return total

            front = conv(0)
            key = conv(1)
            value = conv(2)
            gate = jnp.where(row_ids < reach, key, key * value)
            out_ref[shard, :slab, lanes] = front.astype(out_ref.dtype)
            out_ref[shard, slab:, lanes] = gate.astype(out_ref.dtype)
            return carry

        lax.fori_loop(0, per_device * blocks, one_block, 0)


def slab_fronts(chunk, width, place, arrived, blocks, taps, per_device, after):
    count = len(blocks) + 1
    rows = arrived.shape[1]
    shape = (count * per_device, 2 * (rows // per_device), width)
    return pl.pallas_call(
        functools.partial(front_body, chunk, count),
        grid=(1,),
        in_specs=[SMEM] + [ANY] * (count + len(after)) + [columns_of(taps, chunk, width)],
        out_specs=pl.BlockSpec(shape, lambda g: (0, 0, 0)),
        out_shape=jax.ShapeDtypeStruct(shape, arrived.dtype),
        scratch_shapes=[
            pltpu.VMEM((count, 3, rows, width), arrived.dtype),
            pltpu.VMEM((3, rows // per_device + 8, LANES), jnp.float32),
            pltpu.SemaphoreType.DMA((count,)),
        ],
        compiler_params=PARAMS,
        cost_estimate=pl.CostEstimate(
            flops=60 * count * rows * width,
            bytes_accessed=10 * count * rows * width,
            transcendentals=0,
        ),
        name="slab_fronts",
    )(place, arrived, *blocks, *after, taps)


def spread(values, blocks):
    if len(values) == 1:
        return values[0]
    ids = lax.broadcasted_iota(jnp.int32, (len(values) * blocks, LANES), 0)
    out = jnp.full(ids.shape, values[-1])
    for g in range(len(values) - 2, -1, -1):
        out = jnp.where(ids < (g + 1) * blocks, values[g], out)
    return out


def mode_rows(ref, table, n, sub):
    return ref[table, n * sub : (n + 1) * sub, :]


def scan_body(chunk, segments, shared, *refs):
    slots_ref, resets_ref, busy_ref, clear_ref, slab_ref, edge_ref, before_ref = refs[:7]
    taps_ref, decay_ref, gain_ref, skip_ref, across_ref = refs[7:12]
    earlier_refs = refs[12 : 12 + (shared > 0)]
    front_ref, local_ref, base_ref, ended_ref = refs[12 + shared : 16 + shared]
    slabs, edges, wide, by_mode, sems = refs[16 + shared :]
    count, rows, width = slabs.shape
    taps = taps_ref.shape[1]
    reach = taps - 1
    slab = rows // 2
    modes = decay_ref.shape[0]
    blocks = width // LANES
    sub = segments * blocks
    steps = count * slab // segments

    here = pl.ds(chunk * width, width)
    copies = [pltpu.make_async_copy(before_ref.at[:, here], edges.at[0], sems.at[2 * count])]
    for m in range(count):
        slot = slots_ref[m]
        copies.append(pltpu.make_async_copy(slab_ref.at[m], slabs.at[slot], sems.at[m]))
        copies.append(
            pltpu.make_async_copy(
                edge_ref.at[m, :, here], edges.at[slot + 1], sems.at[count + m]
            )
        )
    for copy in copies:
        copy.start()
    for g in range(segments):
        for j in range(blocks):
            lanes = slice(j * LANES, (j + 1) * LANES)
            at = g * blocks + j
            by_mode[0, pl.ds(at, modes, stride=sub), :] = decay_ref[:, lanes]
            by_mode[1, pl.ds(at, modes, stride=sub), :] = gain_ref[:, lanes]
            by_mode[2, at : at + 1, :] = skip_ref[:, lanes]
    for ref in earlier_refs:
        ended_ref[:, : chunk * width] = ref[:, : chunk * width]
    for copy in copies:
        copy.wait()

    row_ids = lax.broadcasted_iota(jnp.int32, (slab, LANES), 0)
    blank = jnp.zeros((16 - reach, LANES), jnp.float32)

    def one_slot(slot, carry):
        first = slot * slab
        g, t = first // steps, first % steps
        for j in range(blocks):
            lanes = slice(j * LANES, (j + 1) * LANES)
            edge = edges[slot, :, lanes].astype(jnp.float32)
            own = edges[slot + 1, :, lanes].astype(jnp.float32)

            def from_rows(k, rows, least):
                total = jnp.zeros((8, LANES), jnp.float32)
                for tap in range(least, taps):
                    total = total + taps_ref[k, tap : tap + 1, lanes] * shift_window(
                        rows, reach - tap, 8
                    )
                return total

            def tail(k):
                return edge[k * reach : (k + 1) * reach]

            add_front = from_rows(0, jnp.concatenate([tail(0), blank], axis=0), 1)
            add_key = from_rows(1, jnp.concatenate([tail(1), blank], axis=0), 1)
            value = from_rows(
                2, jnp.concatenate([tail(2), own[3 * reach :], blank[reach:]], axis=0), 0
            )
            starts = row_ids[:8] < reach
            front = slabs[slot, :slab, lanes].astype(jnp.float32)
            gate = slabs[slot, slab:, lanes].astype(jnp.float32)
            front_start = jnp.where(starts, front[:8] + add_front, front[:8])
            gate_start = ((gate[:8] + add_key) * value).astype(jnp.bfloat16)
            gate_start = jnp.where(starts, gate_start.astype(jnp.float32), gate[:8])
            front = jnp.concatenate([front_start, front[8:]], axis=0)
            gate = jnp.concatenate([gate_start, gate[8:]], axis=0)
            base = pl.multiple_of(first, slab)
            front_ref[pl.ds(base, slab), lanes] = front.astype(front_ref.dtype)
            wide[pl.ds(t * sub + (g * blocks + j), slab, stride=sub), :] = gate

        return carry

    lax.fori_loop(0, count, one_slot, 0)

    decay = [mode_rows(by_mode, 0, n, sub) for n in range(modes)]
    gain = [mode_rows(by_mode, 1, n, sub) for n in range(modes)]
    skip = by_mode[2, 0:sub, :]

    def tokens(step, states, with_resets):
        states = list(states)
        for u in range(GROUP):
            token = step * GROUP + u
            at = pl.ds(pl.multiple_of(token * sub, sub), sub)
            if with_resets:
                hold = spread(
                    [
                        jnp.where(resets_ref[g * steps + token] == 0, 1.0, 0.0)
                        for g in range(segments)
                    ],
                    blocks,
                )
                states = [state * hold for state in states]
            gate = wide[at, :]
            sums = [skip * gate, None]
            for n in range(modes):
                states[n] = states[n] * decay[n] + gate
                term = gain[n] * states[n]
                sums[n % 2] = term if sums[n % 2] is None else sums[n % 2] + term
            local_ref[at, :] = sums[0] + sums[1]
        return tuple(states)

    def some_tokens(step, states):
        return lax.cond(
            busy_ref[step] == 0,
            lambda held: tokens(step, held, False),
            lambda held: tokens(step, held, True),
            states,
        )

    zero = jnp.zeros((sub, LANES), jnp.float32)
    states = lax.fori_loop(0, steps // GROUP, some_tokens, (zero,) * modes)
    for n in range(modes):
        by_mode[0, n * sub : (n + 1) * sub, :] = states[n]
    open_shard = clear_ref[0]
    for g in range(1, segments):
        open_shard = open_shard * clear_ref[g]
    for j in range(blocks):
        lanes = slice(j * LANES, (j + 1) * LANES)
        entering = jnp.zeros((modes, LANES), jnp.float32)
        for g in range(segments):
            base_ref[g, :, lanes] = entering
            ended = by_mode[0, pl.ds(g * blocks + j, modes, stride=sub), :]
            entering = ended + across_ref[:, lanes] * clear_ref[g] * entering
        ended_ref[:, chunk * width + j * LANES : chunk * width + (j + 1) * LANES] = (
            entering.astype(ended_ref.dtype)
        )
    ended_ref[:, (chunk + 1) * width :] = jnp.full(
        (modes, LANES), open_shard, jnp.float32
    ).astype(ended_ref.dtype)


def whole_block(shape):
    return pl.BlockSpec(shape, lambda g: (0,) * len(shape))


def scan_shard(
    chunk, width, segments, slots, resets, busy, clear, slabs, edges, before, tables, earlier
):
    count, rows, _ = slabs.shape
    length = resets.shape[0]
    modes, channels = tables[1].shape
    blocks = width // LANES
    sub = segments * blocks
    outs = [
        jax.ShapeDtypeStruct((length, channels), jnp.bfloat16),
        jax.ShapeDtypeStruct((length * channels // LANES, LANES), jnp.float32),
        jax.ShapeDtypeStruct((segments, modes, channels), jnp.float32),
        jax.ShapeDtypeStruct((modes, (chunk + 1) * width + LANES), jnp.bfloat16),
    ]
    shared = [*earlier[3:], *earlier[:3]]
    first = 7 + len(tables) + 1
    return pl.pallas_call(
        functools.partial(scan_body, chunk, segments, len(shared)),
        grid=(1,),
        in_specs=[SMEM] * 4 + [ANY] * 3
        + [columns_of(table, chunk, width) for table in tables]
        + [whole_block(value.shape) for value in shared[:1]]
        + [ANY] * len(shared[1:]),
        out_specs=[
            columns_of(outs[0], chunk, width),
            pl.BlockSpec((length * blocks, LANES), lambda g: (chunk, 0)),
            columns_of(outs[2], chunk, width),
            whole_block(outs[3].shape),
        ],
        out_shape=outs,
        input_output_aliases={first + i: i for i in range(len(shared[1:]))},
        scratch_shapes=[
            pltpu.VMEM((count, rows, width), jnp.bfloat16),
            pltpu.VMEM((count + 1, edges.shape[1], width), jnp.bfloat16),
            pltpu.VMEM((length * blocks, LANES), jnp.float32),
            pltpu.VMEM((3, modes * sub, LANES), jnp.float32),
            pltpu.SemaphoreType.DMA((2 * count + 1,)),
        ],
        compiler_params=PARAMS,
        cost_estimate=pl.CostEstimate(
            flops=100 * length * width, bytes_accessed=10 * length * width, transcendentals=0
        ),
        name="scan_shard",
    )(slots, resets, busy, clear, slabs, edges, before, *tables, *shared)


def carry_body(segments, count, *refs):
    limit_ref, clear_ref = refs[:2]
    end_refs = refs[2 : 2 + count]
    through_ref, across_ref, decay_ref, gain_ref = refs[2 + count : 6 + count]
    base_ref, front_ref, local_ref = refs[6 + count : 9 + count]
    out_ref, by_mode, carried = refs[-3:]
    modes, width = decay_ref.shape
    length = front_ref.shape[0]
    blocks = width // LANES
    sub = segments * blocks
    steps = length // segments
    part = min(64, steps)
    for j in range(blocks):
        lanes = slice(j * LANES, (j + 1) * LANES)
        here = pl.ds(pl.multiple_of(pl.program_id(0) * width + j * LANES, LANES), LANES)
        entering = jnp.zeros((modes, LANES), jnp.float32)
        for ref in reversed(end_refs):
            is_open = ref[:, ref.shape[1] - LANES :].astype(jnp.float32)
            entering = ref[:, here].astype(jnp.float32) + (
                through_ref[:, lanes] * is_open * entering
            )
        for g in range(segments):
            at = pl.ds(g * blocks + j, modes, stride=sub)
            by_mode[0, at, :] = decay_ref[:, lanes]
            by_mode[1, at, :] = gain_ref[:, lanes] * (base_ref[g, :, lanes] + entering)
            entering = entering * across_ref[:, lanes] * clear_ref[g]
    decay = [mode_rows(by_mode, 0, n, sub) for n in range(modes)]
    limit = spread([jnp.full((sub, LANES), limit_ref[g]) for g in range(segments)], blocks)

    def some_tokens(step, states):
        states = list(states)
        for u in range(GROUP):
            token = step * GROUP + u
            at = pl.ds(pl.multiple_of(token * sub, sub), sub)
            sums = [None] * 4
            for n in range(modes):
                states[n] = states[n] * decay[n]
                sums[n % 4] = states[n] if sums[n % 4] is None else sums[n % 4] + states[n]
            added = (sums[0] + sums[1]) + (sums[2] + sums[3])
            carried[at, :] = local_ref[at, :] + jnp.where(token < limit, added, 0.0)
        return tuple(states)

    lax.fori_loop(
        0,
        steps // GROUP,
        some_tokens,
        tuple(mode_rows(by_mode, 1, n, sub) for n in range(modes)),
    )

    def finish(step, carry):
        first = step * part
        g, t = first // steps, first % steps
        rows = pl.ds(pl.multiple_of(first, part), part)
        for j in range(blocks):
            lanes = slice(j * LANES, (j + 1) * LANES)
            total = carried[pl.ds(t * sub + (g * blocks + j), part, stride=sub), :]
            out_ref[rows, lanes] = (front_ref[rows, lanes].astype(jnp.float32) * total).astype(
                out_ref.dtype
            )
        return carry

    lax.fori_loop(0, length // part, finish, 0)


def carry_shard(width, segments, limit, clear, ends, tables, base, front, local):
    length, channels = front.shape
    modes = tables[0].shape[0]
    blocks = width // LANES
    sub = segments * blocks
    specs = [SMEM, SMEM]
    specs += [whole_block(value.shape) for value in ends]
    specs += [pl.BlockSpec((modes, width), lambda g: (0, g)) for table in tables]
    specs.append(pl.BlockSpec((segments, modes, width), lambda g: (0, 0, g)))
    specs.append(pl.BlockSpec((length, width), lambda g: (0, g)))
    specs.append(pl.BlockSpec((length * blocks, LANES), lambda g: (g, 0)))
    return pl.pallas_call(
        functools.partial(carry_body, segments, len(ends)),
        grid=(channels // width,),
        in_specs=specs,
        out_specs=pl.BlockSpec((length, width), lambda g: (0, g)),
        out_shape=jax.ShapeDtypeStruct((length, channels), jnp.bfloat16),
        scratch_shapes=[
            pltpu.VMEM((2, modes * sub, LANES), jnp.float32),
            pltpu.VMEM((length * blocks, LANES), jnp.float32),
        ],
        compiler_params=PARAMS,
        cost_estimate=pl.CostEstimate(
            flops=40 * length * channels, bytes_accessed=8 * length * channels, transcendentals=0
        ),
        name="carry_shard",
    )(limit, clear, *ends, *tables, base, front, local)


def on_device(arrived, landing, resets, short_taps, decay_rate, residues, skip_gain):
    shards, chans = lax.axis_size("seq"), lax.axis_size("chan")
    chan = lax.axis_index("chan")
    per_device = shards // chans
    length = resets.shape[0]
    channels = short_taps.shape[2]
    reach = short_taps.shape[1] - 1
    width = channels // CHUNKS
    segments = max(1, SUBLANES * LANES // width)

    def passed_along(value, by):
        return lax.ppermute(value, "seq", [(i, i + by) for i in range(shards - by)])

    place = chan.astype(jnp.int32)[None]
    slots = landing[0]
    final = jnp.argmax(slots == shards - 1)
    marks = resets.reshape(segments, -1)
    steps = marks.shape[1]
    limit = jnp.min(
        jnp.where(marks != 0, lax.broadcasted_iota(jnp.int32, marks.shape, 1), steps), axis=1
    )
    clear = (limit == steps).astype(jnp.float32)
    busy = jnp.sum(marks.reshape(segments, -1, GROUP), axis=(0, 2))
    decay = jnp.exp(-decay_rate)
    through = jnp.exp(-decay_rate * length)
    across = jnp.exp(-decay_rate * steps)
    gain = residues * jnp.sqrt(-jnp.expm1(-2.0 * decay_rate))
    skip = skip_gain[None]

    def across_plane(parts):
        return [
            lax.ppermute(part, "chan", [(c, c ^ d) for c in range(chans)])
            for d, part in enumerate(parts, start=1)
        ]

    def along_column(value):
        return lax.all_to_all(value, "seq", split_axis=0, concat_axis=0, tiled=True)

    own, *parts = cut_edges(place, arrived, per_device, reach, channels, chans)
    parts = [own, *across_plane(parts)]
    cuts = [cut_blocks(0, width, chans, place, arrived, [own])]
    edges = along_column(by_shard(place, parts, cuts[0]))
    last = lax.dynamic_index_in_dim(edges, final, axis=0, keepdims=False)
    before = passed_along(last, 1)

    scanned, ended = [], []
    for chunk in range(CHUNKS):
        blocks = across_plane(cuts[chunk])
        ready = [before] if chunk == 0 else ended[chunk - 2 : chunk - 1]
        if 0 < chunk < CHUNKS - 1:
            cuts.append(cut_blocks(chunk + 1, width, chans, place, arrived, [sent]))
            ready = [*ready, cuts[-1][0]]
        sent = slab_fronts(
            chunk, width, place, arrived, blocks, short_taps, per_device, ready
        )
        if chunk == 0:
            cuts.append(cut_blocks(1, width, chans, place, arrived, [sent]))
        scanned = scan_shard(
            chunk,
            width,
            segments,
            slots,
            resets,
            busy,
            clear,
            along_column(sent),
            edges,
            before,
            (short_taps, decay, gain, skip, across),
            scanned,
        )
        ended.append(scanned[3])
    front, local, base, _ = scanned
    ends = [passed_along(ended[-1], d) for d in range(1, shards)]
    return carry_shard(
        width, segments, limit, clear, ends, (through, across, decay, gain), base, front, local
    )


def solution(mesh):
    in_specs = (
        P(None, ("seq", "chan"), None),
        P("seq", None),
        P("seq"),
        P(None, None, "chan"),
        P(None, "chan"),
        P(None, "chan"),
        P("chan"),
    )
    out_specs = P("seq", "chan")
    return jax.shard_map(
        on_device, mesh=mesh, in_specs=in_specs, out_specs=out_specs, check_vma=False
    )
```

time: 635 us -> 210 us (0.33)
  waiting for transfers between devices: 211 us -> 78.9 us
  matrix products: 124 us -> 0 us
  other arithmetic: 99.8 us -> 1.98 us
  blocking collectives: 97.2 us -> 0 us
  local copies, waits for them, and re-layouts: 77.2 us -> 4.65 us
  Pallas kernels: 0 us -> 61.3 us
  starting transfers between devices: 7.72 us -> 59.9 us
  between operations: 14.3 us -> 2.23 us
    all_to_all x1 -> x5, waiting for transfers between devices: 185 us -> 28.3 us  [along_column(): return lax.all_to_all(value, 'seq', split_axis=0, concat_axis=0, tiled=True)]
    dot_general x8 -> x0, matrix products: 124 us -> none  [advance(): jnp.dot(same_doc, lifted, precision=lax.Precision.HIGHEST)]
    all_to_all x1 -> x0, blocking collectives: 97.2 us -> none  [on_device(): lax.all_to_all(arrived, 'chan', split_axis=2, concat_axis=1, tiled=True)]
    pallas_call x0 -> x15, Pallas kernels: none -> 61.3 us  [the longest x4 27.4 us: scan_shard(): pl.pallas_call(functools.partial(scan_body, chunk, segments, len(shared))...]
    ppermute x1 -> x23, waiting for transfers between devices: 3.77 us -> 50.7 us  [the longest x15 41.2 us: across_plane(): lax.ppermute(part, 'chan', [(c, c ^ d) for c in range(chans)])]
    mul x18 -> x0, other arithmetic: 35.7 us -> none  [the longest x8 34.8 us: advance(): growth * values.astype(jnp.float32)[:, None, :]]
    all_to_all x4 -> x0, local copies, waits for them, and re-layouts: 34.2 us -> none  [the longest x3 23.6 us: on_device(): lax.all_to_all(arrived, 'chan', split_axis=2, concat_axis=1, tiled=True)]
    ppermute x1 -> x23, starting transfers between devices: 2.14 us -> 32.8 us  [the longest x15 17.6 us: across_plane(): lax.ppermute(part, 'chan', [(c, c ^ d) for c in range(chans)])]
  transfers between devices with their start and end apart: 4 -> 28, of which waited for: 3 -> 15; matrix products, arithmetic and copies ran while one was open for 33% -> 1% of each run, Pallas kernels for 0% -> 18%
where the time goes in v1:
time: 210 us; the launch traced here: 209 us
  waiting for transfers between devices  78.9 us (38%)
  Pallas kernels  61.3 us (29%)
  starting transfers between devices  59.9 us (29%)
  local copies, waits for them, and re-layouts  4.65 us (2%)
  between operations  2.23 us (1%)
    ppermute x15, waiting for transfers between devices, across_plane(): lax.ppermute(part, 'chan', [(c, c ^ d) for c in range(chans)])  41.2 us
    all_to_all x5, waiting for transfers between devices, along_column(): return lax.all_to_all(value, 'seq', split_axis=0, concat_axis=0, tiled=True)  28.3 us
    pallas_call x4, Pallas kernels, scan_shard(): pl.pallas_call(functools.partial(scan_body, chunk, segments, len(shared))...  27.4 us
    all_to_all x5, starting transfers between devices, along_column(): return lax.all_to_all(value, 'seq', split_axis=0, concat_axis=0, tiled=True)  27.1 us
    ppermute x15, starting transfers between devices, across_plane(): lax.ppermute(part, 'chan', [(c, c ^ d) for c in range(chans)])  17.6 us
    ppermute x8, starting transfers between devices, passed_along(): return lax.ppermute(value, 'seq', [(i, i + by) for i in range(shards - by)])  15.1 us
    pallas_call x4, Pallas kernels, slab_fronts(): pl.pallas_call(functools.partial(front_body, chunk, count), grid=(1,), in...  14.3 us
    ppermute x8, waiting for transfers between devices, passed_along(): return lax.ppermute(value, 'seq', [(i, i + by) for i in range(shards - by)])  9.42 us
  transfers between devices with their start and end apart: 28, of which 15 were waited for; matrix products, arithmetic and copies ran while one was open for 1% of the time, Pallas kernels for 18%

profile of v1, /device:TPU:16, one launch (start us, length us, event | category | flops | bytes accessed | tf_op | source)
XLA Modules:
  0.0 208.9 jit_solution(1670885119358798192)
XLA Ops:
  10.3 4.3 %collective-permute-done.4.refs_2_ = bf16[2,24,2048]{2,1,0:T(8,128)(2,1)S(1)} collective-permute-done((bf16[2,24,2048]{2,1,0:T(8,128)(2,1)S(1)}, bf16[2,24,2048]{2,1,0:T(8,128)(2,1)S(1)}, u32[]{:S(2)}, u32[]{:S(2)}) %collective-permute-start.4) | collective-permute-done | bytes 196640 | tf_op jit(solution)/shard_map/ppermute | solution.py:551
  16.5 5.2 %all-to-all-start = ((bf16[8,24,2048]{2,1,0:T(8,128)(2,1)}), bf16[8,24,2048]{2,1,0:T(8,128)(2,1)S(1)}, u32[]{:S(2)}, u32[]{:S(2)}) async-start(bf16[8,24,2048]{2,1,0:T(8,128)(2,1)} %by_shard.1), calls=%async_computation | async-start | bytes 1572864 | tf_op jit(solution)/shard_map/all_to_all | solution.py:556
  27.8 11.6 %all-to-all-done.refs_5_ = bf16[8,24,2048]{2,1,0:T(8,128)(2,1)S(1)} async-done(((bf16[8,24,2048]{2,1,0:T(8,128)(2,1)}), bf16[8,24,2048]{2,1,0:T(8,128)(2,1)S(1)}, u32[]{:S(2)}, u32[]{:S(2)}) %all-to-all-start) | async-done | bytes 786464 | tf_op jit(solution)/shard_map/all_to_all | solution.py:556
  42.3 3.1 %collective-permute-done.6.refs_3_.refs_6_ = bf16[24,2048]{1,0:T(8,128)(2,1)S(1)} collective-permute-done((bf16[24,2048]{1,0:T(8,128)(2,1)S(1)}, bf16[24,2048]{1,0:T(8,128)(2,1)S(1)}, u32[]{:S(2)}, u32[]{:S(2)}) %collective-permute-start.6) | collective-permute-done | bytes 98336 | tf_op jit(solution)/shard_map/ppermute | solution.py:531
  45.4 4.0 %slab_fronts.4.refs_0_ = bf16[8,128,512]{2,1,0:T(8,128)(2,1)} custom-call(s32[1]{0:T(128)} %bitcast.1.place_ref, bf16[3,128,8192]{2,1,0:T(8,128)(2,1)} %arrived_ref.17, bf16[3,128,512]{2,1,0:T(8,128)(2,1)S(1)} %collective-permute-done.refs_0_, bf16[3,128,512]{2,1,0:T(8,128)(2,1)S(1)} %collective-permute-done.1.refs_1_, ...), custom_call_target="tpu_custom_call" | custom-call | flops 15728640 | bytes 2621440 | tf_op jit(solution)/shard_map/slab_fronts/pallas_call | solution.py:203
  49.4 5.8 %all-to-all-start.2 = ((bf16[8,128,512]{2,1,0:T(8,128)(2,1)}), bf16[8,128,512]{2,1,0:T(8,128)(2,1)S(1)}, u32[]{:S(2)}, u32[]{:S(2)}) async-start(bf16[8,128,512]{2,1,0:T(8,128)(2,1)} %slab_fronts.4.refs_0_), calls=%async_computation.2 | async-start | bytes 2097152 | tf_op jit(solution)/shard_map/all_to_all | solution.py:556
  62.2 6.3 %collective-permute-done.7.refs_0_ = bf16[3,128,512]{2,1,0:T(8,128)(2,1)S(1)} collective-permute-done((bf16[3,128,512]{2,1,0:T(8,128)(2,1)S(1)}, bf16[3,128,512]{2,1,0:T(8,128)(2,1)S(1)}, u32[]{:S(2)}, u32[]{:S(2)}) %collective-permute-start.7) | collective-permute-done | bytes 393248 | tf_op jit(solution)/shard_map/ppermute | solution.py:551
  68.5 7.0 %collective-permute-done.8.refs_1_ = bf16[3,128,512]{2,1,0:T(8,128)(2,1)S(1)} collective-permute-done((bf16[3,128,512]{2,1,0:T(8,128)(2,1)S(1)}, bf16[3,128,512]{2,1,0:T(8,128)(2,1)S(1)}, u32[]{:S(2)}, u32[]{:S(2)}) %collective-permute-start.8) | collective-permute-done | bytes 393248 | tf_op jit(solution)/shard_map/ppermute | solution.py:551
  77.1 4.1 %slab_fronts.5.refs_0_ = bf16[8,128,512]{2,1,0:T(8,128)(2,1)} custom-call(s32[1]{0:T(128)} %bitcast.1.place_ref, bf16[3,128,8192]{2,1,0:T(8,128)(2,1)} %arrived_ref.17, bf16[3,128,512]{2,1,0:T(8,128)(2,1)S(1)} %collective-permute-done.7.refs_0_, bf16[3,128,512]{2,1,0:T(8,128)(2,1)S(1)} %collective-permute-done.8.refs_1_, ...), custom_call_target="tpu_custom_call" | custom-call | flops 15728640 | bytes 2621440 | tf_op jit(solution)/shard_map/slab_fronts/pallas_call | solution.py:203
  82.3 5.1 %all-to-all-start.1 = ((bf16[8,128,512]{2,1,0:T(8,128)(2,1)}), bf16[8,128,512]{2,1,0:T(8,128)(2,1)S(1)}, u32[]{:S(2)}, u32[]{:S(2)}) async-start(bf16[8,128,512]{2,1,0:T(8,128)(2,1)} %slab_fronts.5.refs_0_), calls=%async_computation.1 | async-start | bytes 2097152 | tf_op jit(solution)/shard_map/all_to_all | solution.py:556
  93.6 6.9 %scan_shard.4 = (bf16[512,2048]{1,0:T(8,128)(2,1)}, f32[8192,128]{1,0:T(8,128)}, f32[2,16,2048]{2,1,0:T(8,128)S(1)}, bf16[16,640]{1,0:T(8,128)(2,1)S(1)}) custom-call(s32[8]{0:T(128)S(1)} %bitcast.10, s32[512]{0:T(512)S(1)} %copy-done.8, s32[32]{0:T(128)S(1)} %reduce_sum.9.refs_2_, f32[2]{0:T(128)S(1)} %compare_convert_fusion.refs_3_.refs_1_, ...), custom_call_target="tpu_custom_call" | custom-call | flops 26214400 | bytes 2621440 | tf_op jit(solution)/shard_map/scan_shard/pallas_call | solution.py:397
  100.6 7.6 %collective-permute-done.14.refs_1_ = bf16[3,128,512]{2,1,0:T(8,128)(2,1)S(1)} collective-permute-done((bf16[3,128,512]{2,1,0:T(8,128)(2,1)}, bf16[3,128,512]{2,1,0:T(8,128)(2,1)S(1)}, u32[]{:S(2)}, u32[]{:S(2)}) %collective-permute-start.14) | collective-permute-done | bytes 393248 | tf_op jit(solution)/shard_map/ppermute | solution.py:551
  108.2 3.1 %slab_fronts.7 = bf16[8,128,512]{2,1,0:T(8,128)(2,1)S(1)} custom-call(s32[1]{0:T(128)} %bitcast.1.place_ref, bf16[3,128,8192]{2,1,0:T(8,128)(2,1)} %arrived_ref.17, bf16[3,128,512]{2,1,0:T(8,128)(2,1)S(1)} %collective-permute-done.13.refs_0_, bf16[3,128,512]{2,1,0:T(8,128)(2,1)S(1)} %collective-permute-done.14.refs_1_, ...), custom_call_target="tpu_custom_call" | custom-call | flops 15728640 | bytes 2621440 | tf_op jit(solution)/shard_map/slab_fronts/pallas_call | solution.py:203
  112.3 5.8 %all-to-all-start.4 = ((bf16[8,128,512]{2,1,0:T(8,128)(2,1)}), bf16[8,128,512]{2,1,0:T(8,128)(2,1)}, u32[]{:S(2)}, u32[]{:S(2)}) async-start(bf16[8,128,512]{2,1,0:T(8,128)(2,1)} %copy-done.2), calls=%async_computation.4 | async-start | bytes 2097152 | tf_op jit(solution)/shard_map/all_to_all | solution.py:556
  121.6 6.9 %scan_shard.5 = (bf16[512,2048]{1,0:T(8,128)(2,1)}, f32[8192,128]{1,0:T(8,128)}, f32[2,16,2048]{2,1,0:T(8,128)S(1)}, bf16[16,1152]{1,0:T(8,128)(2,1)S(1)}) custom-call(s32[8]{0:T(128)S(1)} %bitcast.11, s32[512]{0:T(512)S(1)} %copy-done.8, s32[32]{0:T(128)S(1)} %reduce_sum.9.refs_2_, ...), custom_call_target="tpu_custom_call", output_to_operand_aliasing={{0}: (13, {}), {1}: (14, {}), {2}: (15, {})} | custom-call | flops 26214400 | bytes 2621440 | tf_op jit(solution)/shard_map/scan_shard/pallas_call | solution.py:397
  128.5 9.4 %collective-permute-done.11.refs_1_ = bf16[3,128,512]{2,1,0:T(8,128)(2,1)S(1)} collective-permute-done((bf16[3,128,512]{2,1,0:T(8,128)(2,1)}, bf16[3,128,512]{2,1,0:T(8,128)(2,1)S(1)}, u32[]{:S(2)}, u32[]{:S(2)}) %collective-permute-start.11) | collective-permute-done | bytes 393248 | tf_op jit(solution)/shard_map/ppermute | solution.py:551
  139.1 3.1 %slab_fronts.6 = bf16[8,128,512]{2,1,0:T(8,128)(2,1)S(1)} custom-call(s32[1]{0:T(128)} %bitcast.1.place_ref, bf16[3,128,8192]{2,1,0:T(8,128)(2,1)} %arrived_ref.17, bf16[3,128,512]{2,1,0:T(8,128)(2,1)S(1)} %collective-permute-done.10.refs_0_, bf16[3,128,512]{2,1,0:T(8,128)(2,1)S(1)} %collective-permute-done.11.refs_1_, ...), custom_call_target="tpu_custom_call" | custom-call | flops 15728640 | bytes 2621440 | tf_op jit(solution)/shard_map/slab_fronts/pallas_call | solution.py:203
  143.2 5.1 %all-to-all-start.3 = ((bf16[8,128,512]{2,1,0:T(8,128)(2,1)}), bf16[8,128,512]{2,1,0:T(8,128)(2,1)S(1)}, u32[]{:S(2)}, u32[]{:S(2)}) async-start(bf16[8,128,512]{2,1,0:T(8,128)(2,1)} %copy-done.5), calls=%async_computation.3 | async-start | bytes 2097152 | tf_op jit(solution)/shard_map/all_to_all | solution.py:556
  148.3 6.7 %scan_shard.6 = (bf16[512,2048]{1,0:T(8,128)(2,1)}, f32[8192,128]{1,0:T(8,128)}, f32[2,16,2048]{2,1,0:T(8,128)S(1)}, bf16[16,1664]{1,0:T(8,128)(2,1)S(1)}) custom-call(s32[8]{0:T(128)S(1)} %bitcast.12, s32[512]{0:T(512)S(1)} %copy-done.8, s32[32]{0:T(128)S(1)} %reduce_sum.9.refs_2_, ...), custom_call_target="tpu_custom_call", output_to_operand_aliasing={{0}: (13, {}), {1}: (14, {}), {2}: (15, {})} | custom-call | flops 26214400 | bytes 2621440 | tf_op jit(solution)/shard_map/scan_shard/pallas_call | solution.py:397
  155.0 16.6 %all-to-all-done.3.refs_4_ = bf16[8,128,512]{2,1,0:T(8,128)(2,1)S(1)} async-done(((bf16[8,128,512]{2,1,0:T(8,128)(2,1)}), bf16[8,128,512]{2,1,0:T(8,128)(2,1)S(1)}, u32[]{:S(2)}, u32[]{:S(2)}) %all-to-all-start.3) | async-done | bytes 1048608 | tf_op jit(solution)/shard_map/all_to_all | solution.py:556
  171.6 6.9 %scan_shard.7 = (bf16[512,2048]{1,0:T(8,128)(2,1)}, f32[8192,128]{1,0:T(8,128)}, f32[2,16,2048]{2,1,0:T(8,128)S(1)}, bf16[16,2176]{1,0:T(8,128)(2,1)S(1)}) custom-call(s32[8]{0:T(128)S(1)} %bitcast.13, s32[512]{0:T(512)S(1)} %copy-done.8, s32[32]{0:T(128)S(1)} %reduce_sum.9.refs_2_, ...), custom_call_target="tpu_custom_call", output_to_operand_aliasing={{0}: (13, {}), {1}: (14, {}), {2}: (15, {})} | custom-call | flops 26214400 | bytes 2621440 | tf_op jit(solution)/shard_map/scan_shard/pallas_call | solution.py:397
  181.9 5.7 %collective-permute-start.18 = (bf16[16,2176]{1,0:T(8,128)(2,1)S(1)}, bf16[16,2176]{1,0:T(8,128)(2,1)S(1)}, u32[]{:S(2)}, u32[]{:S(2)}) collective-permute-start(bf16[16,2176]{1,0:T(8,128)(2,1)S(1)} %get-tuple-element.67), channel_id=1, source_target_pairs={{0,12},{4,16},{8,20},{12,24},{16,28},{1,13},{5,17},{9,21},{13,25},... | collective-permute-start | bytes 208904 | tf_op jit(solution)/shard_map/ppermute | solution.py:531
  192.3 5.8 %collective-permute-done.17.refs_3_ = bf16[16,2176]{1,0:T(8,128)(2,1)S(1)} collective-permute-done((bf16[16,2176]{1,0:T(8,128)(2,1)S(1)}, bf16[16,2176]{1,0:T(8,128)(2,1)S(1)}, u32[]{:S(2)}, u32[]{:S(2)}) %collective-permute-start.17) | collective-permute-done | bytes 69664 | tf_op jit(solution)/shard_map/ppermute | solution.py:531
  199.8 9.1 %carry_shard.1 = bf16[512,2048]{1,0:T(8,128)(2,1)} custom-call(s32[2]{0:T(128)S(1)} %select_reduce_fusion.refs_0_, f32[2]{0:T(128)S(1)} %compare_convert_fusion.refs_3_.refs_1_, bf16[16,2176]{1,0:T(8,128)(2,1)S(1)} %collective-permute-done.16.refs_2_, bf16[16,2176]{1,0:T(8,128)(2,1)S(1)} %collective-permute-done.17.refs_3_, ...), custom_call_target="tpu_custom_call" | custom-call | flops 41943040 | bytes 8388608 | tf_op jit(solution)/shard_map/carry_shard/pallas_call | solution.py:502
  (82 shorter events, 51.3 us)
Async XLA Ops:
  4.0 10.6 %collective-permute-start.4 = (bf16[2,24,2048]{2,1,0:T(8,128)(2,1)S(1)}, bf16[2,24,2048]{2,1,0:T(8,128)(2,1)S(1)}, u32[]{:S(2)}, u32[]{:S(2)}) collective-permute-start(bf16[2,24,2048]{2,1,0:T(8,128)(2,1)S(1)} %get-tuple-element.43), channel_id=1, source_target_pairs={{0,2},{1,3},{2,0},{3,1},{4,6},{5,7},{6,4},{7,5},{8,10},{9,11},{10,... | collective-permute-start | bytes 589832 | tf_op jit(solution)/shard_map/ppermute | solution.py:551
  5.5 9.1 %collective-permute-start.5 = (bf16[2,24,2048]{2,1,0:T(8,128)(2,1)S(1)}, bf16[2,24,2048]{2,1,0:T(8,128)(2,1)S(1)}, u32[]{:S(2)}, u32[]{:S(2)}) collective-permute-start(bf16[2,24,2048]{2,1,0:T(8,128)(2,1)S(1)} %get-tuple-element.44), channel_id=1, source_target_pairs={{0,3},{1,2},{2,1},{3,0},{4,7},{5,6},{6,5},{7,4},{8,11},{9,10},{10,... | collective-permute-start | bytes 589832 | tf_op jit(solution)/shard_map/ppermute | solution.py:551
  16.5 22.9 %all-to-all-start = ((bf16[8,24,2048]{2,1,0:T(8,128)(2,1)}), bf16[8,24,2048]{2,1,0:T(8,128)(2,1)S(1)}, u32[]{:S(2)}, u32[]{:S(2)}) async-start(bf16[8,24,2048]{2,1,0:T(8,128)(2,1)} %by_shard.1), calls=%async_computation | async-start | bytes 1572864 | tf_op jit(solution)/shard_map/all_to_all | solution.py:556
  21.7 19.6 %collective-permute-start = (bf16[3,128,512]{2,1,0:T(8,128)(2,1)S(1)}, bf16[3,128,512]{2,1,0:T(8,128)(2,1)S(1)}, u32[]{:S(2)}, u32[]{:S(2)}) collective-permute-start(bf16[3,128,512]{2,1,0:T(8,128)(2,1)S(1)} %get-tuple-element.39.refs_4_), channel_id=1, source_target_pairs={{0,1},{1,0},{2,3},{3,2},{4,5},{5,4},{6,7},{7,6},{8,9},{9,8},{10,11... | collective-permute-start | bytes 1179656 | tf_op jit(solution)/shard_map/ppermute | solution.py:551
  22.9 18.4 %collective-permute-start.1 = (bf16[3,128,512]{2,1,0:T(8,128)(2,1)S(1)}, bf16[3,128,512]{2,1,0:T(8,128)(2,1)S(1)}, u32[]{:S(2)}, u32[]{:S(2)}) collective-permute-start(bf16[3,128,512]{2,1,0:T(8,128)(2,1)S(1)} %get-tuple-element.40.refs_5_), channel_id=1, source_target_pairs={{0,2},{1,3},{2,0},{3,1},{4,6},{5,7},{6,4},{7,5},{8,10},{9,11},{10,... | collective-permute-start | bytes 1179656 | tf_op jit(solution)/shard_map/ppermute | solution.py:551
  23.8 18.5 %collective-permute-start.2 = (bf16[3,128,512]{2,1,0:T(8,128)(2,1)S(1)}, bf16[3,128,512]{2,1,0:T(8,128)(2,1)S(1)}, u32[]{:S(2)}, u32[]{:S(2)}) collective-permute-start(bf16[3,128,512]{2,1,0:T(8,128)(2,1)S(1)} %get-tuple-element.41.refs_6_), channel_id=1, source_target_pairs={{0,3},{1,2},{2,1},{3,0},{4,7},{5,6},{6,5},{7,4},{8,11},{9,10},{10,... | collective-permute-start | bytes 1179656 | tf_op jit(solution)/shard_map/ppermute | solution.py:551
  49.4 31.9 %all-to-all-start.2 = ((bf16[8,128,512]{2,1,0:T(8,128)(2,1)}), bf16[8,128,512]{2,1,0:T(8,128)(2,1)S(1)}, u32[]{:S(2)}, u32[]{:S(2)}) async-start(bf16[8,128,512]{2,1,0:T(8,128)(2,1)} %slab_fronts.4.refs_0_), calls=%async_computation.2 | async-start | bytes 2097152 | tf_op jit(solution)/shard_map/all_to_all | solution.py:556
  56.5 12.0 %collective-permute-start.7 = (bf16[3,128,512]{2,1,0:T(8,128)(2,1)S(1)}, bf16[3,128,512]{2,1,0:T(8,128)(2,1)S(1)}, u32[]{:S(2)}, u32[]{:S(2)}) collective-permute-start(bf16[3,128,512]{2,1,0:T(8,128)(2,1)S(1)} %get-tuple-element.46), channel_id=1, source_target_pairs={{0,1},{1,0},{2,3},{3,2},{4,5},{5,4},{6,7},{7,6},{8,9},{9,8},{10,11... | collective-permute-start | bytes 1179656 | tf_op jit(solution)/shard_map/ppermute | solution.py:551
  57.8 17.7 %collective-permute-start.8 = (bf16[3,128,512]{2,1,0:T(8,128)(2,1)S(1)}, bf16[3,128,512]{2,1,0:T(8,128)(2,1)S(1)}, u32[]{:S(2)}, u32[]{:S(2)}) collective-permute-start(bf16[3,128,512]{2,1,0:T(8,128)(2,1)S(1)} %get-tuple-element.47), channel_id=1, source_target_pairs={{0,2},{1,3},{2,0},{3,1},{4,6},{5,7},{6,4},{7,5},{8,10},{9,11},{10,... | collective-permute-start | bytes 1179656 | tf_op jit(solution)/shard_map/ppermute | solution.py:551
  58.6 18.5 %collective-permute-start.9 = (bf16[3,128,512]{2,1,0:T(8,128)(2,1)S(1)}, bf16[3,128,512]{2,1,0:T(8,128)(2,1)S(1)}, u32[]{:S(2)}, u32[]{:S(2)}) collective-permute-start(bf16[3,128,512]{2,1,0:T(8,128)(2,1)S(1)} %get-tuple-element.48), channel_id=1, source_target_pairs={{0,3},{1,2},{2,1},{3,0},{4,7},{5,6},{6,5},{7,4},{8,11},{9,10},{10,... | collective-permute-start | bytes 1179656 | tf_op jit(solution)/shard_map/ppermute | solution.py:551
  82.3 30.0 %all-to-all-start.1 = ((bf16[8,128,512]{2,1,0:T(8,128)(2,1)}), bf16[8,128,512]{2,1,0:T(8,128)(2,1)S(1)}, u32[]{:S(2)}, u32[]{:S(2)}) async-start(bf16[8,128,512]{2,1,0:T(8,128)(2,1)} %slab_fronts.5.refs_0_), calls=%async_computation.1 | async-start | bytes 2097152 | tf_op jit(solution)/shard_map/all_to_all | solution.py:556
  87.7 20.4 %collective-permute-start.13 = (bf16[3,128,512]{2,1,0:T(8,128)(2,1)S(1)}, bf16[3,128,512]{2,1,0:T(8,128)(2,1)S(1)}, u32[]{:S(2)}, u32[]{:S(2)}) collective-permute-start(bf16[3,128,512]{2,1,0:T(8,128)(2,1)S(1)} %get-tuple-element.49.refs_3_), channel_id=1, source_target_pairs={{0,1},{1,0},{2,3},{3,2},{4,5},{5,4},{6,7},{7,6},{8,9},{9,8},{10,11... | collective-permute-start | bytes 1179656 | tf_op jit(solution)/shard_map/ppermute | solution.py:551
  88.6 19.5 %collective-permute-start.14 = (bf16[3,128,512]{2,1,0:T(8,128)(2,1)}, bf16[3,128,512]{2,1,0:T(8,128)(2,1)S(1)}, u32[]{:S(2)}, u32[]{:S(2)}) collective-permute-start(bf16[3,128,512]{2,1,0:T(8,128)(2,1)} %get-tuple-element.58), channel_id=1, source_target_pairs={{0,2},{1,3},{2,0},{3,1},{4,6},{5,7},{6,4},{7,5},{8,10},{9,11},{10,... | collective-permute-start | bytes 1179656 | tf_op jit(solution)/shard_map/ppermute | solution.py:551
  90.1 18.0 %collective-permute-start.15 = (bf16[3,128,512]{2,1,0:T(8,128)(2,1)}, bf16[3,128,512]{2,1,0:T(8,128)(2,1)S(1)}, u32[]{:S(2)}, u32[]{:S(2)}) collective-permute-start(bf16[3,128,512]{2,1,0:T(8,128)(2,1)} %get-tuple-element.59), channel_id=1, source_target_pairs={{0,3},{1,2},{2,1},{3,0},{4,7},{5,6},{6,5},{7,4},{8,11},{9,10},{10,... | collective-permute-start | bytes 1179656 | tf_op jit(solution)/shard_map/ppermute | solution.py:551
  112.3 30.9 %all-to-all-start.4 = ((bf16[8,128,512]{2,1,0:T(8,128)(2,1)}), bf16[8,128,512]{2,1,0:T(8,128)(2,1)}, u32[]{:S(2)}, u32[]{:S(2)}) async-start(bf16[8,128,512]{2,1,0:T(8,128)(2,1)} %copy-done.2), calls=%async_computation.4 | async-start | bytes 2097152 | tf_op jit(solution)/shard_map/all_to_all | solution.py:556
  118.1 19.8 %collective-permute-start.11 = (bf16[3,128,512]{2,1,0:T(8,128)(2,1)}, bf16[3,128,512]{2,1,0:T(8,128)(2,1)S(1)}, u32[]{:S(2)}, u32[]{:S(2)}) collective-permute-start(bf16[3,128,512]{2,1,0:T(8,128)(2,1)} %copy-done.11), channel_id=1, source_target_pairs={{0,2},{1,3},{2,0},{3,1},{4,6},{5,7},{6,4},{7,5},{8,10},{9,11},{10,... | collective-permute-start | bytes 1179656 | tf_op jit(solution)/shard_map/ppermute | solution.py:551
  118.9 19.0 %collective-permute-start.12 = (bf16[3,128,512]{2,1,0:T(8,128)(2,1)}, bf16[3,128,512]{2,1,0:T(8,128)(2,1)S(1)}, u32[]{:S(2)}, u32[]{:S(2)}) collective-permute-start(bf16[3,128,512]{2,1,0:T(8,128)(2,1)} %copy-done.10), channel_id=1, source_target_pairs={{0,3},{1,2},{2,1},{3,0},{4,7},{5,6},{6,5},{7,4},{8,11},{9,10},{10,... | collective-permute-start | bytes 1179656 | tf_op jit(solution)/shard_map/ppermute | solution.py:551
  120.4 18.8 %collective-permute-start.10 = (bf16[3,128,512]{2,1,0:T(8,128)(2,1)}, bf16[3,128,512]{2,1,0:T(8,128)(2,1)S(1)}, u32[]{:S(2)}, u32[]{:S(2)}) collective-permute-start(bf16[3,128,512]{2,1,0:T(8,128)(2,1)} %copy-done.6), channel_id=1, source_target_pairs={{0,1},{1,0},{2,3},{3,2},{4,5},{5,4},{6,7},{7,6},{8,9},{9,8},{10,11... | collective-permute-start | bytes 1179656 | tf_op jit(solution)/shard_map/ppermute | solution.py:551
  143.2 28.4 %all-to-all-start.3 = ((bf16[8,128,512]{2,1,0:T(8,128)(2,1)}), bf16[8,128,512]{2,1,0:T(8,128)(2,1)S(1)}, u32[]{:S(2)}, u32[]{:S(2)}) async-start(bf16[8,128,512]{2,1,0:T(8,128)(2,1)} %copy-done.5), calls=%async_computation.3 | async-start | bytes 2097152 | tf_op jit(solution)/shard_map/all_to_all | solution.py:556
  179.2 10.3 %collective-permute-start.21 = (bf16[16,2176]{1,0:T(8,128)(2,1)S(1)}, bf16[16,2176]{1,0:T(8,128)(2,1)S(1)}, u32[]{:S(2)}, u32[]{:S(2)}) collective-permute-start(bf16[16,2176]{1,0:T(8,128)(2,1)S(1)} %get-tuple-element.67), channel_id=1, source_target_pairs={{0,24},{4,28},{1,25},{5,29},{2,26},{6,30},{3,27},{7,31}} | collective-permute-start | bytes 208904 | tf_op jit(solution)/shard_map/ppermute | solution.py:531
  179.9 12.0 %collective-permute-start.20 = (bf16[16,2176]{1,0:T(8,128)(2,1)S(1)}, bf16[16,2176]{1,0:T(8,128)(2,1)S(1)}, u32[]{:S(2)}, u32[]{:S(2)}) collective-permute-start(bf16[16,2176]{1,0:T(8,128)(2,1)S(1)} %get-tuple-element.67), channel_id=1, source_target_pairs={{0,20},{4,24},{8,28},{1,21},{5,25},{9,29},{2,22},{6,26},{10,30},{3... | collective-permute-start | bytes 208904 | tf_op jit(solution)/shard_map/ppermute | solution.py:531
  180.6 11.3 %collective-permute-start.19 = (bf16[16,2176]{1,0:T(8,128)(2,1)S(1)}, bf16[16,2176]{1,0:T(8,128)(2,1)S(1)}, u32[]{:S(2)}, u32[]{:S(2)}) collective-permute-start(bf16[16,2176]{1,0:T(8,128)(2,1)S(1)} %get-tuple-element.67), channel_id=1, source_target_pairs={{0,16},{4,20},{8,24},{12,28},{1,17},{5,21},{9,25},{13,29},{2,18},{... | collective-permute-start | bytes 208904 | tf_op jit(solution)/shard_map/ppermute | solution.py:531
  181.9 10.4 %collective-permute-start.18 = (bf16[16,2176]{1,0:T(8,128)(2,1)S(1)}, bf16[16,2176]{1,0:T(8,128)(2,1)S(1)}, u32[]{:S(2)}, u32[]{:S(2)}) collective-permute-start(bf16[16,2176]{1,0:T(8,128)(2,1)S(1)} %get-tuple-element.67), channel_id=1, source_target_pairs={{0,12},{4,16},{8,20},{12,24},{16,28},{1,13},{5,17},{9,21},{13,25},... | collective-permute-start | bytes 208904 | tf_op jit(solution)/shard_map/ppermute | solution.py:531
  187.5 10.6 %collective-permute-start.17 = (bf16[16,2176]{1,0:T(8,128)(2,1)S(1)}, bf16[16,2176]{1,0:T(8,128)(2,1)S(1)}, u32[]{:S(2)}, u32[]{:S(2)}) collective-permute-start(bf16[16,2176]{1,0:T(8,128)(2,1)S(1)} %get-tuple-element.67), channel_id=1, source_target_pairs={{0,8},{4,12},{8,16},{12,20},{16,24},{20,28},{1,9},{5,13},{9,17},{1... | collective-permute-start | bytes 208904 | tf_op jit(solution)/shard_map/ppermute | solution.py:531
  (17 other events, 174.9 us)

commit v2 on v1

--- a/solution.py
+++ b/solution.py
@@ -9,7 +9,7 @@
 
 LANES = 128
 SUBLANES = 8
-GROUP = 8
+GROUP = 16
 CHUNKS = 4
 VMEM_BYTES = 50 * 1024 * 1024
 
@@ -509,7 +509,7 @@
             pltpu.VMEM((2, modes * sub, LANES), jnp.float32),
             pltpu.VMEM((length * blocks, LANES), jnp.float32),
         ],
-        compiler_params=PARAMS,
+        compiler_params=pltpu.CompilerParams(vmem_limit_bytes=52 * 1024 * 1024),
         cost_estimate=pl.CostEstimate(
             flops=40 * length * channels, bytes_accessed=8 * length * channels, transcendentals=0
         ),

time: 210 us -> 208 us (level)
    unnamed x26 -> x24, local copies, waits for them, and re-layouts: 4.55 us -> 3.02 us
  transfers between devices with their start and end apart: 28 -> 28, of which waited for: 15 -> 15; matrix products, arithmetic and copies ran while one was open for 1% -> 1% of each run, Pallas kernels for 18% -> 17%
where the time goes in v2:
time: 208 us; the launch traced here: 207 us
  waiting for transfers between devices  79.6 us (38%)
  Pallas kernels  60.1 us (29%)
  starting transfers between devices  59.8 us (29%)
  local copies, waits for them, and re-layouts  3.13 us (2%)
  between operations  2.22 us (1%)
    ppermute x15, waiting for transfers between devices, across_plane(): lax.ppermute(part, 'chan', [(c, c ^ d) for c in range(chans)])  41.7 us
    all_to_all x5, waiting for transfers between devices, along_column(): return lax.all_to_all(value, 'seq', split_axis=0, concat_axis=0, tiled=True)  28.5 us
    all_to_all x5, starting transfers between devices, along_column(): return lax.all_to_all(value, 'seq', split_axis=0, concat_axis=0, tiled=True)  27.1 us
    pallas_call x4, Pallas kernels, scan_shard(): pl.pallas_call(functools.partial(scan_body, chunk, segments, len(shared))...  26.5 us
    ppermute x15, starting transfers between devices, across_plane(): lax.ppermute(part, 'chan', [(c, c ^ d) for c in range(chans)])  17.6 us
    ppermute x8, starting transfers between devices, passed_along(): return lax.ppermute(value, 'seq', [(i, i + by) for i in range(shards - by)])  15.2 us
    pallas_call x4, Pallas kernels, slab_fronts(): pl.pallas_call(functools.partial(front_body, chunk, count), grid=(1,), in...  14.3 us
    ppermute x8, waiting for transfers between devices, passed_along(): return lax.ppermute(value, 'seq', [(i, i + by) for i in range(shards - by)])  9.42 us
  transfers between devices with their start and end apart: 28, of which 15 were waited for; matrix products, arithmetic and copies ran while one was open for 1% of the time, Pallas kernels for 17%

profile of v2, /device:TPU:16, one launch (start us, length us, event | category | flops | bytes accessed | tf_op | source)
XLA Modules:
  0.0 206.8 jit_solution(12387580150197533305)
XLA Ops:
  10.3 4.3 %collective-permute-done.4.refs_2_ = bf16[2,24,2048]{2,1,0:T(8,128)(2,1)S(1)} collective-permute-done((bf16[2,24,2048]{2,1,0:T(8,128)(2,1)S(1)}, bf16[2,24,2048]{2,1,0:T(8,128)(2,1)S(1)}, u32[]{:S(2)}, u32[]{:S(2)}) %collective-permute-start.4) | collective-permute-done | bytes 196640 | tf_op jit(solution)/shard_map/ppermute | solution.py:551
  16.5 5.2 %all-to-all-start = ((bf16[8,24,2048]{2,1,0:T(8,128)(2,1)}), bf16[8,24,2048]{2,1,0:T(8,128)(2,1)S(1)}, u32[]{:S(2)}, u32[]{:S(2)}) async-start(bf16[8,24,2048]{2,1,0:T(8,128)(2,1)} %by_shard.1), calls=%async_computation | async-start | bytes 1572864 | tf_op jit(solution)/shard_map/all_to_all | solution.py:556
  27.7 11.7 %all-to-all-done.refs_5_ = bf16[8,24,2048]{2,1,0:T(8,128)(2,1)S(1)} async-done(((bf16[8,24,2048]{2,1,0:T(8,128)(2,1)}), bf16[8,24,2048]{2,1,0:T(8,128)(2,1)S(1)}, u32[]{:S(2)}, u32[]{:S(2)}) %all-to-all-start) | async-done | bytes 786464 | tf_op jit(solution)/shard_map/all_to_all | solution.py:556
  42.3 3.1 %collective-permute-done.6.refs_3_.refs_6_ = bf16[24,2048]{1,0:T(8,128)(2,1)S(1)} collective-permute-done((bf16[24,2048]{1,0:T(8,128)(2,1)S(1)}, bf16[24,2048]{1,0:T(8,128)(2,1)S(1)}, u32[]{:S(2)}, u32[]{:S(2)}) %collective-permute-start.6) | collective-permute-done | bytes 98336 | tf_op jit(solution)/shard_map/ppermute | solution.py:531
  45.4 4.0 %slab_fronts.4.refs_0_ = bf16[8,128,512]{2,1,0:T(8,128)(2,1)} custom-call(s32[1]{0:T(128)} %bitcast.1.place_ref, bf16[3,128,8192]{2,1,0:T(8,128)(2,1)} %arrived_ref.17, bf16[3,128,512]{2,1,0:T(8,128)(2,1)S(1)} %collective-permute-done.refs_0_, bf16[3,128,512]{2,1,0:T(8,128)(2,1)S(1)} %collective-permute-done.1.refs_1_, ...), custom_call_target="tpu_custom_call" | custom-call | flops 15728640 | bytes 2621440 | tf_op jit(solution)/shard_map/slab_fronts/pallas_call | solution.py:203
  49.4 5.8 %all-to-all-start.2 = ((bf16[8,128,512]{2,1,0:T(8,128)(2,1)}), bf16[8,128,512]{2,1,0:T(8,128)(2,1)S(1)}, u32[]{:S(2)}, u32[]{:S(2)}) async-start(bf16[8,128,512]{2,1,0:T(8,128)(2,1)} %slab_fronts.4.refs_0_), calls=%async_computation.2 | async-start | bytes 2097152 | tf_op jit(solution)/shard_map/all_to_all | solution.py:556
  62.3 6.2 %collective-permute-done.7.refs_0_ = bf16[3,128,512]{2,1,0:T(8,128)(2,1)S(1)} collective-permute-done((bf16[3,128,512]{2,1,0:T(8,128)(2,1)S(1)}, bf16[3,128,512]{2,1,0:T(8,128)(2,1)S(1)}, u32[]{:S(2)}, u32[]{:S(2)}) %collective-permute-start.7) | collective-permute-done | bytes 393248 | tf_op jit(solution)/shard_map/ppermute | solution.py:551
  68.5 7.0 %collective-permute-done.8.refs_1_ = bf16[3,128,512]{2,1,0:T(8,128)(2,1)S(1)} collective-permute-done((bf16[3,128,512]{2,1,0:T(8,128)(2,1)S(1)}, bf16[3,128,512]{2,1,0:T(8,128)(2,1)S(1)}, u32[]{:S(2)}, u32[]{:S(2)}) %collective-permute-start.8) | collective-permute-done | bytes 393248 | tf_op jit(solution)/shard_map/ppermute | solution.py:551
  77.1 4.1 %slab_fronts.5.refs_0_ = bf16[8,128,512]{2,1,0:T(8,128)(2,1)} custom-call(s32[1]{0:T(128)} %bitcast.1.place_ref, bf16[3,128,8192]{2,1,0:T(8,128)(2,1)} %arrived_ref.17, bf16[3,128,512]{2,1,0:T(8,128)(2,1)S(1)} %collective-permute-done.7.refs_0_, bf16[3,128,512]{2,1,0:T(8,128)(2,1)S(1)} %collective-permute-done.8.refs_1_, ...), custom_call_target="tpu_custom_call" | custom-call | flops 15728640 | bytes 2621440 | tf_op jit(solution)/shard_map/slab_fronts/pallas_call | solution.py:203
  82.2 5.1 %all-to-all-start.1 = ((bf16[8,128,512]{2,1,0:T(8,128)(2,1)}), bf16[8,128,512]{2,1,0:T(8,128)(2,1)S(1)}, u32[]{:S(2)}, u32[]{:S(2)}) async-start(bf16[8,128,512]{2,1,0:T(8,128)(2,1)} %slab_fronts.5.refs_0_), calls=%async_computation.1 | async-start | bytes 2097152 | tf_op jit(solution)/shard_map/all_to_all | solution.py:556
  93.6 6.7 %scan_shard.4 = (bf16[512,2048]{1,0:T(8,128)(2,1)}, f32[8192,128]{1,0:T(8,128)}, f32[2,16,2048]{2,1,0:T(8,128)S(1)}, bf16[16,640]{1,0:T(8,128)(2,1)S(1)}) custom-call(s32[8]{0:T(128)S(1)} %bitcast.10, s32[512]{0:T(512)S(1)} %copy-done.7, s32[16]{0:T(128)S(1)} %reduce_sum.9.refs_2_, f32[2]{0:T(128)S(1)} %compare_convert_fusion.refs_3_.refs_1_, ...), custom_call_target="tpu_custom_call" | custom-call | flops 26214400 | bytes 2621440 | tf_op jit(solution)/shard_map/scan_shard/pallas_call | solution.py:397
  100.3 7.8 %collective-permute-done.14.refs_1_ = bf16[3,128,512]{2,1,0:T(8,128)(2,1)S(1)} collective-permute-done((bf16[3,128,512]{2,1,0:T(8,128)(2,1)}, bf16[3,128,512]{2,1,0:T(8,128)(2,1)S(1)}, u32[]{:S(2)}, u32[]{:S(2)}) %collective-permute-start.14) | collective-permute-done | bytes 393248 | tf_op jit(solution)/shard_map/ppermute | solution.py:551
  108.1 3.1 %slab_fronts.7 = bf16[8,128,512]{2,1,0:T(8,128)(2,1)S(1)} custom-call(s32[1]{0:T(128)} %bitcast.1.place_ref, bf16[3,128,8192]{2,1,0:T(8,128)(2,1)} %arrived_ref.17, bf16[3,128,512]{2,1,0:T(8,128)(2,1)S(1)} %collective-permute-done.13.refs_0_, bf16[3,128,512]{2,1,0:T(8,128)(2,1)S(1)} %collective-permute-done.14.refs_1_, ...), custom_call_target="tpu_custom_call" | custom-call | flops 15728640 | bytes 2621440 | tf_op jit(solution)/shard_map/slab_fronts/pallas_call | solution.py:203
  112.2 5.8 %all-to-all-start.4 = ((bf16[8,128,512]{2,1,0:T(8,128)(2,1)}), bf16[8,128,512]{2,1,0:T(8,128)(2,1)}, u32[]{:S(2)}, u32[]{:S(2)}) async-start(bf16[8,128,512]{2,1,0:T(8,128)(2,1)} %copy-done.1), calls=%async_computation.4 | async-start | bytes 2097152 | tf_op jit(solution)/shard_map/all_to_all | solution.py:556
  121.5 6.6 %scan_shard.5 = (bf16[512,2048]{1,0:T(8,128)(2,1)}, f32[8192,128]{1,0:T(8,128)}, f32[2,16,2048]{2,1,0:T(8,128)S(1)}, bf16[16,1152]{1,0:T(8,128)(2,1)S(1)}) custom-call(s32[8]{0:T(128)S(1)} %bitcast.11, s32[512]{0:T(512)S(1)} %copy-done.7, s32[16]{0:T(128)S(1)} %reduce_sum.9.refs_2_, ...), custom_call_target="tpu_custom_call", output_to_operand_aliasing={{0}: (13, {}), {1}: (14, {}), {2}: (15, {})} | custom-call | flops 26214400 | bytes 2621440 | tf_op jit(solution)/shard_map/scan_shard/pallas_call | solution.py:397
  128.2 9.7 %collective-permute-done.11.refs_1_ = bf16[3,128,512]{2,1,0:T(8,128)(2,1)S(1)} collective-permute-done((bf16[3,128,512]{2,1,0:T(8,128)(2,1)}, bf16[3,128,512]{2,1,0:T(8,128)(2,1)S(1)}, u32[]{:S(2)}, u32[]{:S(2)}) %collective-permute-start.11) | collective-permute-done | bytes 393248 | tf_op jit(solution)/shard_map/ppermute | solution.py:551
  139.1 3.1 %slab_fronts.6 = bf16[8,128,512]{2,1,0:T(8,128)(2,1)S(1)} custom-call(s32[1]{0:T(128)} %bitcast.1.place_ref, bf16[3,128,8192]{2,1,0:T(8,128)(2,1)} %arrived_ref.17, bf16[3,128,512]{2,1,0:T(8,128)(2,1)S(1)} %collective-permute-done.10.refs_0_, bf16[3,128,512]{2,1,0:T(8,128)(2,1)S(1)} %collective-permute-done.11.refs_1_, ...), custom_call_target="tpu_custom_call" | custom-call | flops 15728640 | bytes 2621440 | tf_op jit(solution)/shard_map/slab_fronts/pallas_call | solution.py:203
  143.1 5.1 %all-to-all-start.3 = ((bf16[8,128,512]{2,1,0:T(8,128)(2,1)}), bf16[8,128,512]{2,1,0:T(8,128)(2,1)S(1)}, u32[]{:S(2)}, u32[]{:S(2)}) async-start(bf16[8,128,512]{2,1,0:T(8,128)(2,1)} %copy-done.4), calls=%async_computation.3 | async-start | bytes 2097152 | tf_op jit(solution)/shard_map/all_to_all | solution.py:556
  148.2 6.5 %scan_shard.6 = (bf16[512,2048]{1,0:T(8,128)(2,1)}, f32[8192,128]{1,0:T(8,128)}, f32[2,16,2048]{2,1,0:T(8,128)S(1)}, bf16[16,1664]{1,0:T(8,128)(2,1)S(1)}) custom-call(s32[8]{0:T(128)S(1)} %bitcast.12, s32[512]{0:T(512)S(1)} %copy-done.7, s32[16]{0:T(128)S(1)} %reduce_sum.9.refs_2_, ...), custom_call_target="tpu_custom_call", output_to_operand_aliasing={{0}: (13, {}), {1}: (14, {}), {2}: (15, {})} | custom-call | flops 26214400 | bytes 2621440 | tf_op jit(solution)/shard_map/scan_shard/pallas_call | solution.py:397
  154.8 16.8 %all-to-all-done.3.refs_4_ = bf16[8,128,512]{2,1,0:T(8,128)(2,1)S(1)} async-done(((bf16[8,128,512]{2,1,0:T(8,128)(2,1)}), bf16[8,128,512]{2,1,0:T(8,128)(2,1)S(1)}, u32[]{:S(2)}, u32[]{:S(2)}) %all-to-all-start.3) | async-done | bytes 1048608 | tf_op jit(solution)/shard_map/all_to_all | solution.py:556
  171.6 6.7 %scan_shard.7 = (bf16[512,2048]{1,0:T(8,128)(2,1)}, f32[8192,128]{1,0:T(8,128)}, f32[2,16,2048]{2,1,0:T(8,128)S(1)}, bf16[16,2176]{1,0:T(8,128)(2,1)S(1)}) custom-call(s32[8]{0:T(128)S(1)} %bitcast.13, s32[512]{0:T(512)S(1)} %copy-done.7, s32[16]{0:T(128)S(1)} %reduce_sum.9.refs_2_, ...), custom_call_target="tpu_custom_call", output_to_operand_aliasing={{0}: (13, {}), {1}: (14, {}), {2}: (15, {})} | custom-call | flops 26214400 | bytes 2621440 | tf_op jit(solution)/shard_map/scan_shard/pallas_call | solution.py:397
  181.6 5.7 %collective-permute-start.18 = (bf16[16,2176]{1,0:T(8,128)(2,1)S(1)}, bf16[16,2176]{1,0:T(8,128)(2,1)S(1)}, u32[]{:S(2)}, u32[]{:S(2)}) collective-permute-start(bf16[16,2176]{1,0:T(8,128)(2,1)S(1)} %get-tuple-element.67), channel_id=1, source_target_pairs={{0,12},{4,16},{8,20},{12,24},{16,28},{1,13},{5,17},{9,21},{13,25},... | collective-permute-start | bytes 208904 | tf_op jit(solution)/shard_map/ppermute | solution.py:531
  192.0 5.8 %collective-permute-done.17.refs_3_ = bf16[16,2176]{1,0:T(8,128)(2,1)S(1)} collective-permute-done((bf16[16,2176]{1,0:T(8,128)(2,1)S(1)}, bf16[16,2176]{1,0:T(8,128)(2,1)S(1)}, u32[]{:S(2)}, u32[]{:S(2)}) %collective-permute-start.17) | collective-permute-done | bytes 69664 | tf_op jit(solution)/shard_map/ppermute | solution.py:531
  197.9 8.9 %carry_shard.1 = bf16[512,2048]{1,0:T(8,128)(2,1)} custom-call(s32[2]{0:T(128)S(1)} %select_reduce_fusion.refs_0_, f32[2]{0:T(128)S(1)} %compare_convert_fusion.refs_3_.refs_1_, bf16[16,2176]{1,0:T(8,128)(2,1)S(1)} %collective-permute-done.16.refs_2_, bf16[16,2176]{1,0:T(8,128)(2,1)S(1)} %collective-permute-done.17.refs_3_, ...), custom_call_target="tpu_custom_call" | custom-call | flops 41943040 | bytes 8388608 | tf_op jit(solution)/shard_map/carry_shard/pallas_call | solution.py:502
  (80 shorter events, 49.8 us)
Async XLA Ops:
  4.0 10.6 %collective-permute-start.4 = (bf16[2,24,2048]{2,1,0:T(8,128)(2,1)S(1)}, bf16[2,24,2048]{2,1,0:T(8,128)(2,1)S(1)}, u32[]{:S(2)}, u32[]{:S(2)}) collective-permute-start(bf16[2,24,2048]{2,1,0:T(8,128)(2,1)S(1)} %get-tuple-element.43), channel_id=1, source_target_pairs={{0,2},{1,3},{2,0},{3,1},{4,6},{5,7},{6,4},{7,5},{8,10},{9,11},{10,... | collective-permute-start | bytes 589832 | tf_op jit(solution)/shard_map/ppermute | solution.py:551
  5.5 9.1 %collective-permute-start.5 = (bf16[2,24,2048]{2,1,0:T(8,128)(2,1)S(1)}, bf16[2,24,2048]{2,1,0:T(8,128)(2,1)S(1)}, u32[]{:S(2)}, u32[]{:S(2)}) collective-permute-start(bf16[2,24,2048]{2,1,0:T(8,128)(2,1)S(1)} %get-tuple-element.44), channel_id=1, source_target_pairs={{0,3},{1,2},{2,1},{3,0},{4,7},{5,6},{6,5},{7,4},{8,11},{9,10},{10,... | collective-permute-start | bytes 589832 | tf_op jit(solution)/shard_map/ppermute | solution.py:551
  16.5 22.9 %all-to-all-start = ((bf16[8,24,2048]{2,1,0:T(8,128)(2,1)}), bf16[8,24,2048]{2,1,0:T(8,128)(2,1)S(1)}, u32[]{:S(2)}, u32[]{:S(2)}) async-start(bf16[8,24,2048]{2,1,0:T(8,128)(2,1)} %by_shard.1), calls=%async_computation | async-start | bytes 1572864 | tf_op jit(solution)/shard_map/all_to_all | solution.py:556
  21.7 19.6 %collective-permute-start = (bf16[3,128,512]{2,1,0:T(8,128)(2,1)S(1)}, bf16[3,128,512]{2,1,0:T(8,128)(2,1)S(1)}, u32[]{:S(2)}, u32[]{:S(2)}) collective-permute-start(bf16[3,128,512]{2,1,0:T(8,128)(2,1)S(1)} %get-tuple-element.39.refs_4_), channel_id=1, source_target_pairs={{0,1},{1,0},{2,3},{3,2},{4,5},{5,4},{6,7},{7,6},{8,9},{9,8},{10,11... | collective-permute-start | bytes 1179656 | tf_op jit(solution)/shard_map/ppermute | solution.py:551
  22.9 18.4 %collective-permute-start.1 = (bf16[3,128,512]{2,1,0:T(8,128)(2,1)S(1)}, bf16[3,128,512]{2,1,0:T(8,128)(2,1)S(1)}, u32[]{:S(2)}, u32[]{:S(2)}) collective-permute-start(bf16[3,128,512]{2,1,0:T(8,128)(2,1)S(1)} %get-tuple-element.40.refs_5_), channel_id=1, source_target_pairs={{0,2},{1,3},{2,0},{3,1},{4,6},{5,7},{6,4},{7,5},{8,10},{9,11},{10,... | collective-permute-start | bytes 1179656 | tf_op jit(solution)/shard_map/ppermute | solution.py:551
  23.8 18.5 %collective-permute-start.2 = (bf16[3,128,512]{2,1,0:T(8,128)(2,1)S(1)}, bf16[3,128,512]{2,1,0:T(8,128)(2,1)S(1)}, u32[]{:S(2)}, u32[]{:S(2)}) collective-permute-start(bf16[3,128,512]{2,1,0:T(8,128)(2,1)S(1)} %get-tuple-element.41.refs_6_), channel_id=1, source_target_pairs={{0,3},{1,2},{2,1},{3,0},{4,7},{5,6},{6,5},{7,4},{8,11},{9,10},{10,... | collective-permute-start | bytes 1179656 | tf_op jit(solution)/shard_map/ppermute | solution.py:551
  49.4 31.8 %all-to-all-start.2 = ((bf16[8,128,512]{2,1,0:T(8,128)(2,1)}), bf16[8,128,512]{2,1,0:T(8,128)(2,1)S(1)}, u32[]{:S(2)}, u32[]{:S(2)}) async-start(bf16[8,128,512]{2,1,0:T(8,128)(2,1)} %slab_fronts.4.refs_0_), calls=%async_computation.2 | async-start | bytes 2097152 | tf_op jit(solution)/shard_map/all_to_all | solution.py:556
  56.5 12.0 %collective-permute-start.7 = (bf16[3,128,512]{2,1,0:T(8,128)(2,1)S(1)}, bf16[3,128,512]{2,1,0:T(8,128)(2,1)S(1)}, u32[]{:S(2)}, u32[]{:S(2)}) collective-permute-start(bf16[3,128,512]{2,1,0:T(8,128)(2,1)S(1)} %get-tuple-element.46), channel_id=1, source_target_pairs={{0,1},{1,0},{2,3},{3,2},{4,5},{5,4},{6,7},{7,6},{8,9},{9,8},{10,11... | collective-permute-start | bytes 1179656 | tf_op jit(solution)/shard_map/ppermute | solution.py:551
  57.8 17.7 %collective-permute-start.8 = (bf16[3,128,512]{2,1,0:T(8,128)(2,1)S(1)}, bf16[3,128,512]{2,1,0:T(8,128)(2,1)S(1)}, u32[]{:S(2)}, u32[]{:S(2)}) collective-permute-start(bf16[3,128,512]{2,1,0:T(8,128)(2,1)S(1)} %get-tuple-element.47), channel_id=1, source_target_pairs={{0,2},{1,3},{2,0},{3,1},{4,6},{5,7},{6,4},{7,5},{8,10},{9,11},{10,... | collective-permute-start | bytes 1179656 | tf_op jit(solution)/shard_map/ppermute | solution.py:551
  58.6 18.5 %collective-permute-start.9 = (bf16[3,128,512]{2,1,0:T(8,128)(2,1)S(1)}, bf16[3,128,512]{2,1,0:T(8,128)(2,1)S(1)}, u32[]{:S(2)}, u32[]{:S(2)}) collective-permute-start(bf16[3,128,512]{2,1,0:T(8,128)(2,1)S(1)} %get-tuple-element.48), channel_id=1, source_target_pairs={{0,3},{1,2},{2,1},{3,0},{4,7},{5,6},{6,5},{7,4},{8,11},{9,10},{10,... | collective-permute-start | bytes 1179656 | tf_op jit(solution)/shard_map/ppermute | solution.py:551
  82.2 30.0 %all-to-all-start.1 = ((bf16[8,128,512]{2,1,0:T(8,128)(2,1)}), bf16[8,128,512]{2,1,0:T(8,128)(2,1)S(1)}, u32[]{:S(2)}, u32[]{:S(2)}) async-start(bf16[8,128,512]{2,1,0:T(8,128)(2,1)} %slab_fronts.5.refs_0_), calls=%async_computation.1 | async-start | bytes 2097152 | tf_op jit(solution)/shard_map/all_to_all | solution.py:556
  87.7 20.4 %collective-permute-start.13 = (bf16[3,128,512]{2,1,0:T(8,128)(2,1)S(1)}, bf16[3,128,512]{2,1,0:T(8,128)(2,1)S(1)}, u32[]{:S(2)}, u32[]{:S(2)}) collective-permute-start(bf16[3,128,512]{2,1,0:T(8,128)(2,1)S(1)} %get-tuple-element.49.refs_3_), channel_id=1, source_target_pairs={{0,1},{1,0},{2,3},{3,2},{4,5},{5,4},{6,7},{7,6},{8,9},{9,8},{10,11... | collective-permute-start | bytes 1179656 | tf_op jit(solution)/shard_map/ppermute | solution.py:551
  88.5 19.5 %collective-permute-start.14 = (bf16[3,128,512]{2,1,0:T(8,128)(2,1)}, bf16[3,128,512]{2,1,0:T(8,128)(2,1)S(1)}, u32[]{:S(2)}, u32[]{:S(2)}) collective-permute-start(bf16[3,128,512]{2,1,0:T(8,128)(2,1)} %get-tuple-element.58), channel_id=1, source_target_pairs={{0,2},{1,3},{2,0},{3,1},{4,6},{5,7},{6,4},{7,5},{8,10},{9,11},{10,... | collective-permute-start | bytes 1179656 | tf_op jit(solution)/shard_map/ppermute | solution.py:551
  90.0 18.0 %collective-permute-start.15 = (bf16[3,128,512]{2,1,0:T(8,128)(2,1)}, bf16[3,128,512]{2,1,0:T(8,128)(2,1)S(1)}, u32[]{:S(2)}, u32[]{:S(2)}) collective-permute-start(bf16[3,128,512]{2,1,0:T(8,128)(2,1)} %get-tuple-element.59), channel_id=1, source_target_pairs={{0,3},{1,2},{2,1},{3,0},{4,7},{5,6},{6,5},{7,4},{8,11},{9,10},{10,... | collective-permute-start | bytes 1179656 | tf_op jit(solution)/shard_map/ppermute | solution.py:551
  112.2 30.9 %all-to-all-start.4 = ((bf16[8,128,512]{2,1,0:T(8,128)(2,1)}), bf16[8,128,512]{2,1,0:T(8,128)(2,1)}, u32[]{:S(2)}, u32[]{:S(2)}) async-start(bf16[8,128,512]{2,1,0:T(8,128)(2,1)} %copy-done.1), calls=%async_computation.4 | async-start | bytes 2097152 | tf_op jit(solution)/shard_map/all_to_all | solution.py:556
  118.0 19.8 %collective-permute-start.11 = (bf16[3,128,512]{2,1,0:T(8,128)(2,1)}, bf16[3,128,512]{2,1,0:T(8,128)(2,1)S(1)}, u32[]{:S(2)}, u32[]{:S(2)}) collective-permute-start(bf16[3,128,512]{2,1,0:T(8,128)(2,1)} %copy-done.10), channel_id=1, source_target_pairs={{0,2},{1,3},{2,0},{3,1},{4,6},{5,7},{6,4},{7,5},{8,10},{9,11},{10,... | collective-permute-start | bytes 1179656 | tf_op jit(solution)/shard_map/ppermute | solution.py:551
  118.9 19.0 %collective-permute-start.12 = (bf16[3,128,512]{2,1,0:T(8,128)(2,1)}, bf16[3,128,512]{2,1,0:T(8,128)(2,1)S(1)}, u32[]{:S(2)}, u32[]{:S(2)}) collective-permute-start(bf16[3,128,512]{2,1,0:T(8,128)(2,1)} %copy-done.9), channel_id=1, source_target_pairs={{0,3},{1,2},{2,1},{3,0},{4,7},{5,6},{6,5},{7,4},{8,11},{9,10},{10,... | collective-permute-start | bytes 1179656 | tf_op jit(solution)/shard_map/ppermute | solution.py:551
  120.3 18.8 %collective-permute-start.10 = (bf16[3,128,512]{2,1,0:T(8,128)(2,1)}, bf16[3,128,512]{2,1,0:T(8,128)(2,1)S(1)}, u32[]{:S(2)}, u32[]{:S(2)}) collective-permute-start(bf16[3,128,512]{2,1,0:T(8,128)(2,1)} %copy-done.5), channel_id=1, source_target_pairs={{0,1},{1,0},{2,3},{3,2},{4,5},{5,4},{6,7},{7,6},{8,9},{9,8},{10,11... | collective-permute-start | bytes 1179656 | tf_op jit(solution)/shard_map/ppermute | solution.py:551
  143.1 28.4 %all-to-all-start.3 = ((bf16[8,128,512]{2,1,0:T(8,128)(2,1)}), bf16[8,128,512]{2,1,0:T(8,128)(2,1)S(1)}, u32[]{:S(2)}, u32[]{:S(2)}) async-start(bf16[8,128,512]{2,1,0:T(8,128)(2,1)} %copy-done.4), calls=%async_computation.3 | async-start | bytes 2097152 | tf_op jit(solution)/shard_map/all_to_all | solution.py:556
  178.9 10.3 %collective-permute-start.21 = (bf16[16,2176]{1,0:T(8,128)(2,1)S(1)}, bf16[16,2176]{1,0:T(8,128)(2,1)S(1)}, u32[]{:S(2)}, u32[]{:S(2)}) collective-permute-start(bf16[16,2176]{1,0:T(8,128)(2,1)S(1)} %get-tuple-element.67), channel_id=1, source_target_pairs={{0,24},{4,28},{1,25},{5,29},{2,26},{6,30},{3,27},{7,31}} | collective-permute-start | bytes 208904 | tf_op jit(solution)/shard_map/ppermute | solution.py:531
  179.6 12.0 %collective-permute-start.20 = (bf16[16,2176]{1,0:T(8,128)(2,1)S(1)}, bf16[16,2176]{1,0:T(8,128)(2,1)S(1)}, u32[]{:S(2)}, u32[]{:S(2)}) collective-permute-start(bf16[16,2176]{1,0:T(8,128)(2,1)S(1)} %get-tuple-element.67), channel_id=1, source_target_pairs={{0,20},{4,24},{8,28},{1,21},{5,25},{9,29},{2,22},{6,26},{10,30},{3... | collective-permute-start | bytes 208904 | tf_op jit(solution)/shard_map/ppermute | solution.py:531
  180.3 11.3 %collective-permute-start.19 = (bf16[16,2176]{1,0:T(8,128)(2,1)S(1)}, bf16[16,2176]{1,0:T(8,128)(2,1)S(1)}, u32[]{:S(2)}, u32[]{:S(2)}) collective-permute-start(bf16[16,2176]{1,0:T(8,128)(2,1)S(1)} %get-tuple-element.67), channel_id=1, source_target_pairs={{0,16},{4,20},{8,24},{12,28},{1,17},{5,21},{9,25},{13,29},{2,18},{... | collective-permute-start | bytes 208904 | tf_op jit(solution)/shard_map/ppermute | solution.py:531
  181.6 10.4 %collective-permute-start.18 = (bf16[16,2176]{1,0:T(8,128)(2,1)S(1)}, bf16[16,2176]{1,0:T(8,128)(2,1)S(1)}, u32[]{:S(2)}, u32[]{:S(2)}) collective-permute-start(bf16[16,2176]{1,0:T(8,128)(2,1)S(1)} %get-tuple-element.67), channel_id=1, source_target_pairs={{0,12},{4,16},{8,20},{12,24},{16,28},{1,13},{5,17},{9,21},{13,25},... | collective-permute-start | bytes 208904 | tf_op jit(solution)/shard_map/ppermute | solution.py:531
  187.3 10.6 %collective-permute-start.17 = (bf16[16,2176]{1,0:T(8,128)(2,1)S(1)}, bf16[16,2176]{1,0:T(8,128)(2,1)S(1)}, u32[]{:S(2)}, u32[]{:S(2)}) collective-permute-start(bf16[16,2176]{1,0:T(8,128)(2,1)S(1)} %get-tuple-element.67), channel_id=1, source_target_pairs={{0,8},{4,12},{8,16},{12,20},{16,24},{20,28},{1,9},{5,13},{9,17},{1... | collective-permute-start | bytes 208904 | tf_op jit(solution)/shard_map/ppermute | solution.py:531
  (16 other events, 173.2 us)

commit v3 on v2

--- a/solution.py
+++ b/solution.py
@@ -149,6 +149,21 @@
         compiler_params=PARAMS,
         name="by_shard",
     )(place, *parts, *later)
+
+
+def in_place(value, later):
+    def body(value_ref, later_ref, out_ref):
+        pass
+
+    return pl.pallas_call(
+        body,
+        in_specs=[ANY, ANY],
+        out_specs=ANY,
+        out_shape=jax.ShapeDtypeStruct(value.shape, value.dtype),
+        input_output_aliases={0: 0},
+        compiler_params=PARAMS,
+        name="in_place",
+    )(value, later)
 
 
 def front_body(chunk, count, place_ref, arrived_ref, *refs):
@@ -565,13 +580,15 @@
     scanned, ended = [], []
     for chunk in range(CHUNKS):
         blocks = across_plane(cuts[chunk])
-        ready = [before] if chunk == 0 else ended[chunk - 2 : chunk - 1]
+        ready = []
         if 0 < chunk < CHUNKS - 1:
             cuts.append(cut_blocks(chunk + 1, width, chans, place, arrived, [sent]))
             ready = [*ready, cuts[-1][0]]
         sent = slab_fronts(
             chunk, width, place, arrived, blocks, short_taps, per_device, ready
         )
+        if chunk == CHUNKS - 1:
+            sent = in_place(sent, before)
         if chunk == 0:
             cuts.append(cut_blocks(1, width, chans, place, arrived, [sent]))
         scanned = scan_shard(

time: 208 us -> 204 us (0.981)
  waiting for transfers between devices: 79.6 us -> 74.7 us
    all_to_all x5, waiting for transfers between devices: 28.5 us -> 1.73 us  [along_column(): return lax.all_to_all(value, 'seq', split_axis=0, concat_axis=0, tiled=True)]
    ppermute x15, waiting for transfers between devices: 41.7 us -> 66.5 us  [across_plane(): lax.ppermute(part, 'chan', [(c, c ^ d) for c in range(chans)])]
    ppermute x8, waiting for transfers between devices: 9.42 us -> 6.43 us  [passed_along(): return lax.ppermute(value, 'seq', [(i, i + by) for i in range(shards - by)])]
    unnamed x24 -> x22, local copies, waits for them, and re-layouts: 3.02 us -> 4.48 us
  transfers between devices with their start and end apart: 28 -> 28, of which waited for: 15 -> 15; matrix products, arithmetic and copies ran while one was open for 1% -> 1% of each run, Pallas kernels for 17% -> 20%
where the time goes in v3:
time: 204 us; the launch traced here: 203 us
  waiting for transfers between devices  74.7 us (37%)
  Pallas kernels  60.8 us (30%)
  starting transfers between devices  59.6 us (29%)
  local copies, waits for them, and re-layouts  4.59 us (2%)
  between operations  2.24 us (1%)
    ppermute x15, waiting for transfers between devices, across_plane(): lax.ppermute(part, 'chan', [(c, c ^ d) for c in range(chans)])  66.5 us
    all_to_all x5, starting transfers between devices, along_column(): return lax.all_to_all(value, 'seq', split_axis=0, concat_axis=0, tiled=True)  26.8 us
    pallas_call x4, Pallas kernels, scan_shard(): pl.pallas_call(functools.partial(scan_body, chunk, segments, len(shared))...  26.3 us
    ppermute x15, starting transfers between devices, across_plane(): lax.ppermute(part, 'chan', [(c, c ^ d) for c in range(chans)])  17.6 us
    pallas_call x4, Pallas kernels, slab_fronts(): pl.pallas_call(functools.partial(front_body, chunk, count), grid=(1,), in...  16.2 us
    ppermute x8, starting transfers between devices, passed_along(): return lax.ppermute(value, 'seq', [(i, i + by) for i in range(shards - by)])  15.2 us
    pallas_call x1, Pallas kernels, carry_shard(): pl.pallas_call(functools.partial(carry_body, segments, len(ends)), grid=(...  8.87 us
    ppermute x8, waiting for transfers between devices, passed_along(): return lax.ppermute(value, 'seq', [(i, i + by) for i in range(shards - by)])  6.43 us
  transfers between devices with their start and end apart: 28, of which 15 were waited for; matrix products, arithmetic and copies ran while one was open for 1% of the time, Pallas kernels for 20%

profile of v3, /device:TPU:16, one launch (start us, length us, event | category | flops | bytes accessed | tf_op | source)
XLA Modules:
  0.0 203.0 jit_solution(11497466888497068874)
XLA Ops:
  7.3 3.0 %collective-permute-done.9.refs_1_ = bf16[2,24,2048]{2,1,0:T(8,128)(2,1)S(1)} collective-permute-done((bf16[2,24,2048]{2,1,0:T(8,128)(2,1)S(1)}, bf16[2,24,2048]{2,1,0:T(8,128)(2,1)S(1)}, u32[]{:S(2)}, u32[]{:S(2)}) %collective-permute-start.9) | collective-permute-done | bytes 196640 | tf_op jit(solution)/shard_map/ppermute | solution.py:566
  10.3 4.3 %collective-permute-done.10.refs_2_ = bf16[2,24,2048]{2,1,0:T(8,128)(2,1)S(1)} collective-permute-done((bf16[2,24,2048]{2,1,0:T(8,128)(2,1)S(1)}, bf16[2,24,2048]{2,1,0:T(8,128)(2,1)S(1)}, u32[]{:S(2)}, u32[]{:S(2)}) %collective-permute-start.10) | collective-permute-done | bytes 196640 | tf_op jit(solution)/shard_map/ppermute | solution.py:566
  16.5 5.2 %all-to-all-start = ((bf16[8,24,2048]{2,1,0:T(8,128)(2,1)}), bf16[8,24,2048]{2,1,0:T(8,128)(2,1)S(1)}, u32[]{:S(2)}, u32[]{:S(2)}) async-start(bf16[8,24,2048]{2,1,0:T(8,128)(2,1)} %by_shard.1), calls=%async_computation | async-start | bytes 1572864 | tf_op jit(solution)/shard_map/all_to_all | solution.py:571
  25.2 8.5 %collective-permute-done.refs_0_ = bf16[3,128,512]{2,1,0:T(8,128)(2,1)S(1)} collective-permute-done((bf16[3,128,512]{2,1,0:T(8,128)(2,1)S(1)}, bf16[3,128,512]{2,1,0:T(8,128)(2,1)S(1)}, u32[]{:S(2)}, u32[]{:S(2)}) %collective-permute-start) | collective-permute-done | bytes 393248 | tf_op jit(solution)/shard_map/ppermute | solution.py:566
  33.7 7.0 %collective-permute-done.1.refs_1_ = bf16[3,128,512]{2,1,0:T(8,128)(2,1)S(1)} collective-permute-done((bf16[3,128,512]{2,1,0:T(8,128)(2,1)S(1)}, bf16[3,128,512]{2,1,0:T(8,128)(2,1)S(1)}, u32[]{:S(2)}, u32[]{:S(2)}) %collective-permute-start.1) | collective-permute-done | bytes 393248 | tf_op jit(solution)/shard_map/ppermute | solution.py:566
  42.3 4.0 %slab_fronts.4.refs_0_ = bf16[8,128,512]{2,1,0:T(8,128)(2,1)} custom-call(s32[1]{0:T(128)} %bitcast.1.place_ref, bf16[3,128,8192]{2,1,0:T(8,128)(2,1)} %arrived_ref.17, bf16[3,128,512]{2,1,0:T(8,128)(2,1)S(1)} %collective-permute-done.refs_0_, bf16[3,128,512]{2,1,0:T(8,128)(2,1)S(1)} %collective-permute-done.1.refs_1_, ...), custom_call_target="tpu_custom_call" | custom-call | flops 15728640 | bytes 2621440 | tf_op jit(solution)/shard_map/slab_fronts/pallas_call | solution.py:218
  46.3 5.1 %all-to-all-start.4 = ((bf16[8,128,512]{2,1,0:T(8,128)(2,1)}), bf16[8,128,512]{2,1,0:T(8,128)(2,1)S(1)}, u32[]{:S(2)}, u32[]{:S(2)}) async-start(bf16[8,128,512]{2,1,0:T(8,128)(2,1)} %slab_fronts.4.refs_0_), calls=%async_computation.4 | async-start | bytes 2097152 | tf_op jit(solution)/shard_map/all_to_all | solution.py:571
  59.1 5.7 %collective-permute-done.3.refs_0_ = bf16[3,128,512]{2,1,0:T(8,128)(2,1)S(1)} collective-permute-done((bf16[3,128,512]{2,1,0:T(8,128)(2,1)S(1)}, bf16[3,128,512]{2,1,0:T(8,128)(2,1)S(1)}, u32[]{:S(2)}, u32[]{:S(2)}) %collective-permute-start.3) | collective-permute-done | bytes 393248 | tf_op jit(solution)/shard_map/ppermute | solution.py:566
  64.7 8.2 %collective-permute-done.4.refs_1_ = bf16[3,128,512]{2,1,0:T(8,128)(2,1)S(1)} collective-permute-done((bf16[3,128,512]{2,1,0:T(8,128)(2,1)S(1)}, bf16[3,128,512]{2,1,0:T(8,128)(2,1)S(1)}, u32[]{:S(2)}, u32[]{:S(2)}) %collective-permute-start.4) | collective-permute-done | bytes 393248 | tf_op jit(solution)/shard_map/ppermute | solution.py:566
  72.9 4.1 %slab_fronts.5.refs_0_ = bf16[8,128,512]{2,1,0:T(8,128)(2,1)} custom-call(s32[1]{0:T(128)} %bitcast.1.place_ref, bf16[3,128,8192]{2,1,0:T(8,128)(2,1)} %arrived_ref.17, bf16[3,128,512]{2,1,0:T(8,128)(2,1)S(1)} %collective-permute-done.3.refs_0_, bf16[3,128,512]{2,1,0:T(8,128)(2,1)S(1)} %collective-permute-done.4.refs_1_, ...), custom_call_target="tpu_custom_call" | custom-call | flops 15728640 | bytes 2621440 | tf_op jit(solution)/shard_map/slab_fronts/pallas_call | solution.py:218
  78.0 5.1 %all-to-all-start.3 = ((bf16[8,128,512]{2,1,0:T(8,128)(2,1)}), bf16[8,128,512]{2,1,0:T(8,128)(2,1)S(1)}, u32[]{:S(2)}, u32[]{:S(2)}) async-start(bf16[8,128,512]{2,1,0:T(8,128)(2,1)} %slab_fronts.5.refs_0_), calls=%async_computation.3 | async-start | bytes 2097152 | tf_op jit(solution)/shard_map/all_to_all | solution.py:571
  88.6 14.3 %collective-permute-done.14.refs_1_ = bf16[3,128,512]{2,1,0:T(8,128)(2,1)S(1)} collective-permute-done((bf16[3,128,512]{2,1,0:T(8,128)(2,1)}, bf16[3,128,512]{2,1,0:T(8,128)(2,1)S(1)}, u32[]{:S(2)}, u32[]{:S(2)}) %collective-permute-start.14) | collective-permute-done | bytes 393248 | tf_op jit(solution)/shard_map/ppermute | solution.py:566
  104.1 4.1 %slab_fronts.7 = bf16[8,128,512]{2,1,0:T(8,128)(2,1)} custom-call(s32[1]{0:T(128)} %bitcast.1.place_ref, bf16[3,128,8192]{2,1,0:T(8,128)(2,1)} %arrived_ref.17, bf16[3,128,512]{2,1,0:T(8,128)(2,1)S(1)} %collective-permute-done.13.refs_0_, bf16[3,128,512]{2,1,0:T(8,128)(2,1)S(1)} %collective-permute-done.14.refs_1_, ...), custom_call_target="tpu_custom_call" | custom-call | flops 15728640 | bytes 2621440 | tf_op jit(solution)/shard_map/slab_fronts/pallas_call | solution.py:218
  108.2 5.6 %all-to-all-start.2 = ((bf16[8,128,512]{2,1,0:T(8,128)(2,1)}), bf16[8,128,512]{2,1,0:T(8,128)(2,1)}, u32[]{:S(2)}, u32[]{:S(2)}) async-start(bf16[8,128,512]{2,1,0:T(8,128)(2,1)} %slab_fronts.7), calls=%async_computation.2 | async-start | bytes 2097152 | tf_op jit(solution)/shard_map/all_to_all | solution.py:571
  121.8 12.8 %collective-permute-done.7.refs_1_ = bf16[3,128,512]{2,1,0:T(8,128)(2,1)} collective-permute-done((bf16[3,128,512]{2,1,0:T(8,128)(2,1)}, bf16[3,128,512]{2,1,0:T(8,128)(2,1)}, u32[]{:S(2)}, u32[]{:S(2)}) %collective-permute-start.7) | collective-permute-done | bytes 393248 | tf_op jit(solution)/shard_map/ppermute | solution.py:566
  134.7 4.0 %slab_fronts.6.value_ref = bf16[8,128,512]{2,1,0:T(8,128)(2,1)} custom-call(s32[1]{0:T(128)} %bitcast.1.place_ref, bf16[3,128,8192]{2,1,0:T(8,128)(2,1)} %arrived_ref.17, bf16[3,128,512]{2,1,0:T(8,128)(2,1)S(1)} %collective-permute-done.6.refs_0_, bf16[3,128,512]{2,1,0:T(8,128)(2,1)} %collective-permute-done.7.refs_1_, ...), custom_call_target="tpu_custom_call" | custom-call | flops 15728640 | bytes 2621440 | tf_op jit(solution)/shard_map/slab_fronts/pallas_call | solution.py:218
  138.9 5.8 %all-to-all-start.1 = ((bf16[8,128,512]{2,1,0:T(8,128)(2,1)}), bf16[8,128,512]{2,1,0:T(8,128)(2,1)}, u32[]{:S(2)}, u32[]{:S(2)}) async-start(bf16[8,128,512]{2,1,0:T(8,128)(2,1)} %in_place.1), calls=%async_computation.1 | async-start | bytes 2097152 | tf_op jit(solution)/shard_map/all_to_all | solution.py:571
  146.4 6.7 %scan_shard.4 = (bf16[512,2048]{1,0:T(8,128)(2,1)}, f32[8192,128]{1,0:T(8,128)}, f32[2,16,2048]{2,1,0:T(8,128)S(1)}, bf16[16,640]{1,0:T(8,128)(2,1)S(1)}) custom-call(s32[8]{0:T(128)S(1)} %bitcast.10, s32[512]{0:T(512)S(1)} %copy-done.4, s32[16]{0:T(128)S(1)} %reduce_sum.9.refs_2_, f32[2]{0:T(128)S(1)} %compare_convert_fusion.refs_3_.refs_1_, ...), custom_call_target="tpu_custom_call" | custom-call | flops 26214400 | bytes 2621440 | tf_op jit(solution)/shard_map/scan_shard/pallas_call | solution.py:412
  153.1 6.7 %scan_shard.5 = (bf16[512,2048]{1,0:T(8,128)(2,1)}, f32[8192,128]{1,0:T(8,128)}, f32[2,16,2048]{2,1,0:T(8,128)S(1)}, bf16[16,1152]{1,0:T(8,128)(2,1)S(1)}) custom-call(s32[8]{0:T(128)S(1)} %bitcast.11, s32[512]{0:T(512)S(1)} %copy-done.4, s32[16]{0:T(128)S(1)} %reduce_sum.9.refs_2_, ...), custom_call_target="tpu_custom_call", output_to_operand_aliasing={{0}: (13, {}), {1}: (14, {}), {2}: (15, {})} | custom-call | flops 26214400 | bytes 2621440 | tf_op jit(solution)/shard_map/scan_shard/pallas_call | solution.py:412
  159.7 6.5 %scan_shard.6 = (bf16[512,2048]{1,0:T(8,128)(2,1)}, f32[8192,128]{1,0:T(8,128)}, f32[2,16,2048]{2,1,0:T(8,128)S(1)}, bf16[16,1664]{1,0:T(8,128)(2,1)S(1)}) custom-call(s32[8]{0:T(128)S(1)} %bitcast.12, s32[512]{0:T(512)S(1)} %copy-done.4, s32[16]{0:T(128)S(1)} %reduce_sum.9.refs_2_, ...), custom_call_target="tpu_custom_call", output_to_operand_aliasing={{0}: (13, {}), {1}: (14, {}), {2}: (15, {})} | custom-call | flops 26214400 | bytes 2621440 | tf_op jit(solution)/shard_map/scan_shard/pallas_call | solution.py:412
  168.0 6.5 %scan_shard.7 = (bf16[512,2048]{1,0:T(8,128)(2,1)}, f32[8192,128]{1,0:T(8,128)}, f32[2,16,2048]{2,1,0:T(8,128)S(1)}, bf16[16,2176]{1,0:T(8,128)(2,1)S(1)}) custom-call(s32[8]{0:T(128)S(1)} %bitcast.13, s32[512]{0:T(512)S(1)} %copy-done.4, s32[16]{0:T(128)S(1)} %reduce_sum.9.refs_2_, ...), custom_call_target="tpu_custom_call", output_to_operand_aliasing={{0}: (13, {}), {1}: (14, {}), {2}: (15, {})} | custom-call | flops 26214400 | bytes 2621440 | tf_op jit(solution)/shard_map/scan_shard/pallas_call | solution.py:412
  177.8 5.7 %collective-permute-start.18 = (bf16[16,2176]{1,0:T(8,128)(2,1)S(1)}, bf16[16,2176]{1,0:T(8,128)(2,1)S(1)}, u32[]{:S(2)}, u32[]{:S(2)}) collective-permute-start(bf16[16,2176]{1,0:T(8,128)(2,1)S(1)} %get-tuple-element.67), channel_id=1, source_target_pairs={{0,12},{4,16},{8,20},{12,24},{16,28},{1,13},{5,17},{9,21},{13,25},... | collective-permute-start | bytes 208904 | tf_op jit(solution)/shard_map/ppermute | solution.py:546
  188.2 5.8 %collective-permute-done.17.refs_3_ = bf16[16,2176]{1,0:T(8,128)(2,1)S(1)} collective-permute-done((bf16[16,2176]{1,0:T(8,128)(2,1)S(1)}, bf16[16,2176]{1,0:T(8,128)(2,1)S(1)}, u32[]{:S(2)}, u32[]{:S(2)}) %collective-permute-start.17) | collective-permute-done | bytes 69664 | tf_op jit(solution)/shard_map/ppermute | solution.py:546
  194.2 8.9 %carry_shard.1 = bf16[512,2048]{1,0:T(8,128)(2,1)} custom-call(s32[2]{0:T(128)S(1)} %select_reduce_fusion.refs_0_, f32[2]{0:T(128)S(1)} %compare_convert_fusion.refs_3_.refs_1_, bf16[16,2176]{1,0:T(8,128)(2,1)S(1)} %collective-permute-done.16.refs_2_, bf16[16,2176]{1,0:T(8,128)(2,1)S(1)} %collective-permute-done.17.refs_3_, ...), custom_call_target="tpu_custom_call" | custom-call | flops 41943040 | bytes 8388608 | tf_op jit(solution)/shard_map/carry_shard/pallas_call | solution.py:517
  (79 shorter events, 47.3 us)
Async XLA Ops:
  4.0 10.6 %collective-permute-start.10 = (bf16[2,24,2048]{2,1,0:T(8,128)(2,1)S(1)}, bf16[2,24,2048]{2,1,0:T(8,128)(2,1)S(1)}, u32[]{:S(2)}, u32[]{:S(2)}) collective-permute-start(bf16[2,24,2048]{2,1,0:T(8,128)(2,1)S(1)} %get-tuple-element.50), channel_id=1, source_target_pairs={{0,2},{1,3},{2,0},{3,1},{4,6},{5,7},{6,4},{7,5},{8,10},{9,11},{10,... | collective-permute-start | bytes 589832 | tf_op jit(solution)/shard_map/ppermute | solution.py:566
  16.5 29.8 %all-to-all-start = ((bf16[8,24,2048]{2,1,0:T(8,128)(2,1)}), bf16[8,24,2048]{2,1,0:T(8,128)(2,1)S(1)}, u32[]{:S(2)}, u32[]{:S(2)}) async-start(bf16[8,24,2048]{2,1,0:T(8,128)(2,1)} %by_shard.1), calls=%async_computation | async-start | bytes 1572864 | tf_op jit(solution)/shard_map/all_to_all | solution.py:571
  21.7 12.0 %collective-permute-start = (bf16[3,128,512]{2,1,0:T(8,128)(2,1)S(1)}, bf16[3,128,512]{2,1,0:T(8,128)(2,1)S(1)}, u32[]{:S(2)}, u32[]{:S(2)}) collective-permute-start(bf16[3,128,512]{2,1,0:T(8,128)(2,1)S(1)} %get-tuple-element.39.refs_4_), channel_id=1, source_target_pairs={{0,1},{1,0},{2,3},{3,2},{4,5},{5,4},{6,7},{7,6},{8,9},{9,8},{10,11... | collective-permute-start | bytes 1179656 | tf_op jit(solution)/shard_map/ppermute | solution.py:566
  22.9 17.7 %collective-permute-start.1 = (bf16[3,128,512]{2,1,0:T(8,128)(2,1)S(1)}, bf16[3,128,512]{2,1,0:T(8,128)(2,1)S(1)}, u32[]{:S(2)}, u32[]{:S(2)}) collective-permute-start(bf16[3,128,512]{2,1,0:T(8,128)(2,1)S(1)} %get-tuple-element.40.refs_5_), channel_id=1, source_target_pairs={{0,2},{1,3},{2,0},{3,1},{4,6},{5,7},{6,4},{7,5},{8,10},{9,11},{10,... | collective-permute-start | bytes 1179656 | tf_op jit(solution)/shard_map/ppermute | solution.py:566
  23.8 18.5 %collective-permute-start.2 = (bf16[3,128,512]{2,1,0:T(8,128)(2,1)S(1)}, bf16[3,128,512]{2,1,0:T(8,128)(2,1)S(1)}, u32[]{:S(2)}, u32[]{:S(2)}) collective-permute-start(bf16[3,128,512]{2,1,0:T(8,128)(2,1)S(1)} %get-tuple-element.41.refs_6_), channel_id=1, source_target_pairs={{0,3},{1,2},{2,1},{3,0},{4,7},{5,6},{6,5},{7,4},{8,11},{9,10},{10,... | collective-permute-start | bytes 1179656 | tf_op jit(solution)/shard_map/ppermute | solution.py:566
  46.3 30.6 %all-to-all-start.4 = ((bf16[8,128,512]{2,1,0:T(8,128)(2,1)}), bf16[8,128,512]{2,1,0:T(8,128)(2,1)S(1)}, u32[]{:S(2)}, u32[]{:S(2)}) async-start(bf16[8,128,512]{2,1,0:T(8,128)(2,1)} %slab_fronts.4.refs_0_), calls=%async_computation.4 | async-start | bytes 2097152 | tf_op jit(solution)/shard_map/all_to_all | solution.py:571
  52.7 12.0 %collective-permute-start.3 = (bf16[3,128,512]{2,1,0:T(8,128)(2,1)S(1)}, bf16[3,128,512]{2,1,0:T(8,128)(2,1)S(1)}, u32[]{:S(2)}, u32[]{:S(2)}) collective-permute-start(bf16[3,128,512]{2,1,0:T(8,128)(2,1)S(1)} %get-tuple-element.42), channel_id=1, source_target_pairs={{0,1},{1,0},{2,3},{3,2},{4,5},{5,4},{6,7},{7,6},{8,9},{9,8},{10,11... | collective-permute-start | bytes 1179656 | tf_op jit(solution)/shard_map/ppermute | solution.py:566
  53.6 19.3 %collective-permute-start.4 = (bf16[3,128,512]{2,1,0:T(8,128)(2,1)S(1)}, bf16[3,128,512]{2,1,0:T(8,128)(2,1)S(1)}, u32[]{:S(2)}, u32[]{:S(2)}) collective-permute-start(bf16[3,128,512]{2,1,0:T(8,128)(2,1)S(1)} %get-tuple-element.43), channel_id=1, source_target_pairs={{0,2},{1,3},{2,0},{3,1},{4,6},{5,7},{6,4},{7,5},{8,10},{9,11},{10,... | collective-permute-start | bytes 1179656 | tf_op jit(solution)/shard_map/ppermute | solution.py:566
  55.1 17.8 %collective-permute-start.5 = (bf16[3,128,512]{2,1,0:T(8,128)(2,1)S(1)}, bf16[3,128,512]{2,1,0:T(8,128)(2,1)S(1)}, u32[]{:S(2)}, u32[]{:S(2)}) collective-permute-start(bf16[3,128,512]{2,1,0:T(8,128)(2,1)S(1)} %get-tuple-element.44), channel_id=1, source_target_pairs={{0,3},{1,2},{2,1},{3,0},{4,7},{5,6},{6,5},{7,4},{8,11},{9,10},{10,... | collective-permute-start | bytes 1179656 | tf_op jit(solution)/shard_map/ppermute | solution.py:566
  78.0 30.2 %all-to-all-start.3 = ((bf16[8,128,512]{2,1,0:T(8,128)(2,1)}), bf16[8,128,512]{2,1,0:T(8,128)(2,1)S(1)}, u32[]{:S(2)}, u32[]{:S(2)}) async-start(bf16[8,128,512]{2,1,0:T(8,128)(2,1)} %slab_fronts.5.refs_0_), calls=%async_computation.3 | async-start | bytes 2097152 | tf_op jit(solution)/shard_map/all_to_all | solution.py:571
  83.1 19.8 %collective-permute-start.14 = (bf16[3,128,512]{2,1,0:T(8,128)(2,1)}, bf16[3,128,512]{2,1,0:T(8,128)(2,1)S(1)}, u32[]{:S(2)}, u32[]{:S(2)}) collective-permute-start(bf16[3,128,512]{2,1,0:T(8,128)(2,1)} %copy-done.8), channel_id=1, source_target_pairs={{0,2},{1,3},{2,0},{3,1},{4,6},{5,7},{6,4},{7,5},{8,10},{9,11},{10,... | collective-permute-start | bytes 1179656 | tf_op jit(solution)/shard_map/ppermute | solution.py:566
  84.6 18.3 %collective-permute-start.15 = (bf16[3,128,512]{2,1,0:T(8,128)(2,1)}, bf16[3,128,512]{2,1,0:T(8,128)(2,1)S(1)}, u32[]{:S(2)}, u32[]{:S(2)}) collective-permute-start(bf16[3,128,512]{2,1,0:T(8,128)(2,1)} %copy-done.7), channel_id=1, source_target_pairs={{0,3},{1,2},{2,1},{3,0},{4,7},{5,6},{6,5},{7,4},{8,11},{9,10},{10,... | collective-permute-start | bytes 1179656 | tf_op jit(solution)/shard_map/ppermute | solution.py:566
  85.8 18.3 %collective-permute-start.13 = (bf16[3,128,512]{2,1,0:T(8,128)(2,1)S(1)}, bf16[3,128,512]{2,1,0:T(8,128)(2,1)S(1)}, u32[]{:S(2)}, u32[]{:S(2)}) collective-permute-start(bf16[3,128,512]{2,1,0:T(8,128)(2,1)S(1)} %get-tuple-element.45.refs_3_), channel_id=1, source_target_pairs={{0,1},{1,0},{2,3},{3,2},{4,5},{5,4},{6,7},{7,6},{8,9},{9,8},{10,11... | collective-permute-start | bytes 1179656 | tf_op jit(solution)/shard_map/ppermute | solution.py:566
  108.2 30.7 %all-to-all-start.2 = ((bf16[8,128,512]{2,1,0:T(8,128)(2,1)}), bf16[8,128,512]{2,1,0:T(8,128)(2,1)}, u32[]{:S(2)}, u32[]{:S(2)}) async-start(bf16[8,128,512]{2,1,0:T(8,128)(2,1)} %slab_fronts.7), calls=%async_computation.2 | async-start | bytes 2097152 | tf_op jit(solution)/shard_map/all_to_all | solution.py:571
  113.8 20.9 %collective-permute-start.6 = (bf16[3,128,512]{2,1,0:T(8,128)(2,1)S(1)}, bf16[3,128,512]{2,1,0:T(8,128)(2,1)S(1)}, u32[]{:S(2)}, u32[]{:S(2)}) collective-permute-start(bf16[3,128,512]{2,1,0:T(8,128)(2,1)S(1)} %get-tuple-element.46.refs_3_), channel_id=1, source_target_pairs={{0,1},{1,0},{2,3},{3,2},{4,5},{5,4},{6,7},{7,6},{8,9},{9,8},{10,11... | collective-permute-start | bytes 1179656 | tf_op jit(solution)/shard_map/ppermute | solution.py:566
  115.0 19.6 %collective-permute-start.7 = (bf16[3,128,512]{2,1,0:T(8,128)(2,1)}, bf16[3,128,512]{2,1,0:T(8,128)(2,1)}, u32[]{:S(2)}, u32[]{:S(2)}) collective-permute-start(bf16[3,128,512]{2,1,0:T(8,128)(2,1)} %copy-done.6), channel_id=1, source_target_pairs={{0,2},{1,3},{2,0},{3,1},{4,6},{5,7},{6,4},{7,5},{8,10},{9,11},{10,... | collective-permute-start | bytes 1179656 | tf_op jit(solution)/shard_map/ppermute | solution.py:566
  115.9 18.8 %collective-permute-start.8 = (bf16[3,128,512]{2,1,0:T(8,128)(2,1)S(1)}, bf16[3,128,512]{2,1,0:T(8,128)(2,1)}, u32[]{:S(2)}, u32[]{:S(2)}) collective-permute-start(bf16[3,128,512]{2,1,0:T(8,128)(2,1)S(1)} %get-tuple-element.48), channel_id=1, source_target_pairs={{0,3},{1,2},{2,1},{3,0},{4,7},{5,6},{6,5},{7,4},{8,11},{9,10},{10,... | collective-permute-start | bytes 1179656 | tf_op jit(solution)/shard_map/ppermute | solution.py:566
  119.9 19.0 %collective-permute-start.12 = (bf16[24,2048]{1,0:T(8,128)(2,1)S(1)}, bf16[24,2048]{1,0:T(8,128)(2,1)S(1)}, u32[]{:S(2)}, u32[]{:S(2)}) collective-permute-start(bf16[24,2048]{1,0:T(8,128)(2,1)S(1)} %dynamic-slice_bitcast_fusion), channel_id=1, source_target_pairs={{0,4},{4,8},{8,12},{12,16},{16,20},{20,24},{24,28},{1,5},{5,9},{9,... | collective-permute-start | bytes 294920 | tf_op jit(solution)/shard_map/ppermute | solution.py:546
  138.9 29.1 %all-to-all-start.1 = ((bf16[8,128,512]{2,1,0:T(8,128)(2,1)}), bf16[8,128,512]{2,1,0:T(8,128)(2,1)}, u32[]{:S(2)}, u32[]{:S(2)}) async-start(bf16[8,128,512]{2,1,0:T(8,128)(2,1)} %in_place.1), calls=%async_computation.1 | async-start | bytes 2097152 | tf_op jit(solution)/shard_map/all_to_all | solution.py:571
  175.1 10.3 %collective-permute-start.21 = (bf16[16,2176]{1,0:T(8,128)(2,1)S(1)}, bf16[16,2176]{1,0:T(8,128)(2,1)S(1)}, u32[]{:S(2)}, u32[]{:S(2)}) collective-permute-start(bf16[16,2176]{1,0:T(8,128)(2,1)S(1)} %get-tuple-element.67), channel_id=1, source_target_pairs={{0,24},{4,28},{1,25},{5,29},{2,26},{6,30},{3,27},{7,31}} | collective-permute-start | bytes 208904 | tf_op jit(solution)/shard_map/ppermute | solution.py:546
  175.8 12.0 %collective-permute-start.20 = (bf16[16,2176]{1,0:T(8,128)(2,1)S(1)}, bf16[16,2176]{1,0:T(8,128)(2,1)S(1)}, u32[]{:S(2)}, u32[]{:S(2)}) collective-permute-start(bf16[16,2176]{1,0:T(8,128)(2,1)S(1)} %get-tuple-element.67), channel_id=1, source_target_pairs={{0,20},{4,24},{8,28},{1,21},{5,25},{9,29},{2,22},{6,26},{10,30},{3... | collective-permute-start | bytes 208904 | tf_op jit(solution)/shard_map/ppermute | solution.py:546
  176.5 11.4 %collective-permute-start.19 = (bf16[16,2176]{1,0:T(8,128)(2,1)S(1)}, bf16[16,2176]{1,0:T(8,128)(2,1)S(1)}, u32[]{:S(2)}, u32[]{:S(2)}) collective-permute-start(bf16[16,2176]{1,0:T(8,128)(2,1)S(1)} %get-tuple-element.67), channel_id=1, source_target_pairs={{0,16},{4,20},{8,24},{12,28},{1,17},{5,21},{9,25},{13,29},{2,18},{... | collective-permute-start | bytes 208904 | tf_op jit(solution)/shard_map/ppermute | solution.py:546
  177.8 10.5 %collective-permute-start.18 = (bf16[16,2176]{1,0:T(8,128)(2,1)S(1)}, bf16[16,2176]{1,0:T(8,128)(2,1)S(1)}, u32[]{:S(2)}, u32[]{:S(2)}) collective-permute-start(bf16[16,2176]{1,0:T(8,128)(2,1)S(1)} %get-tuple-element.67), channel_id=1, source_target_pairs={{0,12},{4,16},{8,20},{12,24},{16,28},{1,13},{5,17},{9,21},{13,25},... | collective-permute-start | bytes 208904 | tf_op jit(solution)/shard_map/ppermute | solution.py:546
  183.5 10.6 %collective-permute-start.17 = (bf16[16,2176]{1,0:T(8,128)(2,1)S(1)}, bf16[16,2176]{1,0:T(8,128)(2,1)S(1)}, u32[]{:S(2)}, u32[]{:S(2)}) collective-permute-start(bf16[16,2176]{1,0:T(8,128)(2,1)S(1)} %get-tuple-element.67), channel_id=1, source_target_pairs={{0,8},{4,12},{8,16},{12,20},{16,24},{20,28},{1,9},{5,13},{9,17},{1... | collective-permute-start | bytes 208904 | tf_op jit(solution)/shard_map/ppermute | solution.py:546
  (15 other events, 113.5 us)

commit v4 on v3

--- a/solution.py
+++ b/solution.py
@@ -208,7 +208,7 @@
             out_ref[shard, slab:, lanes] = gate.astype(out_ref.dtype)
             return carry
 
-        lax.fori_loop(0, per_device * blocks, one_block, 0)
+        lax.fori_loop(0, per_device * blocks, one_block, 0, unroll=2)
 
 
 def slab_fronts(chunk, width, place, arrived, blocks, taps, per_device, after):
@@ -427,8 +427,8 @@
         scratch_shapes=[
             pltpu.VMEM((count, rows, width), jnp.bfloat16),
             pltpu.VMEM((count + 1, edges.shape[1], width), jnp.bfloat16),
-            pltpu.VMEM((length * blocks, LANES), jnp.float32),
-            pltpu.VMEM((3, modes * sub, LANES), jnp.float32),
+            pltpu.VMEM((length * blocks + sub, LANES), jnp.float32),
+            pltpu.VMEM((3, (modes + 1) * sub, LANES), jnp.float32),
             pltpu.SemaphoreType.DMA((2 * count + 1,)),
         ],
         compiler_params=PARAMS,
@@ -521,8 +521,8 @@
         out_specs=pl.BlockSpec((length, width), lambda g: (0, g)),
         out_shape=jax.ShapeDtypeStruct((length, channels), jnp.bfloat16),
         scratch_shapes=[
-            pltpu.VMEM((2, modes * sub, LANES), jnp.float32),
-            pltpu.VMEM((length * blocks, LANES), jnp.float32),
+            pltpu.VMEM((2, (modes + 1) * sub, LANES), jnp.float32),
+            pltpu.VMEM((length * blocks + sub, LANES), jnp.float32),
         ],
         compiler_params=pltpu.CompilerParams(vmem_limit_bytes=52 * 1024 * 1024),
         cost_estimate=pl.CostEstimate(

time: 204 us -> 204 us (level)
  no operation moved by 1% of the time
where the time goes in v4:
time: 204 us; the launch traced here: 203 us
  waiting for transfers between devices  74.8 us (37%)
  Pallas kernels  60.2 us (30%)
  starting transfers between devices  59.8 us (29%)
  local copies, waits for them, and re-layouts  4.59 us (2%)
  between operations  2.24 us (1%)
    ppermute x15, waiting for transfers between devices, across_plane(): lax.ppermute(part, 'chan', [(c, c ^ d) for c in range(chans)])  66.5 us
    all_to_all x5, starting transfers between devices, along_column(): return lax.all_to_all(value, 'seq', split_axis=0, concat_axis=0, tiled=True)  27 us
    pallas_call x4, Pallas kernels, scan_shard(): pl.pallas_call(functools.partial(scan_body, chunk, segments, len(shared))...  26.3 us
    ppermute x15, starting transfers between devices, across_plane(): lax.ppermute(part, 'chan', [(c, c ^ d) for c in range(chans)])  17.6 us
    pallas_call x4, Pallas kernels, slab_fronts(): pl.pallas_call(functools.partial(front_body, chunk, count), grid=(1,), in...  15.6 us
    ppermute x8, starting transfers between devices, passed_along(): return lax.ppermute(value, 'seq', [(i, i + by) for i in range(shards - by)])  15.2 us
    pallas_call x1, Pallas kernels, carry_shard(): pl.pallas_call(functools.partial(carry_body, segments, len(ends)), grid=(...  8.87 us
    ppermute x8, waiting for transfers between devices, passed_along(): return lax.ppermute(value, 'seq', [(i, i + by) for i in range(shards - by)])  6.58 us
  transfers between devices with their start and end apart: 28, of which 15 were waited for; matrix products, arithmetic and copies ran while one was open for 1% of the time, Pallas kernels for 20%

profile of v4, /device:TPU:16, one launch (start us, length us, event | category | flops | bytes accessed | tf_op | source)
XLA Modules:
  0.0 202.7 jit_solution(9600510932721471311)
XLA Ops:
  7.3 3.0 %collective-permute-done.9.refs_1_ = bf16[2,24,2048]{2,1,0:T(8,128)(2,1)S(1)} collective-permute-done((bf16[2,24,2048]{2,1,0:T(8,128)(2,1)S(1)}, bf16[2,24,2048]{2,1,0:T(8,128)(2,1)S(1)}, u32[]{:S(2)}, u32[]{:S(2)}) %collective-permute-start.9) | collective-permute-done | bytes 196640 | tf_op jit(solution)/shard_map/ppermute | solution.py:566
  10.3 4.3 %collective-permute-done.10.refs_2_ = bf16[2,24,2048]{2,1,0:T(8,128)(2,1)S(1)} collective-permute-done((bf16[2,24,2048]{2,1,0:T(8,128)(2,1)S(1)}, bf16[2,24,2048]{2,1,0:T(8,128)(2,1)S(1)}, u32[]{:S(2)}, u32[]{:S(2)}) %collective-permute-start.10) | collective-permute-done | bytes 196640 | tf_op jit(solution)/shard_map/ppermute | solution.py:566
  16.5 5.2 %all-to-all-start = ((bf16[8,24,2048]{2,1,0:T(8,128)(2,1)}), bf16[8,24,2048]{2,1,0:T(8,128)(2,1)S(1)}, u32[]{:S(2)}, u32[]{:S(2)}) async-start(bf16[8,24,2048]{2,1,0:T(8,128)(2,1)} %by_shard.1), calls=%async_computation | async-start | bytes 1572864 | tf_op jit(solution)/shard_map/all_to_all | solution.py:571
  25.2 8.5 %collective-permute-done.refs_0_ = bf16[3,128,512]{2,1,0:T(8,128)(2,1)S(1)} collective-permute-done((bf16[3,128,512]{2,1,0:T(8,128)(2,1)S(1)}, bf16[3,128,512]{2,1,0:T(8,128)(2,1)S(1)}, u32[]{:S(2)}, u32[]{:S(2)}) %collective-permute-start) | collective-permute-done | bytes 393248 | tf_op jit(solution)/shard_map/ppermute | solution.py:566
  33.7 7.0 %collective-permute-done.1.refs_1_ = bf16[3,128,512]{2,1,0:T(8,128)(2,1)S(1)} collective-permute-done((bf16[3,128,512]{2,1,0:T(8,128)(2,1)S(1)}, bf16[3,128,512]{2,1,0:T(8,128)(2,1)S(1)}, u32[]{:S(2)}, u32[]{:S(2)}) %collective-permute-start.1) | collective-permute-done | bytes 393248 | tf_op jit(solution)/shard_map/ppermute | solution.py:566
  42.3 3.9 %slab_fronts.4.refs_0_ = bf16[8,128,512]{2,1,0:T(8,128)(2,1)} custom-call(s32[1]{0:T(128)} %bitcast.1.place_ref, bf16[3,128,8192]{2,1,0:T(8,128)(2,1)} %arrived_ref.17, bf16[3,128,512]{2,1,0:T(8,128)(2,1)S(1)} %collective-permute-done.refs_0_, bf16[3,128,512]{2,1,0:T(8,128)(2,1)S(1)} %collective-permute-done.1.refs_1_, ...), custom_call_target="tpu_custom_call" | custom-call | flops 15728640 | bytes 2621440 | tf_op jit(solution)/shard_map/slab_fronts/pallas_call | solution.py:218
  46.2 5.1 %all-to-all-start.4 = ((bf16[8,128,512]{2,1,0:T(8,128)(2,1)}), bf16[8,128,512]{2,1,0:T(8,128)(2,1)S(1)}, u32[]{:S(2)}, u32[]{:S(2)}) async-start(bf16[8,128,512]{2,1,0:T(8,128)(2,1)} %slab_fronts.4.refs_0_), calls=%async_computation.4 | async-start | bytes 2097152 | tf_op jit(solution)/shard_map/all_to_all | solution.py:571
  58.9 5.7 %collective-permute-done.3.refs_0_ = bf16[3,128,512]{2,1,0:T(8,128)(2,1)S(1)} collective-permute-done((bf16[3,128,512]{2,1,0:T(8,128)(2,1)S(1)}, bf16[3,128,512]{2,1,0:T(8,128)(2,1)S(1)}, u32[]{:S(2)}, u32[]{:S(2)}) %collective-permute-start.3) | collective-permute-done | bytes 393248 | tf_op jit(solution)/shard_map/ppermute | solution.py:566
  64.6 8.2 %collective-permute-done.4.refs_1_ = bf16[3,128,512]{2,1,0:T(8,128)(2,1)S(1)} collective-permute-done((bf16[3,128,512]{2,1,0:T(8,128)(2,1)S(1)}, bf16[3,128,512]{2,1,0:T(8,128)(2,1)S(1)}, u32[]{:S(2)}, u32[]{:S(2)}) %collective-permute-start.4) | collective-permute-done | bytes 393248 | tf_op jit(solution)/shard_map/ppermute | solution.py:566
  72.7 3.9 %slab_fronts.5.refs_0_ = bf16[8,128,512]{2,1,0:T(8,128)(2,1)} custom-call(s32[1]{0:T(128)} %bitcast.1.place_ref, bf16[3,128,8192]{2,1,0:T(8,128)(2,1)} %arrived_ref.17, bf16[3,128,512]{2,1,0:T(8,128)(2,1)S(1)} %collective-permute-done.3.refs_0_, bf16[3,128,512]{2,1,0:T(8,128)(2,1)S(1)} %collective-permute-done.4.refs_1_, ...), custom_call_target="tpu_custom_call" | custom-call | flops 15728640 | bytes 2621440 | tf_op jit(solution)/shard_map/slab_fronts/pallas_call | solution.py:218
  77.7 5.1 %all-to-all-start.3 = ((bf16[8,128,512]{2,1,0:T(8,128)(2,1)}), bf16[8,128,512]{2,1,0:T(8,128)(2,1)S(1)}, u32[]{:S(2)}, u32[]{:S(2)}) async-start(bf16[8,128,512]{2,1,0:T(8,128)(2,1)} %slab_fronts.5.refs_0_), calls=%async_computation.3 | async-start | bytes 2097152 | tf_op jit(solution)/shard_map/all_to_all | solution.py:571
  88.3 14.3 %collective-permute-done.14.refs_1_ = bf16[3,128,512]{2,1,0:T(8,128)(2,1)S(1)} collective-permute-done((bf16[3,128,512]{2,1,0:T(8,128)(2,1)}, bf16[3,128,512]{2,1,0:T(8,128)(2,1)S(1)}, u32[]{:S(2)}, u32[]{:S(2)}) %collective-permute-start.14) | collective-permute-done | bytes 393248 | tf_op jit(solution)/shard_map/ppermute | solution.py:566
  103.8 3.9 %slab_fronts.7 = bf16[8,128,512]{2,1,0:T(8,128)(2,1)} custom-call(s32[1]{0:T(128)} %bitcast.1.place_ref, bf16[3,128,8192]{2,1,0:T(8,128)(2,1)} %arrived_ref.17, bf16[3,128,512]{2,1,0:T(8,128)(2,1)S(1)} %collective-permute-done.13.refs_0_, bf16[3,128,512]{2,1,0:T(8,128)(2,1)S(1)} %collective-permute-done.14.refs_1_, ...), custom_call_target="tpu_custom_call" | custom-call | flops 15728640 | bytes 2621440 | tf_op jit(solution)/shard_map/slab_fronts/pallas_call | solution.py:218
  107.7 5.8 %all-to-all-start.2 = ((bf16[8,128,512]{2,1,0:T(8,128)(2,1)}), bf16[8,128,512]{2,1,0:T(8,128)(2,1)}, u32[]{:S(2)}, u32[]{:S(2)}) async-start(bf16[8,128,512]{2,1,0:T(8,128)(2,1)} %slab_fronts.7), calls=%async_computation.2 | async-start | bytes 2097152 | tf_op jit(solution)/shard_map/all_to_all | solution.py:571
  121.5 12.8 %collective-permute-done.7.refs_1_ = bf16[3,128,512]{2,1,0:T(8,128)(2,1)} collective-permute-done((bf16[3,128,512]{2,1,0:T(8,128)(2,1)}, bf16[3,128,512]{2,1,0:T(8,128)(2,1)}, u32[]{:S(2)}, u32[]{:S(2)}) %collective-permute-start.7) | collective-permute-done | bytes 393248 | tf_op jit(solution)/shard_map/ppermute | solution.py:566
  134.4 3.9 %slab_fronts.6.value_ref = bf16[8,128,512]{2,1,0:T(8,128)(2,1)} custom-call(s32[1]{0:T(128)} %bitcast.1.place_ref, bf16[3,128,8192]{2,1,0:T(8,128)(2,1)} %arrived_ref.17, bf16[3,128,512]{2,1,0:T(8,128)(2,1)S(1)} %collective-permute-done.6.refs_0_, bf16[3,128,512]{2,1,0:T(8,128)(2,1)} %collective-permute-done.7.refs_1_, ...), custom_call_target="tpu_custom_call" | custom-call | flops 15728640 | bytes 2621440 | tf_op jit(solution)/shard_map/slab_fronts/pallas_call | solution.py:218
  138.6 5.8 %all-to-all-start.1 = ((bf16[8,128,512]{2,1,0:T(8,128)(2,1)}), bf16[8,128,512]{2,1,0:T(8,128)(2,1)}, u32[]{:S(2)}, u32[]{:S(2)}) async-start(bf16[8,128,512]{2,1,0:T(8,128)(2,1)} %in_place.1), calls=%async_computation.1 | async-start | bytes 2097152 | tf_op jit(solution)/shard_map/all_to_all | solution.py:571
  146.1 6.7 %scan_shard.4 = (bf16[512,2048]{1,0:T(8,128)(2,1)}, f32[8192,128]{1,0:T(8,128)}, f32[2,16,2048]{2,1,0:T(8,128)S(1)}, bf16[16,640]{1,0:T(8,128)(2,1)S(1)}) custom-call(s32[8]{0:T(128)S(1)} %bitcast.10, s32[512]{0:T(512)S(1)} %copy-done.4, s32[16]{0:T(128)S(1)} %reduce_sum.9.refs_2_, f32[2]{0:T(128)S(1)} %compare_convert_fusion.refs_3_.refs_1_, ...), custom_call_target="tpu_custom_call" | custom-call | flops 26214400 | bytes 2621440 | tf_op jit(solution)/shard_map/scan_shard/pallas_call | solution.py:412
  152.8 6.7 %scan_shard.5 = (bf16[512,2048]{1,0:T(8,128)(2,1)}, f32[8192,128]{1,0:T(8,128)}, f32[2,16,2048]{2,1,0:T(8,128)S(1)}, bf16[16,1152]{1,0:T(8,128)(2,1)S(1)}) custom-call(s32[8]{0:T(128)S(1)} %bitcast.11, s32[512]{0:T(512)S(1)} %copy-done.4, s32[16]{0:T(128)S(1)} %reduce_sum.9.refs_2_, ...), custom_call_target="tpu_custom_call", output_to_operand_aliasing={{0}: (13, {}), {1}: (14, {}), {2}: (15, {})} | custom-call | flops 26214400 | bytes 2621440 | tf_op jit(solution)/shard_map/scan_shard/pallas_call | solution.py:412
  159.4 6.5 %scan_shard.6 = (bf16[512,2048]{1,0:T(8,128)(2,1)}, f32[8192,128]{1,0:T(8,128)}, f32[2,16,2048]{2,1,0:T(8,128)S(1)}, bf16[16,1664]{1,0:T(8,128)(2,1)S(1)}) custom-call(s32[8]{0:T(128)S(1)} %bitcast.12, s32[512]{0:T(512)S(1)} %copy-done.4, s32[16]{0:T(128)S(1)} %reduce_sum.9.refs_2_, ...), custom_call_target="tpu_custom_call", output_to_operand_aliasing={{0}: (13, {}), {1}: (14, {}), {2}: (15, {})} | custom-call | flops 26214400 | bytes 2621440 | tf_op jit(solution)/shard_map/scan_shard/pallas_call | solution.py:412
  167.7 6.5 %scan_shard.7 = (bf16[512,2048]{1,0:T(8,128)(2,1)}, f32[8192,128]{1,0:T(8,128)}, f32[2,16,2048]{2,1,0:T(8,128)S(1)}, bf16[16,2176]{1,0:T(8,128)(2,1)S(1)}) custom-call(s32[8]{0:T(128)S(1)} %bitcast.13, s32[512]{0:T(512)S(1)} %copy-done.4, s32[16]{0:T(128)S(1)} %reduce_sum.9.refs_2_, ...), custom_call_target="tpu_custom_call", output_to_operand_aliasing={{0}: (13, {}), {1}: (14, {}), {2}: (15, {})} | custom-call | flops 26214400 | bytes 2621440 | tf_op jit(solution)/shard_map/scan_shard/pallas_call | solution.py:412
  177.5 5.7 %collective-permute-start.18 = (bf16[16,2176]{1,0:T(8,128)(2,1)S(1)}, bf16[16,2176]{1,0:T(8,128)(2,1)S(1)}, u32[]{:S(2)}, u32[]{:S(2)}) collective-permute-start(bf16[16,2176]{1,0:T(8,128)(2,1)S(1)} %get-tuple-element.67), channel_id=1, source_target_pairs={{0,12},{4,16},{8,20},{12,24},{16,28},{1,13},{5,17},{9,21},{13,25},... | collective-permute-start | bytes 208904 | tf_op jit(solution)/shard_map/ppermute | solution.py:546
  187.9 5.8 %collective-permute-done.17.refs_3_ = bf16[16,2176]{1,0:T(8,128)(2,1)S(1)} collective-permute-done((bf16[16,2176]{1,0:T(8,128)(2,1)S(1)}, bf16[16,2176]{1,0:T(8,128)(2,1)S(1)}, u32[]{:S(2)}, u32[]{:S(2)}) %collective-permute-start.17) | collective-permute-done | bytes 69664 | tf_op jit(solution)/shard_map/ppermute | solution.py:546
  193.9 8.9 %carry_shard.1 = bf16[512,2048]{1,0:T(8,128)(2,1)} custom-call(s32[2]{0:T(128)S(1)} %select_reduce_fusion.refs_0_, f32[2]{0:T(128)S(1)} %compare_convert_fusion.refs_3_.refs_1_, bf16[16,2176]{1,0:T(8,128)(2,1)S(1)} %collective-permute-done.16.refs_2_, bf16[16,2176]{1,0:T(8,128)(2,1)S(1)} %collective-permute-done.17.refs_3_, ...), custom_call_target="tpu_custom_call" | custom-call | flops 41943040 | bytes 8388608 | tf_op jit(solution)/shard_map/carry_shard/pallas_call | solution.py:517
  (79 shorter events, 47.5 us)
Async XLA Ops:
  4.0 10.6 %collective-permute-start.10 = (bf16[2,24,2048]{2,1,0:T(8,128)(2,1)S(1)}, bf16[2,24,2048]{2,1,0:T(8,128)(2,1)S(1)}, u32[]{:S(2)}, u32[]{:S(2)}) collective-permute-start(bf16[2,24,2048]{2,1,0:T(8,128)(2,1)S(1)} %get-tuple-element.50), channel_id=1, source_target_pairs={{0,2},{1,3},{2,0},{3,1},{4,6},{5,7},{6,4},{7,5},{8,10},{9,11},{10,... | collective-permute-start | bytes 589832 | tf_op jit(solution)/shard_map/ppermute | solution.py:566
  16.5 29.7 %all-to-all-start = ((bf16[8,24,2048]{2,1,0:T(8,128)(2,1)}), bf16[8,24,2048]{2,1,0:T(8,128)(2,1)S(1)}, u32[]{:S(2)}, u32[]{:S(2)}) async-start(bf16[8,24,2048]{2,1,0:T(8,128)(2,1)} %by_shard.1), calls=%async_computation | async-start | bytes 1572864 | tf_op jit(solution)/shard_map/all_to_all | solution.py:571
  21.7 12.0 %collective-permute-start = (bf16[3,128,512]{2,1,0:T(8,128)(2,1)S(1)}, bf16[3,128,512]{2,1,0:T(8,128)(2,1)S(1)}, u32[]{:S(2)}, u32[]{:S(2)}) collective-permute-start(bf16[3,128,512]{2,1,0:T(8,128)(2,1)S(1)} %get-tuple-element.39.refs_4_), channel_id=1, source_target_pairs={{0,1},{1,0},{2,3},{3,2},{4,5},{5,4},{6,7},{7,6},{8,9},{9,8},{10,11... | collective-permute-start | bytes 1179656 | tf_op jit(solution)/shard_map/ppermute | solution.py:566
  22.9 17.7 %collective-permute-start.1 = (bf16[3,128,512]{2,1,0:T(8,128)(2,1)S(1)}, bf16[3,128,512]{2,1,0:T(8,128)(2,1)S(1)}, u32[]{:S(2)}, u32[]{:S(2)}) collective-permute-start(bf16[3,128,512]{2,1,0:T(8,128)(2,1)S(1)} %get-tuple-element.40.refs_5_), channel_id=1, source_target_pairs={{0,2},{1,3},{2,0},{3,1},{4,6},{5,7},{6,4},{7,5},{8,10},{9,11},{10,... | collective-permute-start | bytes 1179656 | tf_op jit(solution)/shard_map/ppermute | solution.py:566
  23.8 18.5 %collective-permute-start.2 = (bf16[3,128,512]{2,1,0:T(8,128)(2,1)S(1)}, bf16[3,128,512]{2,1,0:T(8,128)(2,1)S(1)}, u32[]{:S(2)}, u32[]{:S(2)}) collective-permute-start(bf16[3,128,512]{2,1,0:T(8,128)(2,1)S(1)} %get-tuple-element.41.refs_6_), channel_id=1, source_target_pairs={{0,3},{1,2},{2,1},{3,0},{4,7},{5,6},{6,5},{7,4},{8,11},{9,10},{10,... | collective-permute-start | bytes 1179656 | tf_op jit(solution)/shard_map/ppermute | solution.py:566
  46.2 30.5 %all-to-all-start.4 = ((bf16[8,128,512]{2,1,0:T(8,128)(2,1)}), bf16[8,128,512]{2,1,0:T(8,128)(2,1)S(1)}, u32[]{:S(2)}, u32[]{:S(2)}) async-start(bf16[8,128,512]{2,1,0:T(8,128)(2,1)} %slab_fronts.4.refs_0_), calls=%async_computation.4 | async-start | bytes 2097152 | tf_op jit(solution)/shard_map/all_to_all | solution.py:571
  52.6 12.0 %collective-permute-start.3 = (bf16[3,128,512]{2,1,0:T(8,128)(2,1)S(1)}, bf16[3,128,512]{2,1,0:T(8,128)(2,1)S(1)}, u32[]{:S(2)}, u32[]{:S(2)}) collective-permute-start(bf16[3,128,512]{2,1,0:T(8,128)(2,1)S(1)} %get-tuple-element.42), channel_id=1, source_target_pairs={{0,1},{1,0},{2,3},{3,2},{4,5},{5,4},{6,7},{7,6},{8,9},{9,8},{10,11... | collective-permute-start | bytes 1179656 | tf_op jit(solution)/shard_map/ppermute | solution.py:566
  53.4 19.3 %collective-permute-start.4 = (bf16[3,128,512]{2,1,0:T(8,128)(2,1)S(1)}, bf16[3,128,512]{2,1,0:T(8,128)(2,1)S(1)}, u32[]{:S(2)}, u32[]{:S(2)}) collective-permute-start(bf16[3,128,512]{2,1,0:T(8,128)(2,1)S(1)} %get-tuple-element.43), channel_id=1, source_target_pairs={{0,2},{1,3},{2,0},{3,1},{4,6},{5,7},{6,4},{7,5},{8,10},{9,11},{10,... | collective-permute-start | bytes 1179656 | tf_op jit(solution)/shard_map/ppermute | solution.py:566
  54.9 17.8 %collective-permute-start.5 = (bf16[3,128,512]{2,1,0:T(8,128)(2,1)S(1)}, bf16[3,128,512]{2,1,0:T(8,128)(2,1)S(1)}, u32[]{:S(2)}, u32[]{:S(2)}) collective-permute-start(bf16[3,128,512]{2,1,0:T(8,128)(2,1)S(1)} %get-tuple-element.44), channel_id=1, source_target_pairs={{0,3},{1,2},{2,1},{3,0},{4,7},{5,6},{6,5},{7,4},{8,11},{9,10},{10,... | collective-permute-start | bytes 1179656 | tf_op jit(solution)/shard_map/ppermute | solution.py:566
  77.7 30.1 %all-to-all-start.3 = ((bf16[8,128,512]{2,1,0:T(8,128)(2,1)}), bf16[8,128,512]{2,1,0:T(8,128)(2,1)S(1)}, u32[]{:S(2)}, u32[]{:S(2)}) async-start(bf16[8,128,512]{2,1,0:T(8,128)(2,1)} %slab_fronts.5.refs_0_), calls=%async_computation.3 | async-start | bytes 2097152 | tf_op jit(solution)/shard_map/all_to_all | solution.py:571
  82.8 19.8 %collective-permute-start.14 = (bf16[3,128,512]{2,1,0:T(8,128)(2,1)}, bf16[3,128,512]{2,1,0:T(8,128)(2,1)S(1)}, u32[]{:S(2)}, u32[]{:S(2)}) collective-permute-start(bf16[3,128,512]{2,1,0:T(8,128)(2,1)} %copy-done.8), channel_id=1, source_target_pairs={{0,2},{1,3},{2,0},{3,1},{4,6},{5,7},{6,4},{7,5},{8,10},{9,11},{10,... | collective-permute-start | bytes 1179656 | tf_op jit(solution)/shard_map/ppermute | solution.py:566
  84.3 18.3 %collective-permute-start.15 = (bf16[3,128,512]{2,1,0:T(8,128)(2,1)}, bf16[3,128,512]{2,1,0:T(8,128)(2,1)S(1)}, u32[]{:S(2)}, u32[]{:S(2)}) collective-permute-start(bf16[3,128,512]{2,1,0:T(8,128)(2,1)} %copy-done.7), channel_id=1, source_target_pairs={{0,3},{1,2},{2,1},{3,0},{4,7},{5,6},{6,5},{7,4},{8,11},{9,10},{10,... | collective-permute-start | bytes 1179656 | tf_op jit(solution)/shard_map/ppermute | solution.py:566
  85.5 18.3 %collective-permute-start.13 = (bf16[3,128,512]{2,1,0:T(8,128)(2,1)S(1)}, bf16[3,128,512]{2,1,0:T(8,128)(2,1)S(1)}, u32[]{:S(2)}, u32[]{:S(2)}) collective-permute-start(bf16[3,128,512]{2,1,0:T(8,128)(2,1)S(1)} %get-tuple-element.45.refs_3_), channel_id=1, source_target_pairs={{0,1},{1,0},{2,3},{3,2},{4,5},{5,4},{6,7},{7,6},{8,9},{9,8},{10,11... | collective-permute-start | bytes 1179656 | tf_op jit(solution)/shard_map/ppermute | solution.py:566
  107.7 30.9 %all-to-all-start.2 = ((bf16[8,128,512]{2,1,0:T(8,128)(2,1)}), bf16[8,128,512]{2,1,0:T(8,128)(2,1)}, u32[]{:S(2)}, u32[]{:S(2)}) async-start(bf16[8,128,512]{2,1,0:T(8,128)(2,1)} %slab_fronts.7), calls=%async_computation.2 | async-start | bytes 2097152 | tf_op jit(solution)/shard_map/all_to_all | solution.py:571
  113.5 20.9 %collective-permute-start.6 = (bf16[3,128,512]{2,1,0:T(8,128)(2,1)S(1)}, bf16[3,128,512]{2,1,0:T(8,128)(2,1)S(1)}, u32[]{:S(2)}, u32[]{:S(2)}) collective-permute-start(bf16[3,128,512]{2,1,0:T(8,128)(2,1)S(1)} %get-tuple-element.46.refs_3_), channel_id=1, source_target_pairs={{0,1},{1,0},{2,3},{3,2},{4,5},{5,4},{6,7},{7,6},{8,9},{9,8},{10,11... | collective-permute-start | bytes 1179656 | tf_op jit(solution)/shard_map/ppermute | solution.py:566
  114.7 19.6 %collective-permute-start.7 = (bf16[3,128,512]{2,1,0:T(8,128)(2,1)}, bf16[3,128,512]{2,1,0:T(8,128)(2,1)}, u32[]{:S(2)}, u32[]{:S(2)}) collective-permute-start(bf16[3,128,512]{2,1,0:T(8,128)(2,1)} %copy-done.6), channel_id=1, source_target_pairs={{0,2},{1,3},{2,0},{3,1},{4,6},{5,7},{6,4},{7,5},{8,10},{9,11},{10,... | collective-permute-start | bytes 1179656 | tf_op jit(solution)/shard_map/ppermute | solution.py:566
  115.6 18.8 %collective-permute-start.8 = (bf16[3,128,512]{2,1,0:T(8,128)(2,1)S(1)}, bf16[3,128,512]{2,1,0:T(8,128)(2,1)}, u32[]{:S(2)}, u32[]{:S(2)}) collective-permute-start(bf16[3,128,512]{2,1,0:T(8,128)(2,1)S(1)} %get-tuple-element.48), channel_id=1, source_target_pairs={{0,3},{1,2},{2,1},{3,0},{4,7},{5,6},{6,5},{7,4},{8,11},{9,10},{10,... | collective-permute-start | bytes 1179656 | tf_op jit(solution)/shard_map/ppermute | solution.py:566
  119.6 19.0 %collective-permute-start.12 = (bf16[24,2048]{1,0:T(8,128)(2,1)S(1)}, bf16[24,2048]{1,0:T(8,128)(2,1)S(1)}, u32[]{:S(2)}, u32[]{:S(2)}) collective-permute-start(bf16[24,2048]{1,0:T(8,128)(2,1)S(1)} %dynamic-slice_bitcast_fusion), channel_id=1, source_target_pairs={{0,4},{4,8},{8,12},{12,16},{16,20},{20,24},{24,28},{1,5},{5,9},{9,... | collective-permute-start | bytes 294920 | tf_op jit(solution)/shard_map/ppermute | solution.py:546
  138.6 29.1 %all-to-all-start.1 = ((bf16[8,128,512]{2,1,0:T(8,128)(2,1)}), bf16[8,128,512]{2,1,0:T(8,128)(2,1)}, u32[]{:S(2)}, u32[]{:S(2)}) async-start(bf16[8,128,512]{2,1,0:T(8,128)(2,1)} %in_place.1), calls=%async_computation.1 | async-start | bytes 2097152 | tf_op jit(solution)/shard_map/all_to_all | solution.py:571
  174.8 10.3 %collective-permute-start.21 = (bf16[16,2176]{1,0:T(8,128)(2,1)S(1)}, bf16[16,2176]{1,0:T(8,128)(2,1)S(1)}, u32[]{:S(2)}, u32[]{:S(2)}) collective-permute-start(bf16[16,2176]{1,0:T(8,128)(2,1)S(1)} %get-tuple-element.67), channel_id=1, source_target_pairs={{0,24},{4,28},{1,25},{5,29},{2,26},{6,30},{3,27},{7,31}} | collective-permute-start | bytes 208904 | tf_op jit(solution)/shard_map/ppermute | solution.py:546
  175.5 12.0 %collective-permute-start.20 = (bf16[16,2176]{1,0:T(8,128)(2,1)S(1)}, bf16[16,2176]{1,0:T(8,128)(2,1)S(1)}, u32[]{:S(2)}, u32[]{:S(2)}) collective-permute-start(bf16[16,2176]{1,0:T(8,128)(2,1)S(1)} %get-tuple-element.67), channel_id=1, source_target_pairs={{0,20},{4,24},{8,28},{1,21},{5,25},{9,29},{2,22},{6,26},{10,30},{3... | collective-permute-start | bytes 208904 | tf_op jit(solution)/shard_map/ppermute | solution.py:546
  176.2 11.4 %collective-permute-start.19 = (bf16[16,2176]{1,0:T(8,128)(2,1)S(1)}, bf16[16,2176]{1,0:T(8,128)(2,1)S(1)}, u32[]{:S(2)}, u32[]{:S(2)}) collective-permute-start(bf16[16,2176]{1,0:T(8,128)(2,1)S(1)} %get-tuple-element.67), channel_id=1, source_target_pairs={{0,16},{4,20},{8,24},{12,28},{1,17},{5,21},{9,25},{13,29},{2,18},{... | collective-permute-start | bytes 208904 | tf_op jit(solution)/shard_map/ppermute | solution.py:546
  177.5 10.5 %collective-permute-start.18 = (bf16[16,2176]{1,0:T(8,128)(2,1)S(1)}, bf16[16,2176]{1,0:T(8,128)(2,1)S(1)}, u32[]{:S(2)}, u32[]{:S(2)}) collective-permute-start(bf16[16,2176]{1,0:T(8,128)(2,1)S(1)} %get-tuple-element.67), channel_id=1, source_target_pairs={{0,12},{4,16},{8,20},{12,24},{16,28},{1,13},{5,17},{9,21},{13,25},... | collective-permute-start | bytes 208904 | tf_op jit(solution)/shard_map/ppermute | solution.py:546
  183.2 10.6 %collective-permute-start.17 = (bf16[16,2176]{1,0:T(8,128)(2,1)S(1)}, bf16[16,2176]{1,0:T(8,128)(2,1)S(1)}, u32[]{:S(2)}, u32[]{:S(2)}) collective-permute-start(bf16[16,2176]{1,0:T(8,128)(2,1)S(1)} %get-tuple-element.67), channel_id=1, source_target_pairs={{0,8},{4,12},{8,16},{12,20},{16,24},{20,28},{1,9},{5,13},{9,17},{1... | collective-permute-start | bytes 208904 | tf_op jit(solution)/shard_map/ppermute | solution.py:546
  (15 other events, 114.1 us)

commit v5 on v4

--- a/solution.py
+++ b/solution.py
@@ -9,7 +9,7 @@
 
 LANES = 128
 SUBLANES = 8
-GROUP = 16
+GROUP = 32
 CHUNKS = 4
 VMEM_BYTES = 50 * 1024 * 1024
 

time: 204 us -> 203 us (level)
  no operation moved by 1% of the time
where the time goes in v5:
time: 203 us
  waiting for transfers between devices  75.2 us (37%)
  starting transfers between devices  59.9 us (30%)
  Pallas kernels  59.6 us (29%)
  local copies, waits for them, and re-layouts  4.59 us (2%)
  between operations  2.23 us (1%)
    ppermute x15, waiting for transfers between devices, across_plane(): lax.ppermute(part, 'chan', [(c, c ^ d) for c in range(chans)])  66.5 us
    all_to_all x5, starting transfers between devices, along_column(): return lax.all_to_all(value, 'seq', split_axis=0, concat_axis=0, tiled=True)  27 us
    pallas_call x4, Pallas kernels, scan_shard(): pl.pallas_call(functools.partial(scan_body, chunk, segments, len(shared))...  25.8 us
    ppermute x15, starting transfers between devices, across_plane(): lax.ppermute(part, 'chan', [(c, c ^ d) for c in range(chans)])  17.6 us
    pallas_call x4, Pallas kernels, slab_fronts(): pl.pallas_call(functools.partial(front_body, chunk, count), grid=(1,), in...  15.6 us
    ppermute x8, starting transfers between devices, passed_along(): return lax.ppermute(value, 'seq', [(i, i + by) for i in range(shards - by)])  15.3 us
    pallas_call x1, Pallas kernels, carry_shard(): pl.pallas_call(functools.partial(carry_body, segments, len(ends)), grid=(...  8.73 us
    ppermute x8, waiting for transfers between devices, passed_along(): return lax.ppermute(value, 'seq', [(i, i + by) for i in range(shards - by)])  6.58 us
  transfers between devices with their start and end apart: 28, of which 15 were waited for; matrix products, arithmetic and copies ran while one was open for 1% of the time, Pallas kernels for 20%

profile of v5, /device:TPU:16, one launch (start us, length us, event | category | flops | bytes accessed | tf_op | source)
XLA Modules:
  0.0 202.5 jit_solution(16258358319379704408)
XLA Ops:
  7.3 3.0 %collective-permute-done.9.refs_1_ = bf16[2,24,2048]{2,1,0:T(8,128)(2,1)S(1)} collective-permute-done((bf16[2,24,2048]{2,1,0:T(8,128)(2,1)S(1)}, bf16[2,24,2048]{2,1,0:T(8,128)(2,1)S(1)}, u32[]{:S(2)}, u32[]{:S(2)}) %collective-permute-start.9) | collective-permute-done | bytes 196640 | tf_op jit(solution)/shard_map/ppermute | solution.py:566
  10.3 4.3 %collective-permute-done.10.refs_2_ = bf16[2,24,2048]{2,1,0:T(8,128)(2,1)S(1)} collective-permute-done((bf16[2,24,2048]{2,1,0:T(8,128)(2,1)S(1)}, bf16[2,24,2048]{2,1,0:T(8,128)(2,1)S(1)}, u32[]{:S(2)}, u32[]{:S(2)}) %collective-permute-start.10) | collective-permute-done | bytes 196640 | tf_op jit(solution)/shard_map/ppermute | solution.py:566
  16.5 5.2 %all-to-all-start = ((bf16[8,24,2048]{2,1,0:T(8,128)(2,1)}), bf16[8,24,2048]{2,1,0:T(8,128)(2,1)S(1)}, u32[]{:S(2)}, u32[]{:S(2)}) async-start(bf16[8,24,2048]{2,1,0:T(8,128)(2,1)} %by_shard.1), calls=%async_computation | async-start | bytes 1572864 | tf_op jit(solution)/shard_map/all_to_all | solution.py:571
  25.2 8.5 %collective-permute-done.refs_0_ = bf16[3,128,512]{2,1,0:T(8,128)(2,1)S(1)} collective-permute-done((bf16[3,128,512]{2,1,0:T(8,128)(2,1)S(1)}, bf16[3,128,512]{2,1,0:T(8,128)(2,1)S(1)}, u32[]{:S(2)}, u32[]{:S(2)}) %collective-permute-start) | collective-permute-done | bytes 393248 | tf_op jit(solution)/shard_map/ppermute | solution.py:566
  33.7 7.0 %collective-permute-done.1.refs_1_ = bf16[3,128,512]{2,1,0:T(8,128)(2,1)S(1)} collective-permute-done((bf16[3,128,512]{2,1,0:T(8,128)(2,1)S(1)}, bf16[3,128,512]{2,1,0:T(8,128)(2,1)S(1)}, u32[]{:S(2)}, u32[]{:S(2)}) %collective-permute-start.1) | collective-permute-done | bytes 393248 | tf_op jit(solution)/shard_map/ppermute | solution.py:566
  42.3 3.9 %slab_fronts.4.refs_0_ = bf16[8,128,512]{2,1,0:T(8,128)(2,1)} custom-call(s32[1]{0:T(128)} %bitcast.1.place_ref, bf16[3,128,8192]{2,1,0:T(8,128)(2,1)} %arrived_ref.17, bf16[3,128,512]{2,1,0:T(8,128)(2,1)S(1)} %collective-permute-done.refs_0_, bf16[3,128,512]{2,1,0:T(8,128)(2,1)S(1)} %collective-permute-done.1.refs_1_, ...), custom_call_target="tpu_custom_call" | custom-call | flops 15728640 | bytes 2621440 | tf_op jit(solution)/shard_map/slab_fronts/pallas_call | solution.py:218
  46.2 5.1 %all-to-all-start.4 = ((bf16[8,128,512]{2,1,0:T(8,128)(2,1)}), bf16[8,128,512]{2,1,0:T(8,128)(2,1)S(1)}, u32[]{:S(2)}, u32[]{:S(2)}) async-start(bf16[8,128,512]{2,1,0:T(8,128)(2,1)} %slab_fronts.4.refs_0_), calls=%async_computation.4 | async-start | bytes 2097152 | tf_op jit(solution)/shard_map/all_to_all | solution.py:571
  58.9 5.7 %collective-permute-done.3.refs_0_ = bf16[3,128,512]{2,1,0:T(8,128)(2,1)S(1)} collective-permute-done((bf16[3,128,512]{2,1,0:T(8,128)(2,1)S(1)}, bf16[3,128,512]{2,1,0:T(8,128)(2,1)S(1)}, u32[]{:S(2)}, u32[]{:S(2)}) %collective-permute-start.3) | collective-permute-done | bytes 393248 | tf_op jit(solution)/shard_map/ppermute | solution.py:566
  64.6 8.2 %collective-permute-done.4.refs_1_ = bf16[3,128,512]{2,1,0:T(8,128)(2,1)S(1)} collective-permute-done((bf16[3,128,512]{2,1,0:T(8,128)(2,1)S(1)}, bf16[3,128,512]{2,1,0:T(8,128)(2,1)S(1)}, u32[]{:S(2)}, u32[]{:S(2)}) %collective-permute-start.4) | collective-permute-done | bytes 393248 | tf_op jit(solution)/shard_map/ppermute | solution.py:566
  72.7 3.9 %slab_fronts.5.refs_0_ = bf16[8,128,512]{2,1,0:T(8,128)(2,1)} custom-call(s32[1]{0:T(128)} %bitcast.1.place_ref, bf16[3,128,8192]{2,1,0:T(8,128)(2,1)} %arrived_ref.17, bf16[3,128,512]{2,1,0:T(8,128)(2,1)S(1)} %collective-permute-done.3.refs_0_, bf16[3,128,512]{2,1,0:T(8,128)(2,1)S(1)} %collective-permute-done.4.refs_1_, ...), custom_call_target="tpu_custom_call" | custom-call | flops 15728640 | bytes 2621440 | tf_op jit(solution)/shard_map/slab_fronts/pallas_call | solution.py:218
  77.7 5.1 %all-to-all-start.3 = ((bf16[8,128,512]{2,1,0:T(8,128)(2,1)}), bf16[8,128,512]{2,1,0:T(8,128)(2,1)S(1)}, u32[]{:S(2)}, u32[]{:S(2)}) async-start(bf16[8,128,512]{2,1,0:T(8,128)(2,1)} %slab_fronts.5.refs_0_), calls=%async_computation.3 | async-start | bytes 2097152 | tf_op jit(solution)/shard_map/all_to_all | solution.py:571
  88.3 14.3 %collective-permute-done.14.refs_1_ = bf16[3,128,512]{2,1,0:T(8,128)(2,1)S(1)} collective-permute-done((bf16[3,128,512]{2,1,0:T(8,128)(2,1)}, bf16[3,128,512]{2,1,0:T(8,128)(2,1)S(1)}, u32[]{:S(2)}, u32[]{:S(2)}) %collective-permute-start.14) | collective-permute-done | bytes 393248 | tf_op jit(solution)/shard_map/ppermute | solution.py:566
  103.8 3.9 %slab_fronts.7 = bf16[8,128,512]{2,1,0:T(8,128)(2,1)} custom-call(s32[1]{0:T(128)} %bitcast.1.place_ref, bf16[3,128,8192]{2,1,0:T(8,128)(2,1)} %arrived_ref.17, bf16[3,128,512]{2,1,0:T(8,128)(2,1)S(1)} %collective-permute-done.13.refs_0_, bf16[3,128,512]{2,1,0:T(8,128)(2,1)S(1)} %collective-permute-done.14.refs_1_, ...), custom_call_target="tpu_custom_call" | custom-call | flops 15728640 | bytes 2621440 | tf_op jit(solution)/shard_map/slab_fronts/pallas_call | solution.py:218
  107.7 5.8 %all-to-all-start.2 = ((bf16[8,128,512]{2,1,0:T(8,128)(2,1)}), bf16[8,128,512]{2,1,0:T(8,128)(2,1)}, u32[]{:S(2)}, u32[]{:S(2)}) async-start(bf16[8,128,512]{2,1,0:T(8,128)(2,1)} %slab_fronts.7), calls=%async_computation.2 | async-start | bytes 2097152 | tf_op jit(solution)/shard_map/all_to_all | solution.py:571
  121.5 12.8 %collective-permute-done.7.refs_1_ = bf16[3,128,512]{2,1,0:T(8,128)(2,1)} collective-permute-done((bf16[3,128,512]{2,1,0:T(8,128)(2,1)}, bf16[3,128,512]{2,1,0:T(8,128)(2,1)}, u32[]{:S(2)}, u32[]{:S(2)}) %collective-permute-start.7) | collective-permute-done | bytes 393248 | tf_op jit(solution)/shard_map/ppermute | solution.py:566
  134.4 3.9 %slab_fronts.6.value_ref = bf16[8,128,512]{2,1,0:T(8,128)(2,1)} custom-call(s32[1]{0:T(128)} %bitcast.1.place_ref, bf16[3,128,8192]{2,1,0:T(8,128)(2,1)} %arrived_ref.17, bf16[3,128,512]{2,1,0:T(8,128)(2,1)S(1)} %collective-permute-done.6.refs_0_, bf16[3,128,512]{2,1,0:T(8,128)(2,1)} %collective-permute-done.7.refs_1_, ...), custom_call_target="tpu_custom_call" | custom-call | flops 15728640 | bytes 2621440 | tf_op jit(solution)/shard_map/slab_fronts/pallas_call | solution.py:218
  138.6 5.8 %all-to-all-start.1 = ((bf16[8,128,512]{2,1,0:T(8,128)(2,1)}), bf16[8,128,512]{2,1,0:T(8,128)(2,1)}, u32[]{:S(2)}, u32[]{:S(2)}) async-start(bf16[8,128,512]{2,1,0:T(8,128)(2,1)} %in_place.1), calls=%async_computation.1 | async-start | bytes 2097152 | tf_op jit(solution)/shard_map/all_to_all | solution.py:571
  146.1 6.5 %scan_shard.4 = (bf16[512,2048]{1,0:T(8,128)(2,1)}, f32[8192,128]{1,0:T(8,128)}, f32[2,16,2048]{2,1,0:T(8,128)S(1)}, bf16[16,640]{1,0:T(8,128)(2,1)S(1)}) custom-call(s32[8]{0:T(128)S(1)} %bitcast.10, s32[512]{0:T(512)S(1)} %copy-done.4, s32[8]{0:T(128)S(1)} %reduce_sum.9.refs_2_, f32[2]{0:T(128)S(1)} %compare_convert_fusion.refs_3_.refs_1_, ...), custom_call_target="tpu_custom_call" | custom-call | flops 26214400 | bytes 2621440 | tf_op jit(solution)/shard_map/scan_shard/pallas_call | solution.py:412
  152.7 6.5 %scan_shard.5 = (bf16[512,2048]{1,0:T(8,128)(2,1)}, f32[8192,128]{1,0:T(8,128)}, f32[2,16,2048]{2,1,0:T(8,128)S(1)}, bf16[16,1152]{1,0:T(8,128)(2,1)S(1)}) custom-call(s32[8]{0:T(128)S(1)} %bitcast.11, s32[512]{0:T(512)S(1)} %copy-done.4, s32[8]{0:T(128)S(1)} %reduce_sum.9.refs_2_, ...), custom_call_target="tpu_custom_call", output_to_operand_aliasing={{0}: (13, {}), {1}: (14, {}), {2}: (15, {})} | custom-call | flops 26214400 | bytes 2621440 | tf_op jit(solution)/shard_map/scan_shard/pallas_call | solution.py:412
  159.2 6.4 %scan_shard.6 = (bf16[512,2048]{1,0:T(8,128)(2,1)}, f32[8192,128]{1,0:T(8,128)}, f32[2,16,2048]{2,1,0:T(8,128)S(1)}, bf16[16,1664]{1,0:T(8,128)(2,1)S(1)}) custom-call(s32[8]{0:T(128)S(1)} %bitcast.12, s32[512]{0:T(512)S(1)} %copy-done.4, s32[8]{0:T(128)S(1)} %reduce_sum.9.refs_2_, ...), custom_call_target="tpu_custom_call", output_to_operand_aliasing={{0}: (13, {}), {1}: (14, {}), {2}: (15, {})} | custom-call | flops 26214400 | bytes 2621440 | tf_op jit(solution)/shard_map/scan_shard/pallas_call | solution.py:412
  167.7 6.3 %scan_shard.7 = (bf16[512,2048]{1,0:T(8,128)(2,1)}, f32[8192,128]{1,0:T(8,128)}, f32[2,16,2048]{2,1,0:T(8,128)S(1)}, bf16[16,2176]{1,0:T(8,128)(2,1)S(1)}) custom-call(s32[8]{0:T(128)S(1)} %bitcast.13, s32[512]{0:T(512)S(1)} %copy-done.4, s32[8]{0:T(128)S(1)} %reduce_sum.9.refs_2_, ...), custom_call_target="tpu_custom_call", output_to_operand_aliasing={{0}: (13, {}), {1}: (14, {}), {2}: (15, {})} | custom-call | flops 26214400 | bytes 2621440 | tf_op jit(solution)/shard_map/scan_shard/pallas_call | solution.py:412
  177.3 5.8 %collective-permute-start.18 = (bf16[16,2176]{1,0:T(8,128)(2,1)S(1)}, bf16[16,2176]{1,0:T(8,128)(2,1)S(1)}, u32[]{:S(2)}, u32[]{:S(2)}) collective-permute-start(bf16[16,2176]{1,0:T(8,128)(2,1)S(1)} %get-tuple-element.67), channel_id=1, source_target_pairs={{0,12},{4,16},{8,20},{12,24},{16,28},{1,13},{5,17},{9,21},{13,25},... | collective-permute-start | bytes 208904 | tf_op jit(solution)/shard_map/ppermute | solution.py:546
  187.9 5.8 %collective-permute-done.17.refs_3_ = bf16[16,2176]{1,0:T(8,128)(2,1)S(1)} collective-permute-done((bf16[16,2176]{1,0:T(8,128)(2,1)S(1)}, bf16[16,2176]{1,0:T(8,128)(2,1)S(1)}, u32[]{:S(2)}, u32[]{:S(2)}) %collective-permute-start.17) | collective-permute-done | bytes 69664 | tf_op jit(solution)/shard_map/ppermute | solution.py:546
  193.8 8.7 %carry_shard.1 = bf16[512,2048]{1,0:T(8,128)(2,1)} custom-call(s32[2]{0:T(128)S(1)} %select_reduce_fusion.refs_0_, f32[2]{0:T(128)S(1)} %compare_convert_fusion.refs_3_.refs_1_, bf16[16,2176]{1,0:T(8,128)(2,1)S(1)} %collective-permute-done.16.refs_2_, bf16[16,2176]{1,0:T(8,128)(2,1)S(1)} %collective-permute-done.17.refs_3_, ...), custom_call_target="tpu_custom_call" | custom-call | flops 41943040 | bytes 8388608 | tf_op jit(solution)/shard_map/carry_shard/pallas_call | solution.py:517
  (79 shorter events, 47.9 us)
Async XLA Ops:
  4.0 10.6 %collective-permute-start.10 = (bf16[2,24,2048]{2,1,0:T(8,128)(2,1)S(1)}, bf16[2,24,2048]{2,1,0:T(8,128)(2,1)S(1)}, u32[]{:S(2)}, u32[]{:S(2)}) collective-permute-start(bf16[2,24,2048]{2,1,0:T(8,128)(2,1)S(1)} %get-tuple-element.50), channel_id=1, source_target_pairs={{0,2},{1,3},{2,0},{3,1},{4,6},{5,7},{6,4},{7,5},{8,10},{9,11},{10,... | collective-permute-start | bytes 589832 | tf_op jit(solution)/shard_map/ppermute | solution.py:566
  16.5 29.7 %all-to-all-start = ((bf16[8,24,2048]{2,1,0:T(8,128)(2,1)}), bf16[8,24,2048]{2,1,0:T(8,128)(2,1)S(1)}, u32[]{:S(2)}, u32[]{:S(2)}) async-start(bf16[8,24,2048]{2,1,0:T(8,128)(2,1)} %by_shard.1), calls=%async_computation | async-start | bytes 1572864 | tf_op jit(solution)/shard_map/all_to_all | solution.py:571
  21.7 12.0 %collective-permute-start = (bf16[3,128,512]{2,1,0:T(8,128)(2,1)S(1)}, bf16[3,128,512]{2,1,0:T(8,128)(2,1)S(1)}, u32[]{:S(2)}, u32[]{:S(2)}) collective-permute-start(bf16[3,128,512]{2,1,0:T(8,128)(2,1)S(1)} %get-tuple-element.39.refs_4_), channel_id=1, source_target_pairs={{0,1},{1,0},{2,3},{3,2},{4,5},{5,4},{6,7},{7,6},{8,9},{9,8},{10,11... | collective-permute-start | bytes 1179656 | tf_op jit(solution)/shard_map/ppermute | solution.py:566
  22.9 17.7 %collective-permute-start.1 = (bf16[3,128,512]{2,1,0:T(8,128)(2,1)S(1)}, bf16[3,128,512]{2,1,0:T(8,128)(2,1)S(1)}, u32[]{:S(2)}, u32[]{:S(2)}) collective-permute-start(bf16[3,128,512]{2,1,0:T(8,128)(2,1)S(1)} %get-tuple-element.40.refs_5_), channel_id=1, source_target_pairs={{0,2},{1,3},{2,0},{3,1},{4,6},{5,7},{6,4},{7,5},{8,10},{9,11},{10,... | collective-permute-start | bytes 1179656 | tf_op jit(solution)/shard_map/ppermute | solution.py:566
  23.8 18.5 %collective-permute-start.2 = (bf16[3,128,512]{2,1,0:T(8,128)(2,1)S(1)}, bf16[3,128,512]{2,1,0:T(8,128)(2,1)S(1)}, u32[]{:S(2)}, u32[]{:S(2)}) collective-permute-start(bf16[3,128,512]{2,1,0:T(8,128)(2,1)S(1)} %get-tuple-element.41.refs_6_), channel_id=1, source_target_pairs={{0,3},{1,2},{2,1},{3,0},{4,7},{5,6},{6,5},{7,4},{8,11},{9,10},{10,... | collective-permute-start | bytes 1179656 | tf_op jit(solution)/shard_map/ppermute | solution.py:566
  46.2 30.5 %all-to-all-start.4 = ((bf16[8,128,512]{2,1,0:T(8,128)(2,1)}), bf16[8,128,512]{2,1,0:T(8,128)(2,1)S(1)}, u32[]{:S(2)}, u32[]{:S(2)}) async-start(bf16[8,128,512]{2,1,0:T(8,128)(2,1)} %slab_fronts.4.refs_0_), calls=%async_computation.4 | async-start | bytes 2097152 | tf_op jit(solution)/shard_map/all_to_all | solution.py:571
  52.6 12.0 %collective-permute-start.3 = (bf16[3,128,512]{2,1,0:T(8,128)(2,1)S(1)}, bf16[3,128,512]{2,1,0:T(8,128)(2,1)S(1)}, u32[]{:S(2)}, u32[]{:S(2)}) collective-permute-start(bf16[3,128,512]{2,1,0:T(8,128)(2,1)S(1)} %get-tuple-element.42), channel_id=1, source_target_pairs={{0,1},{1,0},{2,3},{3,2},{4,5},{5,4},{6,7},{7,6},{8,9},{9,8},{10,11... | collective-permute-start | bytes 1179656 | tf_op jit(solution)/shard_map/ppermute | solution.py:566
  53.4 19.3 %collective-permute-start.4 = (bf16[3,128,512]{2,1,0:T(8,128)(2,1)S(1)}, bf16[3,128,512]{2,1,0:T(8,128)(2,1)S(1)}, u32[]{:S(2)}, u32[]{:S(2)}) collective-permute-start(bf16[3,128,512]{2,1,0:T(8,128)(2,1)S(1)} %get-tuple-element.43), channel_id=1, source_target_pairs={{0,2},{1,3},{2,0},{3,1},{4,6},{5,7},{6,4},{7,5},{8,10},{9,11},{10,... | collective-permute-start | bytes 1179656 | tf_op jit(solution)/shard_map/ppermute | solution.py:566
  54.9 17.8 %collective-permute-start.5 = (bf16[3,128,512]{2,1,0:T(8,128)(2,1)S(1)}, bf16[3,128,512]{2,1,0:T(8,128)(2,1)S(1)}, u32[]{:S(2)}, u32[]{:S(2)}) collective-permute-start(bf16[3,128,512]{2,1,0:T(8,128)(2,1)S(1)} %get-tuple-element.44), channel_id=1, source_target_pairs={{0,3},{1,2},{2,1},{3,0},{4,7},{5,6},{6,5},{7,4},{8,11},{9,10},{10,... | collective-permute-start | bytes 1179656 | tf_op jit(solution)/shard_map/ppermute | solution.py:566
  77.7 30.1 %all-to-all-start.3 = ((bf16[8,128,512]{2,1,0:T(8,128)(2,1)}), bf16[8,128,512]{2,1,0:T(8,128)(2,1)S(1)}, u32[]{:S(2)}, u32[]{:S(2)}) async-start(bf16[8,128,512]{2,1,0:T(8,128)(2,1)} %slab_fronts.5.refs_0_), calls=%async_computation.3 | async-start | bytes 2097152 | tf_op jit(solution)/shard_map/all_to_all | solution.py:571
  82.8 19.8 %collective-permute-start.14 = (bf16[3,128,512]{2,1,0:T(8,128)(2,1)}, bf16[3,128,512]{2,1,0:T(8,128)(2,1)S(1)}, u32[]{:S(2)}, u32[]{:S(2)}) collective-permute-start(bf16[3,128,512]{2,1,0:T(8,128)(2,1)} %copy-done.8), channel_id=1, source_target_pairs={{0,2},{1,3},{2,0},{3,1},{4,6},{5,7},{6,4},{7,5},{8,10},{9,11},{10,... | collective-permute-start | bytes 1179656 | tf_op jit(solution)/shard_map/ppermute | solution.py:566
  84.3 18.3 %collective-permute-start.15 = (bf16[3,128,512]{2,1,0:T(8,128)(2,1)}, bf16[3,128,512]{2,1,0:T(8,128)(2,1)S(1)}, u32[]{:S(2)}, u32[]{:S(2)}) collective-permute-start(bf16[3,128,512]{2,1,0:T(8,128)(2,1)} %copy-done.7), channel_id=1, source_target_pairs={{0,3},{1,2},{2,1},{3,0},{4,7},{5,6},{6,5},{7,4},{8,11},{9,10},{10,... | collective-permute-start | bytes 1179656 | tf_op jit(solution)/shard_map/ppermute | solution.py:566
  85.5 18.3 %collective-permute-start.13 = (bf16[3,128,512]{2,1,0:T(8,128)(2,1)S(1)}, bf16[3,128,512]{2,1,0:T(8,128)(2,1)S(1)}, u32[]{:S(2)}, u32[]{:S(2)}) collective-permute-start(bf16[3,128,512]{2,1,0:T(8,128)(2,1)S(1)} %get-tuple-element.45.refs_3_), channel_id=1, source_target_pairs={{0,1},{1,0},{2,3},{3,2},{4,5},{5,4},{6,7},{7,6},{8,9},{9,8},{10,11... | collective-permute-start | bytes 1179656 | tf_op jit(solution)/shard_map/ppermute | solution.py:566
  107.7 30.9 %all-to-all-start.2 = ((bf16[8,128,512]{2,1,0:T(8,128)(2,1)}), bf16[8,128,512]{2,1,0:T(8,128)(2,1)}, u32[]{:S(2)}, u32[]{:S(2)}) async-start(bf16[8,128,512]{2,1,0:T(8,128)(2,1)} %slab_fronts.7), calls=%async_computation.2 | async-start | bytes 2097152 | tf_op jit(solution)/shard_map/all_to_all | solution.py:571
  113.5 20.9 %collective-permute-start.6 = (bf16[3,128,512]{2,1,0:T(8,128)(2,1)S(1)}, bf16[3,128,512]{2,1,0:T(8,128)(2,1)S(1)}, u32[]{:S(2)}, u32[]{:S(2)}) collective-permute-start(bf16[3,128,512]{2,1,0:T(8,128)(2,1)S(1)} %get-tuple-element.46.refs_3_), channel_id=1, source_target_pairs={{0,1},{1,0},{2,3},{3,2},{4,5},{5,4},{6,7},{7,6},{8,9},{9,8},{10,11... | collective-permute-start | bytes 1179656 | tf_op jit(solution)/shard_map/ppermute | solution.py:566
  114.7 19.6 %collective-permute-start.7 = (bf16[3,128,512]{2,1,0:T(8,128)(2,1)}, bf16[3,128,512]{2,1,0:T(8,128)(2,1)}, u32[]{:S(2)}, u32[]{:S(2)}) collective-permute-start(bf16[3,128,512]{2,1,0:T(8,128)(2,1)} %copy-done.6), channel_id=1, source_target_pairs={{0,2},{1,3},{2,0},{3,1},{4,6},{5,7},{6,4},{7,5},{8,10},{9,11},{10,... | collective-permute-start | bytes 1179656 | tf_op jit(solution)/shard_map/ppermute | solution.py:566
  115.6 18.8 %collective-permute-start.8 = (bf16[3,128,512]{2,1,0:T(8,128)(2,1)S(1)}, bf16[3,128,512]{2,1,0:T(8,128)(2,1)}, u32[]{:S(2)}, u32[]{:S(2)}) collective-permute-start(bf16[3,128,512]{2,1,0:T(8,128)(2,1)S(1)} %get-tuple-element.48), channel_id=1, source_target_pairs={{0,3},{1,2},{2,1},{3,0},{4,7},{5,6},{6,5},{7,4},{8,11},{9,10},{10,... | collective-permute-start | bytes 1179656 | tf_op jit(solution)/shard_map/ppermute | solution.py:566
  119.6 19.0 %collective-permute-start.12 = (bf16[24,2048]{1,0:T(8,128)(2,1)S(1)}, bf16[24,2048]{1,0:T(8,128)(2,1)S(1)}, u32[]{:S(2)}, u32[]{:S(2)}) collective-permute-start(bf16[24,2048]{1,0:T(8,128)(2,1)S(1)} %dynamic-slice_bitcast_fusion), channel_id=1, source_target_pairs={{0,4},{4,8},{8,12},{12,16},{16,20},{20,24},{24,28},{1,5},{5,9},{9,... | collective-permute-start | bytes 294920 | tf_op jit(solution)/shard_map/ppermute | solution.py:546
  138.6 29.1 %all-to-all-start.1 = ((bf16[8,128,512]{2,1,0:T(8,128)(2,1)}), bf16[8,128,512]{2,1,0:T(8,128)(2,1)}, u32[]{:S(2)}, u32[]{:S(2)}) async-start(bf16[8,128,512]{2,1,0:T(8,128)(2,1)} %in_place.1), calls=%async_computation.1 | async-start | bytes 2097152 | tf_op jit(solution)/shard_map/all_to_all | solution.py:571
  174.7 10.4 %collective-permute-start.21 = (bf16[16,2176]{1,0:T(8,128)(2,1)S(1)}, bf16[16,2176]{1,0:T(8,128)(2,1)S(1)}, u32[]{:S(2)}, u32[]{:S(2)}) collective-permute-start(bf16[16,2176]{1,0:T(8,128)(2,1)S(1)} %get-tuple-element.67), channel_id=1, source_target_pairs={{0,24},{4,28},{1,25},{5,29},{2,26},{6,30},{3,27},{7,31}} | collective-permute-start | bytes 208904 | tf_op jit(solution)/shard_map/ppermute | solution.py:546
  175.4 12.1 %collective-permute-start.20 = (bf16[16,2176]{1,0:T(8,128)(2,1)S(1)}, bf16[16,2176]{1,0:T(8,128)(2,1)S(1)}, u32[]{:S(2)}, u32[]{:S(2)}) collective-permute-start(bf16[16,2176]{1,0:T(8,128)(2,1)S(1)} %get-tuple-element.67), channel_id=1, source_target_pairs={{0,20},{4,24},{8,28},{1,21},{5,25},{9,29},{2,22},{6,26},{10,30},{3... | collective-permute-start | bytes 208904 | tf_op jit(solution)/shard_map/ppermute | solution.py:546
  176.0 11.4 %collective-permute-start.19 = (bf16[16,2176]{1,0:T(8,128)(2,1)S(1)}, bf16[16,2176]{1,0:T(8,128)(2,1)S(1)}, u32[]{:S(2)}, u32[]{:S(2)}) collective-permute-start(bf16[16,2176]{1,0:T(8,128)(2,1)S(1)} %get-tuple-element.67), channel_id=1, source_target_pairs={{0,16},{4,20},{8,24},{12,28},{1,17},{5,21},{9,25},{13,29},{2,18},{... | collective-permute-start | bytes 208904 | tf_op jit(solution)/shard_map/ppermute | solution.py:546
  177.3 10.6 %collective-permute-start.18 = (bf16[16,2176]{1,0:T(8,128)(2,1)S(1)}, bf16[16,2176]{1,0:T(8,128)(2,1)S(1)}, u32[]{:S(2)}, u32[]{:S(2)}) collective-permute-start(bf16[16,2176]{1,0:T(8,128)(2,1)S(1)} %get-tuple-element.67), channel_id=1, source_target_pairs={{0,12},{4,16},{8,20},{12,24},{16,28},{1,13},{5,17},{9,21},{13,25},... | collective-permute-start | bytes 208904 | tf_op jit(solution)/shard_map/ppermute | solution.py:546
  183.2 10.6 %collective-permute-start.17 = (bf16[16,2176]{1,0:T(8,128)(2,1)S(1)}, bf16[16,2176]{1,0:T(8,128)(2,1)S(1)}, u32[]{:S(2)}, u32[]{:S(2)}) collective-permute-start(bf16[16,2176]{1,0:T(8,128)(2,1)S(1)} %get-tuple-element.67), channel_id=1, source_target_pairs={{0,8},{4,12},{8,16},{12,20},{16,24},{20,28},{1,9},{5,13},{9,17},{1... | collective-permute-start | bytes 208904 | tf_op jit(solution)/shard_map/ppermute | solution.py:546
  (15 other events, 114.2 us)
